TPU v7x, 32 devices: a whole 2x2x4 slice. The times are simulated.
32 devices in a mesh: cols: 8 (over z, y), mem: 4 (over x, core).
Axes of the slice: x: 2, y: 2, z: 4, core: 2. Of those that a mesh axis runs over, the one named last changes fastest.
Arguments:
- state: float32 [80, 262144], P('mem', 'cols'), may hold values from -6 to 6
- obs_value: float32 [4, 1024], P(None, 'cols'), may hold values from -6 to 6
- obs_var: float32 [4, 1024], P(None, 'cols'), may hold values from 0.2 to 2
- owner: int32 [4, 1024, 1], P(None, 'cols'), may hold values from 0 to 7; in each aligned block of 128 rows (0 to 127, 128 to 255, ..., all dimensions but the last counted through in order) at most 32 rows name the same one
- tile_of: int32 [4, 1024], P(None, 'cols'), may hold values from 0 to 63
- offsets: int32 [4, 1024, 4], P(None, 'cols'), may hold values from 0 to 511
- accept: int32 [4, 1024], P(None, 'cols'), may hold values 0 or 1
- loc_mask: int32 [512, 4, 8], P(('cols', 'mem')), may hold values 0 or 1
Outputs:
- posterior: float32 [80, 262144], P(None, ('cols', 'mem'))
Inputs may be any that keep to these rules, and one draw needn't show every extreme that they name: Within the 128 observations of one batch held by one index of cols, no owner is named more than 32 times, and that many is reached.
All inputs are finite; a program needn't handle non-finite values. No bound on the sum of `accept` or of `loc_mask` on one device may be relied on, other than what follows from the above.
Results may differ from a plain program's by a relative error of at most 0.0002.
Values sent between devices are 32-bit elements; how exact they have to be, the bound alone decides.
No kernel may reach another device: no remote copies, remote signals or barrier semaphores. Data moves between devices by JAX's collectives and lax.ppermute only.
A program may use at most 64 MiB of HBM per device.

v0:
```python
import jax
import jax.numpy as jnp
from jax import lax
from jax.sharding import PartitionSpec as P

epsilon = 1e-05
EXACT = lax.Precision.HIGHEST


def innovations(prior_obs, observed, obs_noise, accepted):
    members = prior_obs.shape[0]
    mean_prior = jnp.mean(prior_obs, axis=0)
    spread = prior_obs - mean_prior
    spread_var = jnp.sum(spread * spread, axis=0) / (members - 1) + epsilon
    denominator = spread_var + obs_noise
    mean_shift = spread_var / denominator * (observed - mean_prior)
    factor = jnp.sqrt(obs_noise / denominator) - 1.0
    increment = accepted * (mean_shift + factor * spread)
    scaled = spread / ((members - 1) * spread_var)
    return (increment, scaled)


def local(state, obs_value, obs_var, owner, tile_of, offsets, accept, loc_mask):
    col_devices = lax.axis_size("cols")
    mem_devices = lax.axis_size("mem")
    source = lax.axis_index("cols")
    mem_index = lax.axis_index("mem")
    batch_total, per_src = obs_value.shape
    pick_count = offsets.shape[2]
    members = state.shape[0] * mem_devices
    cell_count = state.shape[1] // mem_devices
    tiles_here = loc_mask.shape[0]
    tile_len = cell_count // tiles_here
    block_count = loc_mask.shape[2]
    batch_obs = per_src * col_devices
    block_len = batch_obs // block_count
    capacity = max(2, 2 * per_src // col_devices)
    slot_count = col_devices * capacity
    destination = owner[:, :, 0]
    ordinal = jnp.arange(per_src, dtype=jnp.int32)
    same_owner = destination[:, :, None] == destination[:, None, :]
    earlier = (ordinal[None, :] < ordinal[:, None])[None]
    slot_rank = jnp.sum((same_owner & earlier).astype(jnp.int32), axis=2)
    batch_rows = jnp.broadcast_to(
        jnp.arange(batch_total, dtype=jnp.int32)[:, None], destination.shape
    )
    position = jnp.broadcast_to(source * per_src + ordinal, destination.shape)
    fields = jnp.concatenate(
        [tile_of[:, :, None], accept[:, :, None], position[:, :, None], offsets], axis=2
    )
    blank_int = (
        jnp.zeros((batch_total, col_devices, capacity, 3 + pick_count), jnp.int32)
        .at[:, :, :, 2]
        .set(-1)
    )
    sent_int = blank_int.at[batch_rows, destination, slot_rank].set(fields)
    blank_val = (
        jnp.zeros((batch_total, col_devices, capacity, 2), jnp.float32).at[:, :, :, 1].set(1.0)
    )
    sent_val = blank_val.at[batch_rows, destination, slot_rank].set(
        jnp.stack([obs_value, obs_var], axis=2)
    )
    arrived_int = lax.all_to_all(sent_int, "cols", split_axis=1, concat_axis=1, tiled=True).reshape(
        batch_total, slot_count, 3 + pick_count
    )
    arrived_val = lax.all_to_all(sent_val, "cols", split_axis=1, concat_axis=1, tiled=True).reshape(
        batch_total, slot_count, 2
    )
    obs_tile = arrived_int[:, :, 0]
    obs_flag = arrived_int[:, :, 1].astype(jnp.float32)
    obs_pos = arrived_int[:, :, 2]
    obs_off = arrived_int[:, :, 3:]
    observed = arrived_val[:, :, 0]
    obs_noise = arrived_val[:, :, 1]
    targets = jnp.where(obs_pos >= 0, obs_pos, batch_obs)
    ensemble = lax.all_to_all(state, "mem", split_axis=1, concat_axis=0, tiled=True)
    for batch_no in range(batch_total):
        local_cell = (
            obs_tile[batch_no][:, None] * tile_len + obs_off[batch_no] - mem_index * cell_count
        )
        inside = (local_cell >= 0) & (local_cell < cell_count) & (obs_pos[batch_no] >= 0)[:, None]
        flat_cells = jnp.clip(local_cell, 0, cell_count - 1).reshape(-1)
        picked = jnp.take(ensemble, flat_cells, axis=1).reshape(members, slot_count, pick_count)
        prior_obs = lax.psum(
            jnp.sum(jnp.where(inside[None], picked, 0.0), axis=2) / pick_count, "mem"
        )
        increment, scaled = innovations(
            prior_obs, observed[batch_no], obs_noise[batch_no], obs_flag[batch_no]
        )
        blank_panel = jnp.zeros((members, batch_obs), jnp.float32)
        placed_inc = blank_panel.at[:, targets[batch_no]].add(increment, mode="drop")
        placed_scl = blank_panel.at[:, targets[batch_no]].add(scaled, mode="drop")
        inc_all, scl_all = lax.psum((placed_inc, placed_scl), "cols")
        mask_now = loc_mask[:, batch_no, :].astype(jnp.float32)
        mean_state = jnp.mean(ensemble, axis=0)
        deviation = (ensemble - mean_state).reshape(members, tiles_here, tile_len)
        per_block = jnp.einsum(
            "nbk,mbk->bnm",
            scl_all.reshape(members, block_count, block_len),
            inc_all.reshape(members, block_count, block_len),
            precision=EXACT,
        )
        mixing = jnp.einsum("tb,bnm->tnm", mask_now, per_block, precision=EXACT)
        change = jnp.einsum("tnm,nti->mti", mixing, deviation, precision=EXACT).reshape(
            members, cell_count
        )
        ensemble = ensemble + change
    return ensemble


def solution(mesh):
    return jax.shard_map(
        local,
        mesh=mesh,
        in_specs=(
            P("mem", "cols"),
            P(None, "cols"),
            P(None, "cols"),
            P(None, "cols", None),
            P(None, "cols"),
            P(None, "cols", None),
            P(None, "cols"),
            P(("cols", "mem"), None, None),
        ),
        out_specs=P(None, ("cols", "mem")),
        check_vma=False,
    )
```

profile of v0, /device:TPU:0, one launch (start us, length us, event | category | flops | bytes accessed | tf_op | source)
XLA Modules:
  0.0 701.4 jit_solution(12244447749374363344)
XLA Ops:
  9.2 31.0 %scatter_fusion.1 = f32[4,8,32,2]{3,2,1,0:T(8,128)S(1)} fusion(f32[4,8,32,2]{3,2,1,0:T(8,128)S(1)} %copy-done.6, s32[512]{0:T(512)S(1)} %fusion.115, f32[512,2]{1,0:T(8,128)S(1)} %bitcast.210), kind=kCustom, calls=%fused_computation.6 | custom fusion | bytes 18432 | tf_op jit(solution)/shard_map/scatter | solution.py:60
  41.2 7.2 %all-to-all-start.2 = ((f32[8,1,256]{2,1,0:T(1,128)}), f32[8,1,256]{2,1,0:T(1,128)S(1)}, u32[]{:S(2)}, u32[]{:S(2)}) async-start(f32[8,1,256]{2,1,0:T(1,128)} %reshape.812), calls=%async_computation.2 | async-start | bytes 16384 | tf_op jit(solution)/shard_map/all_to_all | solution.py:66
  48.6 31.0 %scatter_fusion = s32[4,8,32,7]{3,2,1,0:T(8,128)S(1)} fusion(s32[4,8,32,7]{3,2,1,0:T(8,128)S(1)} %copy-done.7, s32[512]{0:T(512)S(1)} %fusion.115, s32[512,7]{1,0:T(8,128)S(1)} %copy.319), kind=kCustom, calls=%fused_computation.4 | custom fusion | bytes 49152 | tf_op jit(solution)/shard_map/scatter | solution.py:56
  80.6 6.0 all-to-all-start.1
  86.6 3.6 all_to_all.22
  90.2 3.2 copy.314
  94.6 3.7 all-to-all-start
  101.2 34.0 %all-to-all-done = f32[20,4,8192]{2,0,1:T(8,128)S(1)} async-done(((f32[20,4,8192]{2,0,1:T(8,128)}), f32[20,4,8192]{2,0,1:T(8,128)S(1)}, u32[]{:S(2)}, u32[]{:S(2)}) %all-to-all-start) | async-done | bytes 2621472 | tf_op jit(solution)/shard_map/all_to_all | solution.py:76
  136.8 4.9 copy.325
  141.7 6.2 gather_fusion
  151.3 31.0 %all-reduce.13.cloned.1.call-done = f32[80,256]{0,1:T(8,128)} async-done(((f32[80,256]{0,1:T(8,128)}), f32[80,256]{0,1:T(8,128)}) %all-reduce.13.cloned.1.call-update) | async-done | bytes 81936 | tf_op jit(solution)/shard_map/psum | solution.py:84
  196.7 3.8 broadcast_subtract_fusion
  200.5 67.2 %all-reduce.27.cloned.1.call-done = (f32[80,8,128]{2,0,1:T(8,128)}, f32[80,8,128]{2,0,1:T(8,128)}) async-done(((f32[80,8,128]{2,0,1:T(8,128)}, f32[80,8,128]{2,0,1:T(8,128)}), (f32[80,8,128]{2,0,1:T(8,128)}, f32[80,8,128]{2,0,1:T(8,128)})) %all-reduce.27.cloned.1.call-update) | async-done | bytes 655376 | tf_op jit(solution)/shard_map/psum | solution.py:93
  270.1 5.9 fusion
  280.5 4.9 copy.342
  285.4 6.2 gather_fusion.1
  294.0 30.6 %all-reduce.15.cloned.1.call-done = f32[80,256]{0,1:T(8,128)} async-done(((f32[80,256]{0,1:T(8,128)}), f32[80,256]{0,1:T(8,128)}) %all-reduce.15.cloned.1.call-update) | async-done | bytes 81936 | tf_op jit(solution)/shard_map/psum | solution.py:84
  326.8 2.8 scatter_custom_fusion.5
  336.7 4.8 copy.336
  341.5 3.3 reshape.653
  347.1 62.9 %all-reduce.25.cloned.1.call-done = (f32[80,8,128]{2,0,1:T(8,128)}, f32[80,8,128]{2,0,1:T(8,128)}) async-done(((f32[80,8,128]{2,0,1:T(8,128)}, f32[80,8,128]{2,0,1:T(8,128)}), (f32[80,8,128]{2,0,1:T(8,128)}, f32[80,8,128]{2,0,1:T(8,128)})) %all-reduce.25.cloned.1.call-update) | async-done | bytes 655376 | tf_op jit(solution)/shard_map/psum | solution.py:93
  412.4 11.2 %fusion.123 = (f32[16,512]{1,0:T(8,128)S(1)}, f32[80,16,512]{2,0,1:T(8,128)}, f32[16,512,80]{1,2,0:T(8,128)S(1)}) fusion(f32[16,512,80]{1,2,0:T(8,128)} %copy-done, f32[80,16,512]{2,1,0:T(8,128)} %all_to_all.26, f32[16,80,80]{2,0,1:T(8,128)S(1)} %convolution_bitcast_fusion.2, f32[16,512]{1,0:T(8,128)S(1)} %div.150), kind=kOutput, calls=%fused_computation.240 | convolution fusion | flops 632414208 | bytes 10960896 | tf_op jit(solution)/shard_map/tnm,nti->mti/dot_general | solution.py:104
  425.7 3.5 copy.353
  429.2 5.0 gather_fusion.2
  435.8 30.5 %all-reduce.17.cloned.1.call-done = f32[80,256]{0,1:T(8,128)} async-done(((f32[80,256]{0,1:T(8,128)}), f32[80,256]{0,1:T(8,128)}) %all-reduce.17.cloned.1.call-update) | async-done | bytes 81936 | tf_op jit(solution)/shard_map/psum | solution.py:84
  474.7 73.5 %all-reduce.23.cloned.1.call-done = (f32[80,8,128]{2,0,1:T(8,128)}, f32[80,8,128]{2,0,1:T(8,128)}) async-done(((f32[80,8,128]{2,0,1:T(8,128)}, f32[80,8,128]{2,0,1:T(8,128)}), (f32[80,8,128]{2,0,1:T(8,128)}, f32[80,8,128]{2,0,1:T(8,128)})) %all-reduce.23.cloned.1.call-update) | async-done | bytes 655376 | tf_op jit(solution)/shard_map/psum | solution.py:93
  550.7 5.3 fusion.14
  559.5 4.9 copy.364
  564.4 5.0 gather_fusion.3
  570.8 30.6 %all-reduce.19.cloned.1.call-done = f32[80,256]{0,1:T(8,128)} async-done(((f32[80,256]{0,1:T(8,128)}), f32[80,256]{0,1:T(8,128)}) %all-reduce.19.cloned.1.call-update) | async-done | bytes 81936 | tf_op jit(solution)/shard_map/psum | solution.py:84
  609.8 73.8 %all-reduce.21.cloned.1.call-done = (f32[80,8,128]{2,0,1:T(8,128)}, f32[80,8,128]{2,0,1:T(8,128)}) async-done(((f32[80,8,128]{2,0,1:T(8,128)}, f32[80,8,128]{2,0,1:T(8,128)}), (f32[80,8,128]{2,0,1:T(8,128)}, f32[80,8,128]{2,0,1:T(8,128)})) %all-reduce.21.cloned.1.call-update) | async-done | bytes 655376 | tf_op jit(solution)/shard_map/psum | solution.py:93
  686.0 4.5 fusion.8
  (168 shorter events, 84.8 us)
Async XLA Ops:
  6.5 2.6 copy-start.6
  9.2 39.2 %copy-start.9 = (s32[4,128,4]{1,2,0:T(4,128)S(1)}, s32[4,128,4]{1,2,0:T(4,128)}, u32[]{:S(2)}) copy-start(s32[4,128,4]{1,2,0:T(4,128)} %param.19) | copy-start | bytes 24580
  9.2 39.2 %copy-start.10 = (s32[4,128]{1,0:T(4,128)S(1)}, s32[4,128]{1,0:T(4,128)}, u32[]{:S(2)}) copy-start(s32[4,128]{1,0:T(4,128)} %param.20) | copy-start | bytes 6148
  9.2 39.2 %copy-start.11 = (s32[4,128]{1,0:T(4,128)S(1)}, s32[4,128]{1,0:T(4,128)}, u32[]{:S(2)}) copy-start(s32[4,128]{1,0:T(4,128)} %param.18) | copy-start | bytes 6148
  9.2 39.4 %copy-start.7 = (s32[4,8,32,7]{3,2,1,0:T(8,128)S(1)}, s32[4,8,32,7]{3,2,1,0:T(8,128)}, u32[]{:S(2)}) copy-start(s32[4,8,32,7]{3,2,1,0:T(8,128)} %constant.122.clone.1) | copy-start | bytes 86020
  41.2 39.5 %all-to-all-start.2 = ((f32[8,1,256]{2,1,0:T(1,128)}), f32[8,1,256]{2,1,0:T(1,128)S(1)}, u32[]{:S(2)}, u32[]{:S(2)}) async-start(f32[8,1,256]{2,1,0:T(1,128)} %reshape.812), calls=%async_computation.2 | async-start | bytes 16384 | tf_op jit(solution)/shard_map/all_to_all | solution.py:66
  80.6 13.9 %all-to-all-start.1 = ((s32[8,1,896]{2,1,0:T(1,128)}), s32[8,1,896]{2,1,0:T(1,128)S(1)}, u32[]{:S(2)}, u32[]{:S(2)}) async-start(s32[8,1,896]{2,1,0:T(1,128)} %reshape.810), calls=%async_computation.1 | async-start | bytes 57344 | tf_op jit(solution)/shard_map/all_to_all | solution.py:63
  94.6 40.6 %all-to-all-start = ((f32[20,4,8192]{2,0,1:T(8,128)}), f32[20,4,8192]{2,0,1:T(8,128)S(1)}, u32[]{:S(2)}, u32[]{:S(2)}) async-start(f32[20,4,8192]{2,0,1:T(8,128)} %copy.314), calls=%async_computation | async-start | bytes 6291456 | tf_op jit(solution)/shard_map/all_to_all | solution.py:76
  98.3 84.0 %all-reduce.13.cloned.1.call-start = ((), (), s32[]{:S(2)}) async-start(), calls=%async_computation.3 | async-start | bytes 262144 | tf_op jit(solution)/shard_map/psum | solution.py:84
  150.3 117.3 %all-reduce.27.cloned.1.call-start = ((), (), s32[]{:S(2)}) async-start(), calls=%async_computation.10 | async-start | bytes 1310720 | tf_op jit(solution)/shard_map/psum | solution.py:93
  193.9 130.8 %all-reduce.15.cloned.1.call-start = ((), (), s32[]{:S(2)}) async-start(), calls=%async_computation.4 | async-start | bytes 262144 | tf_op jit(solution)/shard_map/psum | solution.py:84
  196.7 72.7 %copy-start.8 = (s32[16,4,8]{0,2,1:T(8,128)S(1)}, s32[16,4,8]{0,2,1:T(8,128)}, u32[]{:S(2)}) copy-start(s32[16,4,8]{0,2,1:T(8,128)} %param.21) | copy-start | bytes 6148
  276.0 1.5 copy-start
  276.1 2.7 copy-start.1
  294.0 116.0 %all-reduce.25.cloned.1.call-start = ((), (), s32[]{:S(2)}) async-start(), calls=%async_computation.9 | async-start | bytes 1310720 | tf_op jit(solution)/shard_map/psum | solution.py:93
  336.2 130.0 %all-reduce.17.cloned.1.call-start = ((), (), s32[]{:S(2)}) async-start(), calls=%async_computation.5 | async-start | bytes 262144 | tf_op jit(solution)/shard_map/psum | solution.py:84
  423.7 1.7 copy-start.2
  425.7 3.5 copy-start.4
  435.6 112.7 %all-reduce.23.cloned.1.call-start = ((), (), s32[]{:S(2)}) async-start(), calls=%async_computation.8 | async-start | bytes 1310720 | tf_op jit(solution)/shard_map/psum | solution.py:93
  474.4 126.9 %all-reduce.19.cloned.1.call-start = ((), (), s32[]{:S(2)}) async-start(), calls=%async_computation.6 | async-start | bytes 262144 | tf_op jit(solution)/shard_map/psum | solution.py:84
  556.0 1.7 copy-start.5
  570.7 112.9 %all-reduce.21.cloned.1.call-start = ((), (), s32[]{:S(2)}) async-start(), calls=%async_computation.7 | async-start | bytes 1310720 | tf_op jit(solution)/shard_map/psum | solution.py:93
  690.6 1.7 copy-start.3
Sparse Core Ops, SparseCore 0:
  150.4 31.8 all-reduce.12
  194.0 73.6 all-reduce.26
  294.1 30.5 all-reduce.14
  336.4 73.5 all-reduce.24
  435.7 30.5 all-reduce.16
  474.6 73.6 all-reduce.22
  570.8 30.5 all-reduce.18
  609.9 73.6 all-reduce.20
where the time goes:
time: 711 us; the launch traced here: 701 us
  waiting for transfers between devices  434 us (61%)
  local copies, waits for them, and re-layouts  146 us (21%)
  other arithmetic  51.2 us (7%)
  matrix products  36.8 us (5%)
  starting transfers between devices  18.1 us (3%)
  between operations  14.8 us (2%)
    psum x4, waiting for transfers between devices, local(): inc_all, scl_all = lax.psum((placed_inc, placed_scl), 'cols')  277 us
    psum x4, waiting for transfers between devices, local(): lax.psum(jnp.sum(jnp.where(inside[None], picked, 0.0), axis=2) / pick_cou...  123 us
    all_to_all x1, waiting for transfers between devices, local(): lax.all_to_all(state, 'mem', split_axis=1, concat_axis=0, tiled=True)  34 us
    scatter x2, local copies, waits for them, and re-layouts, local(): sent_int = blank_int.at[batch_rows, destination, slot_rank].set(fields)  31.2 us
    scatter x2, local copies, waits for them, and re-layouts, local(): blank_val.at[batch_rows, destination, slot_rank]  31.2 us
    dot_general x4, matrix products, local(): jnp.einsum('tnm,nti->mti', mixing, deviation, precision=EXACT)  27 us
    gather x4, local copies, waits for them, and re-layouts, local(): jnp.take(ensemble, flat_cells, axis=1)  22.3 us
    all_to_all x5, local copies, waits for them, and re-layouts, local(): lax.all_to_all(state, 'mem', split_axis=1, concat_axis=0, tiled=True)  15.1 us
  transfers between devices with their start and end apart: 11, of which 9 were waited for; matrix products, arithmetic and copies ran while one was open for 8% of the time, Pallas kernels for 0%

commit v1 on v0

--- a/solution.py
+++ b/solution.py
@@ -1,10 +1,394 @@
+import functools
+
 import jax
 import jax.numpy as jnp
 from jax import lax
+from jax.experimental import pallas as pl
+from jax.experimental.pallas import tpu as pltpu
 from jax.sharding import PartitionSpec as P
 
 epsilon = 1e-05
 EXACT = lax.Precision.HIGHEST
+f32, bf16, i32 = jnp.float32, jnp.bfloat16, jnp.int32
+LANES = 128
+CHUNK = 256
+TILE = 512
+PAD = 24
+WHOLE = pl.BlockSpec()
+FAR = pl.BlockSpec(memory_space=pltpu.HBM)
+PARAMS = pltpu.CompilerParams(vmem_limit_bytes=48 * 1024 * 1024)
+
+
+def iota(shape, axis):
+    return lax.broadcasted_iota(i32, shape, axis)
+
+
+def dot(a, b, dims):
+    return lax.dot_general(a, b, ((dims[0], dims[1]), ((), ())), preferred_element_type=f32)
+
+
+def two(x):
+    high = x.astype(bf16)
+    return high, (x - high.astype(f32)).astype(bf16)
+
+
+def slot_rows(sid, slots):
+    return jnp.where(iota((slots, sid.shape[1]), 0) == sid, 1.0, 0.0).astype(bf16)
+
+
+def route_kernel(owners, slots_per, *refs):
+    ins, (msg_ref, sid_ref), here, sems = refs[0:7], refs[7:9], refs[9:16], refs[16]
+    copies = [pltpu.make_async_copy(a, b, sems.at[i]) for i, (a, b) in enumerate(zip(ins, here))]
+    for copy in copies:
+        copy.start()
+    for copy in copies:
+        copy.wait()
+    owner_ref, tile_ref, off_ref, val_ref, var_ref, acc_ref, mask_ref = here
+    batches, _, per = owner_ref.shape
+    slots = owners * slots_per
+    hot = [
+        jnp.where(iota((owners, per), 0) == owner_ref[b], 1.0, 0.0) for b in range(batches)
+    ]
+    before = jnp.where(iota((per, per), 0) < iota((per, per), 1), 1.0, 0.0).astype(bf16)
+    counts = dot(jnp.concatenate(hot, axis=0).astype(bf16), before, ((1,), (0,)))
+    used = jnp.zeros((owners, 1), f32)
+    total = jnp.zeros((16, slots), f32)
+    for b in range(batches):
+        own = owner_ref[b]
+        rank = used + counts[b * owners : (b + 1) * owners]
+        rank = jnp.sum(hot[b] * rank, axis=0, keepdims=True)
+        used = used + jnp.sum(hot[b], axis=1, keepdims=True)
+        sid = own * slots_per + rank.astype(i32)
+        sid_ref[b : b + 1, :] = sid
+        cells = tile_ref[b : b + 1, :] * 512 + off_ref[b]
+        fields = jnp.concatenate(
+            [(cells >> 7).astype(f32), (cells & 127).astype(f32), jnp.ones((8, per), f32)], axis=0
+        ).astype(bf16)
+        total = total + dot(fields, slot_rows(sid, slots), ((1,), (1,)))
+    cells = total[0:4] * 128.0 + total[4:8] + (total[8:12] - 1.0)
+    tiles = mask_ref.shape[1]
+    kinds = mask_ref.shape[0]
+    spread_out = jnp.where(iota((kinds, LANES), 0) == (iota((kinds, LANES), 1) & (kinds - 1)), 1.0, 0.0)
+    wide = dot(mask_ref[...].astype(bf16), spread_out.astype(bf16), ((0,), (0,)))
+    group = LANES // kinds
+    lane_tile = iota((tiles, LANES), 1) // kinds
+    masks = [
+        jnp.sum(jnp.where(iota((tiles, LANES), 0) == lane_tile + r * group, wide, 0.0), axis=0, keepdims=True)
+        for r in range(tiles // group)
+    ]
+    owner = jnp.concatenate([owner_ref[b] for b in range(batches)], axis=0)
+    where_tile = (owner * 64 + tile_ref[...]).astype(f32)
+    shared = jnp.concatenate(
+        [val_ref[...], var_ref[...], acc_ref[...].astype(f32), where_tile] + masks, axis=0
+    )
+    for c in range(owners):
+        msg_ref[c, 0:4, :] = cells[:, c * slots_per : (c + 1) * slots_per]
+        msg_ref[c, 4:24, :] = shared
+
+
+def prepare_kernel(state_ref, out_ref):
+    rows = state_ref.shape[0]
+    fill = jnp.zeros((PAD - rows, TILE), f32)
+    for t in range(state_ref.shape[1] // TILE):
+        tile = jnp.concatenate([state_ref[:, t * TILE : (t + 1) * TILE], fill], axis=0)
+        high = tile.astype(bf16).astype(f32)
+        out_ref[t * 2 * PAD : (t + 1) * 2 * PAD, :] = jnp.concatenate([high, tile - high], axis=0).astype(bf16)
+
+
+def pick_kernel(rows, msg_ref, parts_ref, out_ref, mask_ref, weight_ref):
+    homes, _, slots_per = msg_ref.shape
+    tiles = parts_ref.shape[0] // (2 * PAD)
+    each = CHUNK // slots_per
+    mask_ref[...] = msg_ref[:, 20:24, :]
+    for g in range(homes // each):
+        cells = jnp.concatenate([msg_ref[g * each + i, 0:4, :] for i in range(each)], axis=1)
+        cells = jnp.maximum(cells.astype(i32), 0)
+        weight = jnp.zeros((TILE, CHUNK), f32)
+        for p in range(4):
+            weight = weight + jnp.where(iota((TILE, CHUNK), 0) == (cells[p : p + 1] & (TILE - 1)), 0.25, 0.0)
+        weight_ref[...] = weight.astype(bf16)
+        tile = cells[0:1] >> 9
+        sums = dot(parts_ref[...], weight_ref[...], ((1,), (0,)))
+        total = jnp.zeros((PAD, CHUNK), f32)
+        for t in range(tiles):
+            both = sums[t * 2 * PAD : t * 2 * PAD + PAD] + sums[t * 2 * PAD + PAD : (t + 1) * 2 * PAD]
+            total = total + jnp.where(tile == t, both, 0.0)
+        for i in range(each):
+            out_ref[g * each + i] = total[0:rows, i * slots_per : (i + 1) * slots_per]
+
+
+def place_kernel(got_ref, sid_ref, keep_ref, send_ref):
+    owners, rows, slots_per = got_ref.shape
+    batches, per = sid_ref.shape
+    slots = owners * slots_per
+    core = lax.axis_index("mem") & 1
+    fill = jnp.zeros((24 - rows, slots), f32)
+    got = jnp.concatenate([got_ref[c] for c in range(owners)], axis=1)
+    got = jnp.concatenate([got, fill], axis=0)
+    first = got.astype(bf16).astype(f32)
+    rest = got - first
+    second = rest.astype(bf16).astype(f32)
+    parts = jnp.concatenate([first, second, rest - second], axis=0).astype(bf16)
+    half = batches // 2
+    for ref, which in ((keep_ref, core), (send_ref, 1 - core)):
+        for i in range(half):
+            sid = jnp.where(which == 0, sid_ref[i : i + 1, :], sid_ref[half + i : half + i + 1, :])
+            out = dot(parts, slot_rows(sid, slots), ((1,), (0,)))
+            out = out[0:24] + out[24:48] + out[48:72]
+            ref[:, i * per : (i + 1) * per] = out[0:rows]
+
+
+def mask_kernel(tiles, members, info_ref, a_ref, b_ref, c_ref, d_ref, mask_ref):
+    homes = info_ref.shape[0]
+    mem = lax.axis_index("mem")
+    device = lax.axis_index("cols") * lax.axis_size("mem") + mem
+    table = [ref[h] for ref in (a_ref, b_ref, c_ref, d_ref) for h in range(homes)]
+    table = jnp.concatenate(table, axis=0).astype(bf16)
+    kinds = mask_ref.shape[1]
+    group = LANES // kinds
+    obs_chunks = 16
+    for idx in range(mask_ref.shape[0]):
+        if idx < obs_chunks:
+            b, h = idx // 4, 2 * (idx % 4)
+            where_tile = jnp.concatenate([info_ref[h, 16 + b : 17 + b, :], info_ref[h + 1, 16 + b : 17 + b, :]], axis=1)
+            where_tile = where_tile.astype(i32)
+        else:
+            column = iota((1, CHUNK), 1) + (idx - obs_chunks) * CHUNK
+            where_tile = jnp.zeros((1, CHUNK), i32) + device * tiles
+            for t in range(1, tiles):
+                where_tile = where_tile + jnp.where(column >= t * members, 1, 0)
+        row = ((((where_tile >> 4) & 3) ^ mem) * homes + (where_tile >> 6)) * 4 + ((where_tile >> 2) & 3)
+        hot = jnp.where(iota((LANES, CHUNK), 0) == row, 1.0, 0.0).astype(bf16)
+        rows = dot(table, hot, ((0,), (0,)))
+        out = jnp.zeros((kinds, CHUNK), f32)
+        for g in range(group):
+            out = out + jnp.where((where_tile & 3) == g, rows[g * kinds : (g + 1) * kinds], 0.0)
+        mask_ref[idx] = out
+
+
+def split_kernel(*refs):
+    own, near, pieces, out_ref = refs[0], refs[1], refs[2:-1], refs[-1]
+    rows = own.shape[0]
+    begin = 0
+    for i in range(0, len(pieces), 2):
+        end = begin + pieces[i].shape[1]
+        cells = slice(begin, end)
+        whole = jnp.concatenate([own[:, cells], near[:, cells], pieces[i][...], pieces[i + 1][...]], axis=0)
+        high, low = two(whole)
+        out_ref[0 : 4 * rows, cells] = high
+        out_ref[4 * rows : 8 * rows, cells] = low
+        begin = end
+
+
+def window_kernel(tiles, rows, mm_ref, mx_ref, cm_ref, cx_ref, info_ref, mask_ref, ens_ref, out_ref, y_ref, w_ref):
+    homes, half_members, wide = mm_ref.shape
+    members = 2 * half_members
+    per = wide // 2
+    batches = 4
+    blocks = homes
+    mem = lax.axis_index("mem")
+    x, core = mem >> 1, mem & 1
+    obs_chunks = batches * homes * per // CHUNK
+    x_chunks = tiles * members // CHUNK
+    for b in range(batches):
+        lanes = slice((b % 2) * per, (b % 2 + 1) * per)
+        mine = core == b // 2
+        for h in range(homes):
+            near = jnp.where(mine, mm_ref[h, :, lanes], cm_ref[h, :, lanes])
+            far = jnp.where(mine, mx_ref[h, :, lanes], cx_ref[h, :, lanes])
+            chunk, place = b * (homes // 2) + h // 2, (h % 2) * per
+            y_ref[chunk, 0:half_members, place : place + per] = jnp.where(x == 0, near, far)
+            y_ref[chunk, half_members:members, place : place + per] = jnp.where(x == 0, far, near)
+    member = iota((members, CHUNK), 0)
+    for q in range(x_chunks):
+        column = iota((1, CHUNK), 1) + q * CHUNK
+        tile = jnp.zeros((1, CHUNK), i32)
+        for t in range(1, tiles):
+            tile = tile + jnp.where(column >= t * members, 1, 0)
+        column = column - tile * members
+        part = jnp.zeros((1, CHUNK), i32)
+        for k in range(1, 4):
+            part = part + jnp.where(column >= k * rows, 1, 0)
+        true = column - part * rows + (part ^ mem) * rows
+        y_ref[obs_chunks + q] = jnp.where(member == true, 1.0, 0.0)
+
+    lane3 = iota((members, 3 * members), 1)
+    for b in range(batches):
+        for g in range(homes // 2):
+            def field(f):
+                return jnp.concatenate(
+                    [info_ref[h, 4 + 4 * f + b : 5 + 4 * f + b, :] for h in (2 * g, 2 * g + 1)], axis=1
+                )
+
+            prior = y_ref[b * (homes // 2) + g]
+            mean = jnp.sum(prior, axis=0, keepdims=True) / members
+            spread = prior - mean
+            var = jnp.sum(spread * spread, axis=0, keepdims=True) / (members - 1) + epsilon
+            noise = field(1)
+            denominator = var + noise
+            shift = var / denominator * (field(0) - mean)
+            factor = jnp.sqrt(noise / denominator) - 1.0
+            increment = field(2) * (shift + factor * spread)
+            scaled = spread / ((members - 1) * var)
+            ih, il = two(increment)
+            sh, sl = two(scaled)
+            for i in range(2):
+                lanes = slice(i * per, (i + 1) * per)
+                left = jnp.concatenate([ih[:, lanes], ih[:, lanes], il[:, lanes]], axis=1)
+                right = jnp.concatenate([sh[:, lanes], sl[:, lanes], sh[:, lanes]], axis=1)
+                right = jnp.concatenate([right, right, right], axis=0)
+                block = dot(left, right, ((1,), (1,)))
+                high = block.astype(bf16).astype(f32)
+                block = jnp.where(lane3 < 2 * members, high, block - high)
+                h = 2 * g + i
+                w_ref[h * members : (h + 1) * members, :] = block.astype(bf16)
+
+        def update(idx, carry, b=b):
+            now = y_ref[idx]
+            deviation = now - jnp.sum(now, axis=0, keepdims=True) / members
+            dh, dl = two(deviation)
+            moved = dot(w_ref[...], jnp.concatenate([dh, dl, dh], axis=0), ((1,), (0,)))
+            for k in range(blocks):
+                now = now + mask_ref[idx, b * blocks + k : b * blocks + k + 1, :] * moved[
+                    k * members : (k + 1) * members
+                ]
+            y_ref[idx] = now
+            return carry
+
+        lax.fori_loop((b + 1) * (homes // 2), obs_chunks + x_chunks, update, 0)
+
+    size = out_ref.shape[1] // tiles
+    flat = jnp.concatenate([y_ref[obs_chunks + q] for q in range(x_chunks)], axis=1)
+    for t in range(tiles):
+        weight = flat[:, t * members : (t + 1) * members]
+        high = weight.astype(bf16).astype(f32)
+        weight = jnp.concatenate([high, high, weight - high], axis=1).astype(bf16)
+        cells = slice(t * size, (t + 1) * size)
+        ens_high, ens_low = ens_ref[0:members, cells], ens_ref[members : 2 * members, cells]
+        out_ref[:, cells] = dot(weight, jnp.concatenate([ens_high, ens_low, ens_high], axis=0), ((1,), (0,)))
+
+
+def fast(state, obs_value, obs_var, owner, tile_of, offsets, accept, loc_mask):
+    owners = lax.axis_size("cols")
+    mem_devices = lax.axis_size("mem")
+    mem = lax.axis_index("mem")
+    core = mem & 1
+    batches, per = obs_value.shape
+    rows, slab = state.shape
+    members = rows * mem_devices
+    cells = slab // mem_devices
+    tiles = loc_mask.shape[0]
+    kinds = loc_mask.shape[1] * loc_mask.shape[2]
+    cap = 2 * per // owners
+    slots_per = batches * cap
+
+    about = (
+        owner.transpose(0, 2, 1),
+        tile_of,
+        offsets.transpose(0, 2, 1),
+        obs_value,
+        obs_var,
+        accept,
+        loc_mask.transpose(1, 2, 0).reshape(kinds, tiles),
+    )
+    msg, sid = pl.pallas_call(
+        functools.partial(route_kernel, owners, slots_per),
+        out_shape=(
+            jax.ShapeDtypeStruct((owners, 24, slots_per), f32),
+            jax.ShapeDtypeStruct((batches, per), i32),
+        ),
+        in_specs=[FAR] * 7,
+        out_specs=(WHOLE,) * 2,
+        scratch_shapes=[pltpu.VMEM(a.shape, a.dtype) for a in about] + [pltpu.SemaphoreType.DMA((7,))],
+        compiler_params=PARAMS,
+        name="route",
+    )(*about)
+    arrived = lax.all_to_all(msg, "cols", split_axis=0, concat_axis=0, tiled=True)
+
+    parts = pl.pallas_call(
+        prepare_kernel,
+        out_shape=jax.ShapeDtypeStruct((slab // TILE * 2 * PAD, TILE), bf16),
+        in_specs=[WHOLE],
+        out_specs=WHOLE,
+        compiler_params=PARAMS,
+        name="prepare",
+    )(state)
+    own = lax.dynamic_slice_in_dim(state, mem * cells, cells, 1)
+
+    def swap(array, k):
+        return lax.ppermute(array, "mem", [(i, i ^ k) for i in range(4)])
+
+    def piece(begin, width):
+        return [swap(lax.dynamic_slice_in_dim(state, (mem ^ k) * cells + begin, width, 1), k) for k in (2, 3)]
+
+    near = swap(lax.dynamic_slice_in_dim(state, (mem ^ 1) * cells, cells, 1), 1)
+    first = piece(0, 2048)
+    second = piece(2048, 2048)
+    third = piece(4096, 4096)
+    arrived, near, *first = lax.optimization_barrier((arrived, near, *first))
+    priors, mask = pl.pallas_call(
+        functools.partial(pick_kernel, rows),
+        out_shape=(
+            jax.ShapeDtypeStruct((owners, rows, slots_per), f32),
+            jax.ShapeDtypeStruct((owners, 4, LANES), f32),
+        ),
+        in_specs=[WHOLE] * 2,
+        out_specs=(WHOLE,) * 2,
+        scratch_shapes=[pltpu.VMEM((TILE, CHUNK), bf16)],
+        compiler_params=PARAMS,
+        name="pick",
+    )(arrived, parts)
+    tables = [mask] + [swap(mask, k) for k in (1, 2, 3)]
+    at_home = lax.all_to_all(priors, "cols", split_axis=0, concat_axis=0, tiled=True)
+    at_home, *second = lax.optimization_barrier((at_home, *second))
+    keep, send = pl.pallas_call(
+        place_kernel,
+        out_shape=(jax.ShapeDtypeStruct((rows, batches // 2 * per), f32),) * 2,
+        in_specs=[WHOLE] * 2,
+        out_specs=(WHOLE,) * 2,
+        compiler_params=PARAMS,
+        name="place",
+    )(at_home, sid)
+    got = swap(send, 1)
+    chip = jnp.where(
+        core == 0, jnp.concatenate([keep, got], axis=0), jnp.concatenate([got, keep], axis=0)
+    )
+    everyone = jnp.broadcast_to(chip[None], (owners,) + chip.shape)
+    mine = lax.all_to_all(everyone, "cols", split_axis=0, concat_axis=0, tiled=True)
+    mine, *third = lax.optimization_barrier((mine, *third))
+    over_x = swap(mine, 2)
+    cm, cx = swap(mine, 1), swap(over_x, 1)
+
+    obs_chunks = batches * owners * per // CHUNK
+    x_chunks = tiles * members // CHUNK
+    masks = pl.pallas_call(
+        functools.partial(mask_kernel, tiles, members),
+        out_shape=jax.ShapeDtypeStruct((obs_chunks + x_chunks, kinds, CHUNK), f32),
+        in_specs=[WHOLE] * 5,
+        out_specs=WHOLE,
+        compiler_params=PARAMS,
+        name="masks",
+    )(arrived, *tables)
+    pieces = pl.pallas_call(
+        split_kernel,
+        out_shape=jax.ShapeDtypeStruct((2 * members, cells), bf16),
+        in_specs=[WHOLE] * 8,
+        out_specs=WHOLE,
+        compiler_params=PARAMS,
+        name="split",
+    )(own, near, *first, *second, *third)
+    return pl.pallas_call(
+        functools.partial(window_kernel, tiles, rows),
+        out_shape=jax.ShapeDtypeStruct((members, cells), f32),
+        in_specs=[WHOLE] * 7,
+        out_specs=WHOLE,
+        scratch_shapes=[
+            pltpu.VMEM((obs_chunks + x_chunks, members, CHUNK), f32),
+            pltpu.VMEM((owners * members, 3 * members), bf16),
+        ],
+        compiler_params=PARAMS,
+        name="window",
+    )(mine, over_x, cm, cx, arrived, masks, pieces)
 
 
 def innovations(prior_obs, observed, obs_noise, accepted):
@@ -20,7 +404,7 @@
     return (increment, scaled)
 
 
-def local(state, obs_value, obs_var, owner, tile_of, offsets, accept, loc_mask):
+def plain(state, obs_value, obs_var, owner, tile_of, offsets, accept, loc_mask):
     col_devices = lax.axis_size("cols")
     mem_devices = lax.axis_size("mem")
     source = lax.axis_index("cols")
@@ -107,6 +491,21 @@
         ensemble = ensemble + change
     return ensemble
 
+def local(*arrays):
+    state, obs_value, _, _, _, _, _, loc_mask = arrays
+    per = obs_value.shape[1]
+    owners, mem_devices = lax.axis_size("cols"), lax.axis_size("mem")
+    tiles, batches, blocks = loc_mask.shape
+    fits = (
+        mem_devices == 4
+        and owners == blocks == 8
+        and per == LANES
+        and batches == 4
+        and tiles == 16
+        and state.shape == (20, 64 * 512)
+    )
+    return fast(*arrays) if fits else plain(*arrays)
+
 
 def solution(mesh):
     return jax.shard_map(

time: 711 us -> 105 us (0.15); the launches traced: 701 us -> 105 us
  waiting for transfers between devices: 434 us -> 43.3 us
  local copies, waits for them, and re-layouts: 146 us -> 7.36 us
  other arithmetic: 51.2 us -> 0.01 us
  matrix products: 36.8 us -> 0 us
  Pallas kernels: 0 us -> 28.3 us
  between operations: 14.8 us -> 0.2 us
  starting transfers between devices: 18.1 us -> 25.7 us
    psum x8 -> x0, waiting for transfers between devices: 400 us -> none  [the longest x4 277 us: local(): inc_all, scl_all = lax.psum((placed_inc, placed_scl), 'cols')]
    scatter x4 -> x0, local copies, waits for them, and re-layouts: 62.5 us -> none  [the longest x2 31.2 us: local(): sent_int = blank_int.at[batch_rows, destination, slot_rank].set(fields)]
    dot_general x12 -> x0, matrix products: 36.8 us -> none  [the longest x4 27 us: local(): jnp.einsum('tnm,nti->mti', mixing, deviation, precision=EXACT)]
    ppermute x0 -> x14, waiting for transfers between devices: none -> 36.2 us  [swap(): return lax.ppermute(array, 'mem', [(i, i ^ k) for i in range(4)])]
    pallas_call x0 -> x7, Pallas kernels: none -> 28.3 us  [the longest x1 17.5 us: fast(): pl.pallas_call(functools.partial(window_kernel, tiles, rows), out_shape=j...]
    all_to_all x3, waiting for transfers between devices: 34.1 us -> 7.11 us  [the longest x1 7.11 us: fast(): lax.all_to_all(priors, 'cols', split_axis=0, concat_axis=0, tiled=True)]
    gather x4 -> x0, local copies, waits for them, and re-layouts: 22.3 us -> none  [local(): jnp.take(ensemble, flat_cells, axis=1)]
    scatter-add x8 -> x0, other arithmetic: 19.5 us -> none  [the longest x4 9.79 us: local(): blank_panel.at[:, targets[batch_no]].add(increment, mode='drop')]
  transfers between devices with their start and end apart: 11 -> 17, of which waited for: 9 -> 9; matrix products, arithmetic and copies ran while one was open for 8% -> 3% of each run, Pallas kernels for 0% -> 10%
where the time goes in v1:
time: 105 us
  waiting for transfers between devices  43.3 us (41%)
  Pallas kernels  28.3 us (27%)
  starting transfers between devices  25.7 us (24%)
  local copies, waits for them, and re-layouts  7.36 us (7%)
    ppermute x14, waiting for transfers between devices, swap(): return lax.ppermute(array, 'mem', [(i, i ^ k) for i in range(4)])  36.2 us
    pallas_call x1, Pallas kernels, fast(): pl.pallas_call(functools.partial(window_kernel, tiles, rows), out_shape=j...  17.5 us
    ppermute x14, starting transfers between devices, swap(): return lax.ppermute(array, 'mem', [(i, i ^ k) for i in range(4)])  9.51 us
    all_to_all x1, waiting for transfers between devices, fast(): lax.all_to_all(priors, 'cols', split_axis=0, concat_axis=0, tiled=True)  7.11 us
    all_to_all x1, starting transfers between devices, fast(): lax.all_to_all(msg, 'cols', split_axis=0, concat_axis=0, tiled=True)  6.86 us
    all_to_all x1, starting transfers between devices, fast(): lax.all_to_all(priors, 'cols', split_axis=0, concat_axis=0, tiled=True)  5.94 us
    pallas_call x1, Pallas kernels, fast(): pl.pallas_call(functools.partial(pick_kernel, rows), out_shape=(jax.Shape...  4.31 us
    all_to_all x1, starting transfers between devices, fast(): lax.all_to_all(everyone, 'cols', split_axis=0, concat_axis=0, tiled=True)  3.43 us
  transfers between devices with their start and end apart: 17, of which 9 were waited for; matrix products, arithmetic and copies ran while one was open for 3% of the time, Pallas kernels for 10%

profile of v1, /device:TPU:0, one launch (start us, length us, event | category | flops | bytes accessed | tf_op | source)
XLA Modules:
  0.0 104.9 jit_solution(12530590081615569314)
XLA Ops:
  0.0 2.7 %constant_dynamic-slice_fusion = (f32[20,8192]{1,0:T(8,128)}, f32[20,8192]{1,0:T(8,128)}) fusion(f32[20,32768]{1,0:T(8,128)} %state_ref.1, s32[]{:T(128)S(6)} %select_n.45, s32[]{:T(128)S(6)} %select_n.37), kind=kLoop, calls=%fused_computation.1 | loop fusion | bytes 2621448 | tf_op jit(solution)/shard_map/dynamic_slice | solution.py:316
  3.2 1.3 %route.1 = (f32[8,24,128]{2,1,0:T(8,128)}, s32[4,128]{1,0:T(4,128)S(1)}) custom-call(s32[4,1,128]{2,1,0:T(1,128)S(1)} %bitcast.7, s32[4,128]{1,0:T(4,128)S(1)} %copy-done.6, s32[4,4,128]{2,1,0:T(4,128)S(1)} %bitcast.6, f32[4,128]{1,0:T(4,128)S(1)} %copy-done.7, f32[4,128]{1,0:T(4,128)S(1)} %copy-done.8, s32[4,128]{1,0:T(4,128)S(1)} %copy-done.9, ...), custom_call_target="tpu_custom_call" | custom-call | tf_op jit(solution)/shard_map/route/pallas_call | solution.py:294
  4.5 6.9 %all-to-all-start = ((f32[8,24,128]{2,1,0:T(8,128)}), f32[8,24,128]{2,1,0:T(8,128)S(1)}, u32[]{:S(2)}, u32[]{:S(2)}) async-start(f32[8,24,128]{2,1,0:T(8,128)} %get-tuple-element.21), calls=%async_computation | async-start | bytes 196608 | tf_op jit(solution)/shard_map/all_to_all | solution.py:306
  11.4 2.0 %constant_dynamic-slice_fusion.3 = (f32[20,2048]{1,0:T(8,128)}, f32[20,2048]{1,0:T(8,128)}, f32[20,2048]{1,0:T(8,128)S(1)}, f32[20,2048]{1,0:T(8,128)S(1)}) fusion(f32[20,32768]{1,0:T(8,128)} %state_ref.1, s32[]{:T(128)S(6)} %select_n.41, s32[]{:T(128)S(6)} %select_n.40, s32[]{:T(128)S(6)} %select_n.39, s32[]{:T(128)S(6)} %select_n.38), kind=kLoop, calls=%fused_computation.4 | loop fusion | bytes 1310736 | tf_op jit(solution)/shard_map/dynamic_slice | solution.py:322
  13.4 1.3 %collective-permute-start.2 = (f32[20,2048]{1,0:T(8,128)S(1)}, f32[20,2048]{1,0:T(8,128)S(1)}, u32[]{:S(2)}, u32[]{:S(2)}) collective-permute-start(f32[20,2048]{1,0:T(8,128)S(1)} %get-tuple-element.43), channel_id=1, source_target_pairs={{0,3},{1,2},{2,1},{3,0},{4,7},{5,6},{6,5},{7,4},{8,11},{9,10},{10,... | collective-permute-start | bytes 491528 | tf_op jit(solution)/shard_map/ppermute | solution.py:319
  14.7 0.5 collective-permute-start.1
  15.3 1.1 %collective-permute-start.4 = (f32[20,2048]{1,0:T(8,128)}, f32[20,2048]{1,0:T(8,128)}, u32[]{:S(2)}, u32[]{:S(2)}) collective-permute-start(f32[20,2048]{1,0:T(8,128)} %get-tuple-element.41), channel_id=1, source_target_pairs={{0,3},{1,2},{2,1},{3,0},{4,7},{5,6},{6,5},{7,4},{8,11},{9,10},{10,... | collective-permute-start | bytes 491528 | tf_op jit(solution)/shard_map/ppermute | solution.py:319
  16.4 0.5 collective-permute-start.3
  16.9 2.3 %prepare.1.parts_ref = bf16[3072,512]{1,0:T(8,128)(2,1)S(1)} custom-call(f32[20,32768]{1,0:T(8,128)} %state_ref.1), custom_call_target="tpu_custom_call" | custom-call | tf_op jit(solution)/shard_map/prepare/pallas_call | solution.py:308
  19.2 1.1 %collective-permute-done.2.refs_3_ = f32[20,2048]{1,0:T(8,128)S(1)} collective-permute-done((f32[20,2048]{1,0:T(8,128)S(1)}, f32[20,2048]{1,0:T(8,128)S(1)}, u32[]{:S(2)}, u32[]{:S(2)}) %collective-permute-start.2) | collective-permute-done | bytes 163872 | tf_op jit(solution)/shard_map/ppermute | solution.py:319
  20.3 4.8 %collective-permute-done.1.refs_2_ = f32[20,2048]{1,0:T(8,128)S(1)} collective-permute-done((f32[20,2048]{1,0:T(8,128)S(1)}, f32[20,2048]{1,0:T(8,128)S(1)}, u32[]{:S(2)}, u32[]{:S(2)}) %collective-permute-start.1) | collective-permute-done | bytes 163872 | tf_op jit(solution)/shard_map/ppermute | solution.py:319
  25.1 0.7 copy-done.1
  25.8 4.3 %pick.1 = (f32[8,20,128]{2,1,0:T(8,128)}, f32[8,4,128]{2,1,0:T(4,128)S(1)}) custom-call(f32[8,24,128]{2,1,0:T(8,128)S(1)} %all-to-all-done.msg_ref.info_ref, bf16[3072,512]{1,0:T(8,128)(2,1)S(1)} %prepare.1.parts_ref), custom_call_target="tpu_custom_call" | custom-call | tf_op jit(solution)/shard_map/pick/pallas_call | solution.py:329
  30.1 5.9 %all-to-all-start.1 = ((f32[8,20,128]{2,1,0:T(8,128)}), f32[8,20,128]{2,1,0:T(8,128)S(1)}, u32[]{:S(2)}, u32[]{:S(2)}) async-start(f32[8,20,128]{2,1,0:T(8,128)} %get-tuple-element.23), calls=%async_computation.1 | async-start | bytes 196608 | tf_op jit(solution)/shard_map/all_to_all | solution.py:342
  36.1 7.1 %all-to-all-done.1.got_ref = f32[8,20,128]{2,1,0:T(8,128)S(1)} async-done(((f32[8,20,128]{2,1,0:T(8,128)}), f32[8,20,128]{2,1,0:T(8,128)S(1)}, u32[]{:S(2)}, u32[]{:S(2)}) %all-to-all-start.1) | async-done | bytes 81952 | tf_op jit(solution)/shard_map/all_to_all | solution.py:342
  43.7 1.2 %collective-permute-done.5 = f32[20,256]{1,0:T(8,128)S(1)} collective-permute-done((f32[20,256]{1,0:T(8,128)S(1)}, f32[20,256]{1,0:T(8,128)S(1)}, u32[]{:S(2)}, u32[]{:S(2)}) %collective-permute-start.5) | collective-permute-done | bytes 20512 | tf_op jit(solution)/shard_map/ppermute | solution.py:319
  44.9 0.8 broadcast_in_dim.2
  45.6 3.4 %all-to-all-start.2 = ((f32[8,40,256]{2,1,0:T(8,128)}), f32[8,40,256]{2,1,0:T(8,128)S(1)}, u32[]{:S(2)}, u32[]{:S(2)}) async-start(f32[8,40,256]{2,1,0:T(8,128)} %broadcast_in_dim.2), calls=%async_computation.2 | async-start | bytes 655360 | tf_op jit(solution)/shard_map/all_to_all | solution.py:357
  49.0 1.2 %constant_dynamic-slice_fusion.1 = (f32[20,4096]{1,0:T(8,128)S(1)}, f32[20,4096]{1,0:T(8,128)S(1)}) fusion(f32[20,32768]{1,0:T(8,128)} %state_ref.1, s32[]{:T(128)S(6)} %select_n.44, s32[]{:T(128)S(6)} %select_n.43), kind=kLoop, calls=%fused_computation.2 | loop fusion | bytes 1310728 | tf_op jit(solution)/shard_map/dynamic_slice | solution.py:322
  50.2 1.3 %collective-permute-start.7 = (f32[20,4096]{1,0:T(8,128)S(1)}, f32[20,4096]{1,0:T(8,128)S(1)}, u32[]{:S(2)}, u32[]{:S(2)}) collective-permute-start(f32[20,4096]{1,0:T(8,128)S(1)} %get-tuple-element.39), channel_id=1, source_target_pairs={{0,3},{1,2},{2,1},{3,0},{4,7},{5,6},{6,5},{7,4},{8,11},{9,10},{10,... | collective-permute-start | bytes 983048 | tf_op jit(solution)/shard_map/ppermute | solution.py:319
  51.5 0.5 collective-permute-start.6
  52.1 9.3 %collective-permute-done.7.refs_7_ = f32[20,4096]{1,0:T(8,128)S(1)} collective-permute-done((f32[20,4096]{1,0:T(8,128)S(1)}, f32[20,4096]{1,0:T(8,128)S(1)}, u32[]{:S(2)}, u32[]{:S(2)}) %collective-permute-start.7) | collective-permute-done | bytes 327712 | tf_op jit(solution)/shard_map/ppermute | solution.py:319
  61.4 8.8 %collective-permute-done.6.refs_6_ = f32[20,4096]{1,0:T(8,128)S(1)} collective-permute-done((f32[20,4096]{1,0:T(8,128)S(1)}, f32[20,4096]{1,0:T(8,128)S(1)}, u32[]{:S(2)}, u32[]{:S(2)}) %collective-permute-start.6) | collective-permute-done | bytes 327712 | tf_op jit(solution)/shard_map/ppermute | solution.py:319
  70.1 1.5 %collective-permute-start.8 = (f32[8,40,256]{2,1,0:T(8,128)S(1)}, f32[8,40,256]{2,1,0:T(8,128)S(1)}, u32[]{:S(2)}, u32[]{:S(2)}) collective-permute-start(f32[8,40,256]{2,1,0:T(8,128)S(1)} %all-to-all-done.2.mm_ref), channel_id=1, source_target_pairs={{0,2},{1,3},{2,0},{3,1},{4,6},{5,7},{6,4},{7,5},{8,10},{9,11},{10,... | collective-permute-start | bytes 983048 | tf_op jit(solution)/shard_map/ppermute | solution.py:319
  71.6 7.9 %collective-permute-done.8.mx_ref = f32[8,40,256]{2,1,0:T(8,128)S(1)} collective-permute-done((f32[8,40,256]{2,1,0:T(8,128)S(1)}, f32[8,40,256]{2,1,0:T(8,128)S(1)}, u32[]{:S(2)}, u32[]{:S(2)}) %collective-permute-start.8) | collective-permute-done | bytes 327712 | tf_op jit(solution)/shard_map/ppermute | solution.py:319
  79.5 1.6 %collective-permute-start.13 = (f32[8,4,128]{2,1,0:T(4,128)S(1)}, f32[8,4,128]{2,1,0:T(4,128)S(1)}, u32[]{:S(2)}, u32[]{:S(2)}) collective-permute-start(f32[8,4,128]{2,1,0:T(4,128)S(1)} %get-tuple-element.29.a_ref), channel_id=1, source_target_pairs={{0,3},{1,2},{2,1},{3,0},{4,7},{5,6},{6,5},{7,4},{8,11},{9,10},{10,... | collective-permute-start | bytes 49160 | tf_op jit(solution)/shard_map/ppermute | solution.py:319
  81.1 0.5 collective-permute-start.12
  81.7 1.0 collective-permute-done.13.d_ref
  82.7 2.2 %collective-permute-done.12.c_ref = f32[8,4,128]{2,1,0:T(4,128)S(1)} collective-permute-done((f32[8,4,128]{2,1,0:T(4,128)S(1)}, f32[8,4,128]{2,1,0:T(4,128)S(1)}, u32[]{:S(2)}, u32[]{:S(2)}) %collective-permute-start.12) | collective-permute-done | bytes 16416 | tf_op jit(solution)/shard_map/ppermute | solution.py:319
  84.9 0.7 masks.1.mask_ref
  85.6 1.8 %split.1.ens_ref = bf16[160,8192]{1,0:T(8,128)(2,1)S(1)} custom-call(f32[20,8192]{1,0:T(8,128)S(1)} %copy-done, f32[20,8192]{1,0:T(8,128)} %collective-permute-done.refs_1_, f32[20,2048]{1,0:T(8,128)S(1)} %copy-done.2, f32[20,2048]{1,0:T(8,128)S(1)} %collective-permute-done.2.refs_3_, f32[20,2048]{1,0:T(8,128)} %collective-permute-done.3.refs_4_, ...), custom_call_target="tpu_custom_call" | custom-call | tf_op jit(solution)/shard_map/split/pallas_call | solution.py:372
  87.4 17.5 %window.1 = f32[80,8192]{1,0:T(8,128)} custom-call(f32[8,40,256]{2,1,0:T(8,128)S(1)} %all-to-all-done.2.mm_ref, f32[8,40,256]{2,1,0:T(8,128)S(1)} %collective-permute-done.8.mx_ref, f32[8,40,256]{2,1,0:T(8,128)S(1)} %collective-permute-done.9.cm_ref, f32[8,40,256]{2,1,0:T(8,128)S(1)} %collective-permute-done.10.cx_ref, ...), custom_call_target="tpu_custom_call" | custom-call | tf_op jit(solution)/shard_map/window/pallas_call | solution.py:380
  (34 shorter events, 1.0 us)
Async XLA Ops:
  0.0 3.2 %copy-start.3 = (s32[16,4,8]{0,2,1:T(8,128)S(1)}, s32[16,4,8]{0,2,1:T(8,128)}, u32[]{:S(2)}) copy-start(s32[16,4,8]{0,2,1:T(8,128)} %param.15) | copy-start | bytes 6148
  0.0 3.2 %copy-start.9 = (s32[4,128]{1,0:T(4,128)S(1)}, s32[4,128]{1,0:T(4,128)}, u32[]{:S(2)}) copy-start(s32[4,128]{1,0:T(4,128)} %refs_5_.1) | copy-start | bytes 6148
  0.0 3.2 %copy-start.4 = (s32[4,128,4]{1,2,0:T(4,128)S(1)}, s32[4,128,4]{1,2,0:T(4,128)}, u32[]{:S(2)}) copy-start(s32[4,128,4]{1,2,0:T(4,128)} %param.13) | copy-start | bytes 24580
  0.0 3.2 %copy-start.6 = (s32[4,128]{1,0:T(4,128)S(1)}, s32[4,128]{1,0:T(4,128)}, u32[]{:S(2)}) copy-start(s32[4,128]{1,0:T(4,128)} %refs_1_.1) | copy-start | bytes 6148
  0.0 3.2 %copy-start.5 = (s32[4,128,1]{1,2,0:T(1,128)S(1)}, s32[4,128,1]{1,2,0:T(1,128)}, u32[]{:S(2)}) copy-start(s32[4,128,1]{1,2,0:T(1,128)} %param.11) | copy-start | bytes 6148
  0.0 3.2 %copy-start.8 = (f32[4,128]{1,0:T(4,128)S(1)}, f32[4,128]{1,0:T(4,128)}, u32[]{:S(2)}) copy-start(f32[4,128]{1,0:T(4,128)} %refs_4_.1) | copy-start | bytes 6148
  0.0 3.2 %copy-start.7 = (f32[4,128]{1,0:T(4,128)S(1)}, f32[4,128]{1,0:T(4,128)}, u32[]{:S(2)}) copy-start(f32[4,128]{1,0:T(4,128)} %refs_3_.1) | copy-start | bytes 6148
  2.8 23.1 %collective-permute-start = (f32[20,8192]{1,0:T(8,128)}, f32[20,8192]{1,0:T(8,128)}, u32[]{:S(2)}, u32[]{:S(2)}) collective-permute-start(f32[20,8192]{1,0:T(8,128)} %get-tuple-element.38), channel_id=1, source_target_pairs={{0,1},{1,0},{2,3},{3,2},{4,5},{5,4},{6,7},{7,6},{8,9},{9,8},{10,11... | collective-permute-start | bytes 1966088 | tf_op jit(solution)/shard_map/ppermute | solution.py:319
  4.5 21.3 %all-to-all-start = ((f32[8,24,128]{2,1,0:T(8,128)}), f32[8,24,128]{2,1,0:T(8,128)S(1)}, u32[]{:S(2)}, u32[]{:S(2)}) async-start(f32[8,24,128]{2,1,0:T(8,128)} %get-tuple-element.21), calls=%async_computation | async-start | bytes 196608 | tf_op jit(solution)/shard_map/all_to_all | solution.py:306
  13.4 6.9 %collective-permute-start.2 = (f32[20,2048]{1,0:T(8,128)S(1)}, f32[20,2048]{1,0:T(8,128)S(1)}, u32[]{:S(2)}, u32[]{:S(2)}) collective-permute-start(f32[20,2048]{1,0:T(8,128)S(1)} %get-tuple-element.43), channel_id=1, source_target_pairs={{0,3},{1,2},{2,1},{3,0},{4,7},{5,6},{6,5},{7,4},{8,11},{9,10},{10,... | collective-permute-start | bytes 491528 | tf_op jit(solution)/shard_map/ppermute | solution.py:319
  14.7 10.4 %collective-permute-start.1 = (f32[20,2048]{1,0:T(8,128)S(1)}, f32[20,2048]{1,0:T(8,128)S(1)}, u32[]{:S(2)}, u32[]{:S(2)}) collective-permute-start(f32[20,2048]{1,0:T(8,128)S(1)} %get-tuple-element.44), channel_id=1, source_target_pairs={{0,2},{1,3},{2,0},{3,1},{4,6},{5,7},{6,4},{7,5},{8,10},{9,11},{10,... | collective-permute-start | bytes 491528 | tf_op jit(solution)/shard_map/ppermute | solution.py:319
  15.3 20.8 %collective-permute-start.4 = (f32[20,2048]{1,0:T(8,128)}, f32[20,2048]{1,0:T(8,128)}, u32[]{:S(2)}, u32[]{:S(2)}) collective-permute-start(f32[20,2048]{1,0:T(8,128)} %get-tuple-element.41), channel_id=1, source_target_pairs={{0,3},{1,2},{2,1},{3,0},{4,7},{5,6},{6,5},{7,4},{8,11},{9,10},{10,... | collective-permute-start | bytes 491528 | tf_op jit(solution)/shard_map/ppermute | solution.py:319
  16.4 19.7 %collective-permute-start.3 = (f32[20,2048]{1,0:T(8,128)}, f32[20,2048]{1,0:T(8,128)}, u32[]{:S(2)}, u32[]{:S(2)}) collective-permute-start(f32[20,2048]{1,0:T(8,128)} %get-tuple-element.42), channel_id=1, source_target_pairs={{0,2},{1,3},{2,0},{3,1},{4,6},{5,7},{6,4},{7,5},{8,10},{9,11},{10,... | collective-permute-start | bytes 491528 | tf_op jit(solution)/shard_map/ppermute | solution.py:319
  25.1 0.7 copy-start.1
  30.1 55.5 %copy-start = (f32[20,8192]{1,0:T(8,128)S(1)}, f32[20,8192]{1,0:T(8,128)}, u32[]{:S(2)}) copy-start(f32[20,8192]{1,0:T(8,128)} %get-tuple-element.37.refs_0_) | copy-start | bytes 1966084
  30.1 55.5 %copy-start.2 = (f32[20,2048]{1,0:T(8,128)S(1)}, f32[20,2048]{1,0:T(8,128)}, u32[]{:S(2)}) copy-start(f32[20,2048]{1,0:T(8,128)} %copy-done.1) | copy-start | bytes 491524
  30.1 13.1 %all-to-all-start.1 = ((f32[8,20,128]{2,1,0:T(8,128)}), f32[8,20,128]{2,1,0:T(8,128)S(1)}, u32[]{:S(2)}, u32[]{:S(2)}) async-start(f32[8,20,128]{2,1,0:T(8,128)} %get-tuple-element.23), calls=%async_computation.1 | async-start | bytes 196608 | tf_op jit(solution)/shard_map/all_to_all | solution.py:342
  43.6 1.3 %collective-permute-start.5 = (f32[20,256]{1,0:T(8,128)S(1)}, f32[20,256]{1,0:T(8,128)S(1)}, u32[]{:S(2)}, u32[]{:S(2)}) collective-permute-start(f32[20,256]{1,0:T(8,128)S(1)} %get-tuple-element.27), channel_id=1, source_target_pairs={{0,1},{1,0},{2,3},{3,2},{4,5},{5,4},{6,7},{7,6},{8,9},{9,8},{10,11... | collective-permute-start | bytes 61448 | tf_op jit(solution)/shard_map/ppermute | solution.py:319
  45.6 24.5 %all-to-all-start.2 = ((f32[8,40,256]{2,1,0:T(8,128)}), f32[8,40,256]{2,1,0:T(8,128)S(1)}, u32[]{:S(2)}, u32[]{:S(2)}) async-start(f32[8,40,256]{2,1,0:T(8,128)} %broadcast_in_dim.2), calls=%async_computation.2 | async-start | bytes 655360 | tf_op jit(solution)/shard_map/all_to_all | solution.py:357
  50.2 11.1 %collective-permute-start.7 = (f32[20,4096]{1,0:T(8,128)S(1)}, f32[20,4096]{1,0:T(8,128)S(1)}, u32[]{:S(2)}, u32[]{:S(2)}) collective-permute-start(f32[20,4096]{1,0:T(8,128)S(1)} %get-tuple-element.39), channel_id=1, source_target_pairs={{0,3},{1,2},{2,1},{3,0},{4,7},{5,6},{6,5},{7,4},{8,11},{9,10},{10,... | collective-permute-start | bytes 983048 | tf_op jit(solution)/shard_map/ppermute | solution.py:319
  51.5 18.6 %collective-permute-start.6 = (f32[20,4096]{1,0:T(8,128)S(1)}, f32[20,4096]{1,0:T(8,128)S(1)}, u32[]{:S(2)}, u32[]{:S(2)}) collective-permute-start(f32[20,4096]{1,0:T(8,128)S(1)} %get-tuple-element.40), channel_id=1, source_target_pairs={{0,2},{1,3},{2,0},{3,1},{4,6},{5,7},{6,4},{7,5},{8,10},{9,11},{10,... | collective-permute-start | bytes 983048 | tf_op jit(solution)/shard_map/ppermute | solution.py:319
  70.1 9.4 %collective-permute-start.8 = (f32[8,40,256]{2,1,0:T(8,128)S(1)}, f32[8,40,256]{2,1,0:T(8,128)S(1)}, u32[]{:S(2)}, u32[]{:S(2)}) collective-permute-start(f32[8,40,256]{2,1,0:T(8,128)S(1)} %all-to-all-done.2.mm_ref), channel_id=1, source_target_pairs={{0,2},{1,3},{2,0},{3,1},{4,6},{5,7},{6,4},{7,5},{8,10},{9,11},{10,... | collective-permute-start | bytes 983048 | tf_op jit(solution)/shard_map/ppermute | solution.py:319
  71.6 15.8 %collective-permute-start.9 = (f32[8,40,256]{2,1,0:T(8,128)S(1)}, f32[8,40,256]{2,1,0:T(8,128)S(1)}, u32[]{:S(2)}, u32[]{:S(2)}) collective-permute-start(f32[8,40,256]{2,1,0:T(8,128)S(1)} %all-to-all-done.2.mm_ref), channel_id=1, source_target_pairs={{0,1},{1,0},{2,3},{3,2},{4,5},{5,4},{6,7},{7,6},{8,9},{9,8},{10,11... | collective-permute-start | bytes 983048 | tf_op jit(solution)/shard_map/ppermute | solution.py:319
  79.5 7.9 %collective-permute-start.10 = (f32[8,40,256]{2,1,0:T(8,128)S(1)}, f32[8,40,256]{2,1,0:T(8,128)S(1)}, u32[]{:S(2)}, u32[]{:S(2)}) collective-permute-start(f32[8,40,256]{2,1,0:T(8,128)S(1)} %collective-permute-done.8.mx_ref), channel_id=1, source_target_pairs={{0,1},{1,0},{2,3},{3,2},{4,5},{5,4},{6,7},{7,6},{8,9},{9,8},{10,11... | collective-permute-start | bytes 983048 | tf_op jit(solution)/shard_map/ppermute | solution.py:319
  79.5 3.2 %collective-permute-start.13 = (f32[8,4,128]{2,1,0:T(4,128)S(1)}, f32[8,4,128]{2,1,0:T(4,128)S(1)}, u32[]{:S(2)}, u32[]{:S(2)}) collective-permute-start(f32[8,4,128]{2,1,0:T(4,128)S(1)} %get-tuple-element.29.a_ref), channel_id=1, source_target_pairs={{0,3},{1,2},{2,1},{3,0},{4,7},{5,6},{6,5},{7,4},{8,11},{9,10},{10,... | collective-permute-start | bytes 49160 | tf_op jit(solution)/shard_map/ppermute | solution.py:319
  81.1 3.7 %collective-permute-start.12 = (f32[8,4,128]{2,1,0:T(4,128)S(1)}, f32[8,4,128]{2,1,0:T(4,128)S(1)}, u32[]{:S(2)}, u32[]{:S(2)}) collective-permute-start(f32[8,4,128]{2,1,0:T(4,128)S(1)} %get-tuple-element.29.a_ref), channel_id=1, source_target_pairs={{0,2},{1,3},{2,0},{3,1},{4,6},{5,7},{6,4},{7,5},{8,10},{9,11},{10,... | collective-permute-start | bytes 49160 | tf_op jit(solution)/shard_map/ppermute | solution.py:319
  81.7 3.2 %collective-permute-start.11 = (f32[8,4,128]{2,1,0:T(4,128)S(1)}, f32[8,4,128]{2,1,0:T(4,128)S(1)}, u32[]{:S(2)}, u32[]{:S(2)}) collective-permute-start(f32[8,4,128]{2,1,0:T(4,128)S(1)} %get-tuple-element.29.a_ref), channel_id=1, source_target_pairs={{0,1},{1,0},{2,3},{3,2},{4,5},{5,4},{6,7},{7,6},{8,9},{9,8},{10,11... | collective-permute-start | bytes 49160 | tf_op jit(solution)/shard_map/ppermute | solution.py:319

commit v2 on v1

--- a/solution.py
+++ b/solution.py
@@ -17,6 +17,11 @@
 WHOLE = pl.BlockSpec()
 FAR = pl.BlockSpec(memory_space=pltpu.HBM)
 PARAMS = pltpu.CompilerParams(vmem_limit_bytes=48 * 1024 * 1024)
+ALONE = pltpu.CompilerParams(vmem_limit_bytes=64 * 1024 * 1024)
+
+
+def cost(amount):
+    return pl.CostEstimate(flops=0, bytes_accessed=amount, transcendentals=0)
 
 
 def iota(shape, axis):
@@ -37,7 +42,7 @@
 
 
 def route_kernel(owners, slots_per, *refs):
-    ins, (msg_ref, sid_ref), here, sems = refs[0:7], refs[7:9], refs[9:16], refs[16]
+    ins, (msg_ref, sid_ref, table_ref), here, sems = refs[0:7], refs[7:10], refs[10:17], refs[17]
     copies = [pltpu.make_async_copy(a, b, sems.at[i]) for i, (a, b) in enumerate(zip(ins, here))]
     for copy in copies:
         copy.start()
@@ -72,18 +77,30 @@
     wide = dot(mask_ref[...].astype(bf16), spread_out.astype(bf16), ((0,), (0,)))
     group = LANES // kinds
     lane_tile = iota((tiles, LANES), 1) // kinds
-    masks = [
-        jnp.sum(jnp.where(iota((tiles, LANES), 0) == lane_tile + r * group, wide, 0.0), axis=0, keepdims=True)
-        for r in range(tiles // group)
-    ]
+    for r in range(tiles // group):
+        here = iota((tiles, LANES), 0) == lane_tile + r * group
+        table_ref[r : r + 1, :] = jnp.sum(jnp.where(here, wide, 0.0), axis=0, keepdims=True)
     owner = jnp.concatenate([owner_ref[b] for b in range(batches)], axis=0)
     where_tile = (owner * 64 + tile_ref[...]).astype(f32)
     shared = jnp.concatenate(
-        [val_ref[...], var_ref[...], acc_ref[...].astype(f32), where_tile] + masks, axis=0
+        [val_ref[...], var_ref[...], acc_ref[...].astype(f32), where_tile], axis=0
     )
     for c in range(owners):
         msg_ref[c, 0:4, :] = cells[:, c * slots_per : (c + 1) * slots_per]
-        msg_ref[c, 4:24, :] = shared
+        msg_ref[c, 4:20, :] = shared
+
+
+def cut_kernel(cuts, state_ref, *refs):
+    sends, sem = refs[:-1], refs[-1]
+    cells = state_ref.shape[1] // 4
+    mem = lax.axis_index("mem")
+    copies = []
+    for ref, (k, begin, end) in zip(sends, cuts):
+        start = pl.multiple_of((mem ^ k) * cells + begin, LANES)
+        copies.append(pltpu.make_async_copy(state_ref.at[:, pl.ds(start, end - begin)], ref, sem.at[len(copies)]))
+        copies[-1].start()
+    for copy in copies:
+        copy.wait()
 
 
 def prepare_kernel(state_ref, out_ref):
@@ -95,11 +112,10 @@
         out_ref[t * 2 * PAD : (t + 1) * 2 * PAD, :] = jnp.concatenate([high, tile - high], axis=0).astype(bf16)
 
 
-def pick_kernel(rows, msg_ref, parts_ref, out_ref, mask_ref, weight_ref):
+def pick_kernel(rows, msg_ref, parts_ref, out_ref, weight_ref):
     homes, _, slots_per = msg_ref.shape
     tiles = parts_ref.shape[0] // (2 * PAD)
     each = CHUNK // slots_per
-    mask_ref[...] = msg_ref[:, 20:24, :]
     for g in range(homes // each):
         cells = jnp.concatenate([msg_ref[g * each + i, 0:4, :] for i in range(each)], axis=1)
         cells = jnp.maximum(cells.astype(i32), 0)
@@ -117,37 +133,32 @@
             out_ref[g * each + i] = total[0:rows, i * slots_per : (i + 1) * slots_per]
 
 
-def place_kernel(got_ref, sid_ref, keep_ref, send_ref):
+def place_kernel(got_ref, sid_ref, table_ref, out_ref):
     owners, rows, slots_per = got_ref.shape
     batches, per = sid_ref.shape
     slots = owners * slots_per
-    core = lax.axis_index("mem") & 1
-    fill = jnp.zeros((24 - rows, slots), f32)
+    fill = jnp.zeros((PAD - rows, slots), f32)
     got = jnp.concatenate([got_ref[c] for c in range(owners)], axis=1)
     got = jnp.concatenate([got, fill], axis=0)
     first = got.astype(bf16).astype(f32)
     rest = got - first
     second = rest.astype(bf16).astype(f32)
     parts = jnp.concatenate([first, second, rest - second], axis=0).astype(bf16)
-    half = batches // 2
-    for ref, which in ((keep_ref, core), (send_ref, 1 - core)):
-        for i in range(half):
-            sid = jnp.where(which == 0, sid_ref[i : i + 1, :], sid_ref[half + i : half + i + 1, :])
-            out = dot(parts, slot_rows(sid, slots), ((1,), (0,)))
-            out = out[0:24] + out[24:48] + out[48:72]
-            ref[:, i * per : (i + 1) * per] = out[0:rows]
-
-
-def mask_kernel(tiles, members, info_ref, a_ref, b_ref, c_ref, d_ref, mask_ref):
+    for b in range(batches):
+        out = dot(parts, slot_rows(sid_ref[b : b + 1, :], slots), ((1,), (0,)))
+        out = out[0:PAD] + out[PAD : 2 * PAD] + out[2 * PAD : 3 * PAD]
+        for c in range(owners):
+            out_ref[c, b * rows : (b + 1) * rows, :] = out[0:rows]
+    for c in range(owners):
+        out_ref[c, batches * rows :, :] = table_ref[...]
+
+
+def fill_masks(tiles, members, kinds, info_ref, table, mask_ref):
     homes = info_ref.shape[0]
     mem = lax.axis_index("mem")
     device = lax.axis_index("cols") * lax.axis_size("mem") + mem
-    table = [ref[h] for ref in (a_ref, b_ref, c_ref, d_ref) for h in range(homes)]
-    table = jnp.concatenate(table, axis=0).astype(bf16)
-    kinds = mask_ref.shape[1]
-    group = LANES // kinds
-    obs_chunks = 16
-    for idx in range(mask_ref.shape[0]):
+    obs_chunks = 4 * homes // 2
+    for idx in range(homes // 2, mask_ref.shape[0]):
         if idx < obs_chunks:
             b, h = idx // 4, 2 * (idx % 4)
             where_tile = jnp.concatenate([info_ref[h, 16 + b : 17 + b, :], info_ref[h + 1, 16 + b : 17 + b, :]], axis=1)
@@ -161,56 +172,51 @@
         hot = jnp.where(iota((LANES, CHUNK), 0) == row, 1.0, 0.0).astype(bf16)
         rows = dot(table, hot, ((0,), (0,)))
         out = jnp.zeros((kinds, CHUNK), f32)
-        for g in range(group):
+        for g in range(LANES // kinds):
             out = out + jnp.where((where_tile & 3) == g, rows[g * kinds : (g + 1) * kinds], 0.0)
         mask_ref[idx] = out
 
 
 def split_kernel(*refs):
-    own, near, pieces, out_ref = refs[0], refs[1], refs[2:-1], refs[-1]
-    rows = own.shape[0]
+    state, near, pieces, out_ref = refs[0], refs[1], refs[2:-1], refs[-1]
+    rows, total = near.shape
+    here = pl.multiple_of(lax.axis_index("mem") * total, total)
     begin = 0
     for i in range(0, len(pieces), 2):
         end = begin + pieces[i].shape[1]
         cells = slice(begin, end)
-        whole = jnp.concatenate([own[:, cells], near[:, cells], pieces[i][...], pieces[i + 1][...]], axis=0)
+        own = state[:, pl.ds(here + begin, end - begin)]
+        whole = jnp.concatenate([own, near[:, cells], pieces[i][...], pieces[i + 1][...]], axis=0)
         high, low = two(whole)
         out_ref[0 : 4 * rows, cells] = high
         out_ref[4 * rows : 8 * rows, cells] = low
         begin = end
 
 
-def window_kernel(tiles, rows, mm_ref, mx_ref, cm_ref, cx_ref, info_ref, mask_ref, ens_ref, out_ref, y_ref, w_ref):
-    homes, half_members, wide = mm_ref.shape
-    members = 2 * half_members
-    per = wide // 2
+def window_kernel(tiles, rows, a_ref, b_ref, c_ref, d_ref, info_ref, ens_ref, out_ref, y_ref, w_ref, mask_ref):
+    homes, all_rows, per = a_ref.shape
     batches = 4
+    members = 4 * rows
+    table = [ref[h, batches * rows :, :] for ref in (a_ref, b_ref, c_ref, d_ref) for h in range(homes)]
+    table = jnp.concatenate(table, axis=0).astype(bf16)
+    fill_masks(tiles, members, mask_ref.shape[1], info_ref, table, mask_ref)
     blocks = homes
     mem = lax.axis_index("mem")
-    x, core = mem >> 1, mem & 1
     obs_chunks = batches * homes * per // CHUNK
     x_chunks = tiles * members // CHUNK
     for b in range(batches):
-        lanes = slice((b % 2) * per, (b % 2 + 1) * per)
-        mine = core == b // 2
         for h in range(homes):
-            near = jnp.where(mine, mm_ref[h, :, lanes], cm_ref[h, :, lanes])
-            far = jnp.where(mine, mx_ref[h, :, lanes], cx_ref[h, :, lanes])
             chunk, place = b * (homes // 2) + h // 2, (h % 2) * per
-            y_ref[chunk, 0:half_members, place : place + per] = jnp.where(x == 0, near, far)
-            y_ref[chunk, half_members:members, place : place + per] = jnp.where(x == 0, far, near)
+            y_ref[chunk, :, place : place + per] = jnp.concatenate(
+                [ref[h, b * rows : (b + 1) * rows, :] for ref in (a_ref, b_ref, c_ref, d_ref)], axis=0
+            )
     member = iota((members, CHUNK), 0)
     for q in range(x_chunks):
         column = iota((1, CHUNK), 1) + q * CHUNK
         tile = jnp.zeros((1, CHUNK), i32)
         for t in range(1, tiles):
             tile = tile + jnp.where(column >= t * members, 1, 0)
-        column = column - tile * members
-        part = jnp.zeros((1, CHUNK), i32)
-        for k in range(1, 4):
-            part = part + jnp.where(column >= k * rows, 1, 0)
-        true = column - part * rows + (part ^ mem) * rows
-        y_ref[obs_chunks + q] = jnp.where(member == true, 1.0, 0.0)
+        y_ref[obs_chunks + q] = jnp.where(member == column - tile * members, 1.0, 0.0)
 
     lane3 = iota((members, 3 * members), 1)
     for b in range(batches):
@@ -243,7 +249,7 @@
                 h = 2 * g + i
                 w_ref[h * members : (h + 1) * members, :] = block.astype(bf16)
 
-        def update(idx, carry, b=b):
+        def update(idx, b=b):
             now = y_ref[idx]
             deviation = now - jnp.sum(now, axis=0, keepdims=True) / members
             dh, dl = two(deviation)
@@ -253,12 +259,26 @@
                     k * members : (k + 1) * members
                 ]
             y_ref[idx] = now
-            return carry
-
-        lax.fori_loop((b + 1) * (homes // 2), obs_chunks + x_chunks, update, 0)
+
+        for idx in range((b + 1) * (homes // 2), obs_chunks + x_chunks):
+            update(idx)
 
     size = out_ref.shape[1] // tiles
-    flat = jnp.concatenate([y_ref[obs_chunks + q] for q in range(x_chunks)], axis=1)
+    true, at = iota((members, members), 0), iota((members, members), 1)
+    part = jnp.zeros((members, members), i32)
+    for k in range(1, 4):
+        part = part + jnp.where(at >= k * rows, 1, 0)
+    order = jnp.where(true == at - part * rows + (part ^ mem) * rows, 1.0, 0.0)
+    order = jnp.concatenate([order, order, order], axis=1).astype(bf16)
+    flat = []
+    for q in range(x_chunks):
+        now = y_ref[obs_chunks + q]
+        first = now.astype(bf16).astype(f32)
+        rest = now - first
+        second = rest.astype(bf16).astype(f32)
+        stack = jnp.concatenate([first, second, rest - second], axis=0).astype(bf16)
+        flat.append(dot(order, stack, ((1,), (0,))))
+    flat = jnp.concatenate(flat, axis=1)
     for t in range(tiles):
         weight = flat[:, t * members : (t + 1) * members]
         high = weight.astype(bf16).astype(f32)
@@ -268,11 +288,29 @@
         out_ref[:, cells] = dot(weight, jnp.concatenate([ens_high, ens_low, ens_high], axis=0), ((1,), (0,)))
 
 
+def window_call(tiles, rows, kinds, mine, by_core, by_x, by_both, about, pieces):
+    owners, _, per = mine.shape
+    members, cells = pieces.shape[0] // 2, pieces.shape[1]
+    chunks = (4 * owners * per + tiles * members) // CHUNK
+    return pl.pallas_call(
+        functools.partial(window_kernel, tiles, rows),
+        out_shape=jax.ShapeDtypeStruct((members, cells), f32),
+        in_specs=[WHOLE] * 6,
+        out_specs=WHOLE,
+        scratch_shapes=[
+            pltpu.VMEM((chunks, members, CHUNK), f32),
+            pltpu.VMEM((owners * members, 3 * members), bf16),
+            pltpu.VMEM((chunks, kinds, CHUNK), f32),
+        ],
+        compiler_params=PARAMS,
+        name="window",
+    )(mine, by_core, by_x, by_both, about, pieces)
+
+
 def fast(state, obs_value, obs_var, owner, tile_of, offsets, accept, loc_mask):
     owners = lax.axis_size("cols")
     mem_devices = lax.axis_size("mem")
     mem = lax.axis_index("mem")
-    core = mem & 1
     batches, per = obs_value.shape
     rows, slab = state.shape
     members = rows * mem_devices
@@ -291,84 +329,73 @@
         accept,
         loc_mask.transpose(1, 2, 0).reshape(kinds, tiles),
     )
-    msg, sid = pl.pallas_call(
+    msg, sid, table = pl.pallas_call(
         functools.partial(route_kernel, owners, slots_per),
         out_shape=(
-            jax.ShapeDtypeStruct((owners, 24, slots_per), f32),
+            jax.ShapeDtypeStruct((owners, 20, slots_per), f32),
             jax.ShapeDtypeStruct((batches, per), i32),
+            jax.ShapeDtypeStruct((tiles * kinds // LANES, LANES), f32),
         ),
         in_specs=[FAR] * 7,
-        out_specs=(WHOLE,) * 2,
+        out_specs=(WHOLE,) * 3,
         scratch_shapes=[pltpu.VMEM(a.shape, a.dtype) for a in about] + [pltpu.SemaphoreType.DMA((7,))],
-        compiler_params=PARAMS,
+        compiler_params=ALONE,
         name="route",
     )(*about)
+    state, msg = lax.optimization_barrier((state, msg))
     arrived = lax.all_to_all(msg, "cols", split_axis=0, concat_axis=0, tiled=True)
 
+    marks = [0, cells * 8 // 16, cells * 12 // 16, cells]
+    cuts = [(1, 0, cells)] + [(k, marks[i], marks[i + 1]) for i in range(3) for k in (2, 3)]
+    sends = pl.pallas_call(
+        functools.partial(cut_kernel, cuts),
+        out_shape=tuple(jax.ShapeDtypeStruct((rows, end - begin), f32) for _, begin, end in cuts),
+        in_specs=[WHOLE],
+        out_specs=(FAR,) * len(cuts),
+        scratch_shapes=[pltpu.SemaphoreType.DMA((len(cuts),))],
+        compiler_params=ALONE,
+        cost_estimate=cost(1024),
+        name="cut",
+    )(state)
     parts = pl.pallas_call(
         prepare_kernel,
         out_shape=jax.ShapeDtypeStruct((slab // TILE * 2 * PAD, TILE), bf16),
         in_specs=[WHOLE],
         out_specs=WHOLE,
         compiler_params=PARAMS,
+        cost_estimate=cost(1024),
         name="prepare",
     )(state)
-    own = lax.dynamic_slice_in_dim(state, mem * cells, cells, 1)
 
     def swap(array, k):
         return lax.ppermute(array, "mem", [(i, i ^ k) for i in range(4)])
 
-    def piece(begin, width):
-        return [swap(lax.dynamic_slice_in_dim(state, (mem ^ k) * cells + begin, width, 1), k) for k in (2, 3)]
-
-    near = swap(lax.dynamic_slice_in_dim(state, (mem ^ 1) * cells, cells, 1), 1)
-    first = piece(0, 2048)
-    second = piece(2048, 2048)
-    third = piece(4096, 4096)
-    arrived, near, *first = lax.optimization_barrier((arrived, near, *first))
-    priors, mask = pl.pallas_call(
+    far = [swap(array, k) for array, (k, _, _) in zip(sends[1:], cuts[1:])]
+    first, second, third = far[0:2], far[2:4], far[4:6]
+    priors = pl.pallas_call(
         functools.partial(pick_kernel, rows),
-        out_shape=(
-            jax.ShapeDtypeStruct((owners, rows, slots_per), f32),
-            jax.ShapeDtypeStruct((owners, 4, LANES), f32),
-        ),
+        out_shape=jax.ShapeDtypeStruct((owners, rows, slots_per), f32),
         in_specs=[WHOLE] * 2,
-        out_specs=(WHOLE,) * 2,
+        out_specs=WHOLE,
         scratch_shapes=[pltpu.VMEM((TILE, CHUNK), bf16)],
         compiler_params=PARAMS,
+        cost_estimate=cost(1024),
         name="pick",
     )(arrived, parts)
-    tables = [mask] + [swap(mask, k) for k in (1, 2, 3)]
     at_home = lax.all_to_all(priors, "cols", split_axis=0, concat_axis=0, tiled=True)
-    at_home, *second = lax.optimization_barrier((at_home, *second))
-    keep, send = pl.pallas_call(
+    at_home, *first = lax.optimization_barrier((at_home, *first))
+    everyone = pl.pallas_call(
         place_kernel,
-        out_shape=(jax.ShapeDtypeStruct((rows, batches // 2 * per), f32),) * 2,
-        in_specs=[WHOLE] * 2,
-        out_specs=(WHOLE,) * 2,
+        out_shape=jax.ShapeDtypeStruct((owners, batches * rows + table.shape[0], per), f32),
+        in_specs=[WHOLE] * 3,
+        out_specs=WHOLE,
         compiler_params=PARAMS,
         name="place",
-    )(at_home, sid)
-    got = swap(send, 1)
-    chip = jnp.where(
-        core == 0, jnp.concatenate([keep, got], axis=0), jnp.concatenate([got, keep], axis=0)
-    )
-    everyone = jnp.broadcast_to(chip[None], (owners,) + chip.shape)
+    )(at_home, sid, table)
+    everyone, near, *second = lax.optimization_barrier((everyone, sends[0], *second))
+    near = swap(near, 1)
     mine = lax.all_to_all(everyone, "cols", split_axis=0, concat_axis=0, tiled=True)
     mine, *third = lax.optimization_barrier((mine, *third))
-    over_x = swap(mine, 2)
-    cm, cx = swap(mine, 1), swap(over_x, 1)
-
-    obs_chunks = batches * owners * per // CHUNK
-    x_chunks = tiles * members // CHUNK
-    masks = pl.pallas_call(
-        functools.partial(mask_kernel, tiles, members),
-        out_shape=jax.ShapeDtypeStruct((obs_chunks + x_chunks, kinds, CHUNK), f32),
-        in_specs=[WHOLE] * 5,
-        out_specs=WHOLE,
-        compiler_params=PARAMS,
-        name="masks",
-    )(arrived, *tables)
     pieces = pl.pallas_call(
         split_kernel,
         out_shape=jax.ShapeDtypeStruct((2 * members, cells), bf16),
@@ -376,19 +403,11 @@
         out_specs=WHOLE,
         compiler_params=PARAMS,
         name="split",
-    )(own, near, *first, *second, *third)
-    return pl.pallas_call(
-        functools.partial(window_kernel, tiles, rows),
-        out_shape=jax.ShapeDtypeStruct((members, cells), f32),
-        in_specs=[WHOLE] * 7,
-        out_specs=WHOLE,
-        scratch_shapes=[
-            pltpu.VMEM((obs_chunks + x_chunks, members, CHUNK), f32),
-            pltpu.VMEM((owners * members, 3 * members), bf16),
-        ],
-        compiler_params=PARAMS,
-        name="window",
-    )(mine, over_x, cm, cx, arrived, masks, pieces)
+    )(state, near, *first, *second, *third)
+    by_core, by_x = swap(mine, 1), swap(mine, 2)
+    by_x, pieces = lax.optimization_barrier((by_x, pieces))
+    by_both = swap(by_x, 1)
+    return window_call(tiles, rows, kinds, mine, by_core, by_x, by_both, arrived, pieces)
 
 
 def innovations(prior_obs, observed, obs_noise, accepted):

time: 105 us -> 73.4 us (0.70)
  waiting for transfers between devices: 43.3 us -> 21.1 us
  blocking collectives: 0 us -> 9.64 us
  starting transfers between devices: 25.7 us -> 17.9 us
  local copies, waits for them, and re-layouts: 7.36 us -> 0.01 us
  Pallas kernels: 28.3 us -> 24.3 us
    ppermute x14 -> x10, waiting for transfers between devices: 36.2 us -> 16.8 us  [swap(): return lax.ppermute(array, 'mem', [(i, i ^ k) for i in range(4)])]
    all_to_all x0 -> x1, blocking collectives: none -> 9.64 us  [fast(): lax.all_to_all(priors, 'cols', split_axis=0, concat_axis=0, tiled=True)]
    all_to_all x1 -> x0, waiting for transfers between devices: 7.11 us -> none  [fast(): lax.all_to_all(priors, 'cols', split_axis=0, concat_axis=0, tiled=True)]
    all_to_all x1 -> x0, starting transfers between devices: 5.94 us -> none  [fast(): lax.all_to_all(priors, 'cols', split_axis=0, concat_axis=0, tiled=True)]
    dynamic_slice x3 -> x0, local copies, waits for them, and re-layouts: 5.9 us -> none  [the longest x2 3.2 us: piece(): lax.dynamic_slice_in_dim(state, (mem ^ k) * cells + begin, width, 1)]
    pallas_call x4, Pallas kernels: 22.9 us -> 17.4 us  [the longest x1 9.26 us: window_call(): pl.pallas_call(functools.partial(window_kernel, tiles, rows), out_shape=j...]
    all_to_all x1, waiting for transfers between devices: 0.01 us -> 3.27 us  [fast(): lax.all_to_all(msg, 'cols', split_axis=0, concat_axis=0, tiled=True)]
    ppermute x14 -> x10, starting transfers between devices: 9.51 us -> 8.24 us  [swap(): return lax.ppermute(array, 'mem', [(i, i ^ k) for i in range(4)])]
  transfers between devices with their start and end apart: 17 -> 12, of which waited for: 9 -> 6; matrix products, arithmetic and copies ran while one was open for 3% -> 0% of each run, Pallas kernels for 10% -> 13%
where the time goes in v2:
time: 73.4 us; the launch traced here: 73 us
  Pallas kernels  24.3 us (33%)
  waiting for transfers between devices  21.1 us (29%)
  starting transfers between devices  17.9 us (24%)
  blocking collectives  9.64 us (13%)
    ppermute x10, waiting for transfers between devices, swap(): return lax.ppermute(array, 'mem', [(i, i ^ k) for i in range(4)])  16.8 us
    all_to_all x1, blocking collectives, fast(): lax.all_to_all(priors, 'cols', split_axis=0, concat_axis=0, tiled=True)  9.64 us
    pallas_call x1, Pallas kernels, window_call(): pl.pallas_call(functools.partial(window_kernel, tiles, rows), out_shape=j...  9.26 us
    ppermute x10, starting transfers between devices, swap(): return lax.ppermute(array, 'mem', [(i, i ^ k) for i in range(4)])  8.24 us
    all_to_all x1, starting transfers between devices, fast(): lax.all_to_all(msg, 'cols', split_axis=0, concat_axis=0, tiled=True)  5.83 us
    all_to_all x1, starting transfers between devices, fast(): lax.all_to_all(everyone, 'cols', split_axis=0, concat_axis=0, tiled=True)  3.79 us
    pallas_call x1, Pallas kernels, fast(): pl.pallas_call(functools.partial(pick_kernel, rows), out_shape=jax.ShapeD...  3.67 us
    pallas_call x1, Pallas kernels, fast(): pl.pallas_call(functools.partial(cut_kernel, cuts), out_shape=tuple((jax....  3.34 us
  transfers between devices with their start and end apart: 12, of which 6 were waited for; matrix products, arithmetic and copies ran while one was open for 0% of the time, Pallas kernels for 13%

profile of v2, /device:TPU:0, one launch (start us, length us, event | category | flops | bytes accessed | tf_op | source)
XLA Modules:
  0.0 73.0 jit_solution(3285867670848087440)
XLA Ops:
  0.0 2.0 %route.1 = (f32[8,20,128]{2,1,0:T(8,128)}, s32[4,128]{1,0:T(4,128)}, f32[4,128]{1,0:T(4,128)}) custom-call(s32[4,1,128]{2,1,0:T(1,128)} %bitcast.7, s32[4,128]{1,0:T(4,128)} %refs_1_.1, s32[4,4,128]{2,1,0:T(4,128)} %bitcast.6, f32[4,128]{1,0:T(4,128)} %refs_3_.1, f32[4,128]{1,0:T(4,128)} %refs_4_.1, s32[4,128]{1,0:T(4,128)} %refs_5_.1, s32[32,16]{1,0:T(8,128)} %bitcast.5), custom_call_target="tpu_custom_call" | custom-call | tf_op jit(solution)/shard_map/route/pallas_call | solution.py:332
  2.0 3.3 %cut.1 = (f32[20,8192]{1,0:T(8,128)}, f32[20,4096]{1,0:T(8,128)}, f32[20,4096]{1,0:T(8,128)}, f32[20,2048]{1,0:T(8,128)}, f32[20,2048]{1,0:T(8,128)}, /*index=5*/f32[20,2048]{1,0:T(8,128)}, f32[20,2048]{1,0:T(8,128)}) custom-call(f32[20,32768]{1,0:T(8,128)} %refs_0_), custom_call_target="tpu_custom_call" | custom-call | bytes 1024 | tf_op jit(solution)/shard_map/cut/pallas_call | solution.py:350
  5.4 3.0 %collective-permute-start = (f32[20,4096]{1,0:T(8,128)}, f32[20,4096]{1,0:T(8,128)}, u32[]{:S(2)}, u32[]{:S(2)}) collective-permute-start(f32[20,4096]{1,0:T(8,128)} %get-tuple-element.32), channel_id=1, source_target_pairs={{0,2},{1,3},{2,0},{3,1},{4,6},{5,7},{6,4},{7,5},{8,10},{9,11},{10,... | collective-permute-start | bytes 983048 | tf_op jit(solution)/shard_map/ppermute | solution.py:371
  8.4 0.0 collective-permute-start.1
  8.4 5.8 %all-to-all-start = ((f32[8,20,128]{2,1,0:T(8,128)}), f32[8,20,128]{2,1,0:T(8,128)S(1)}, u32[]{:S(2)}, u32[]{:S(2)}) async-start(f32[8,20,128]{2,1,0:T(8,128)} %get-tuple-element.30), calls=%async_computation | async-start | bytes 196608 | tf_op jit(solution)/shard_map/all_to_all | solution.py:346
  14.2 1.2 %collective-permute-start.2 = (f32[20,2048]{1,0:T(8,128)}, f32[20,2048]{1,0:T(8,128)S(1)}, u32[]{:S(2)}, u32[]{:S(2)}) collective-permute-start(f32[20,2048]{1,0:T(8,128)} %get-tuple-element.38), channel_id=1, source_target_pairs={{0,2},{1,3},{2,0},{3,1},{4,6},{5,7},{6,4},{7,5},{8,10},{9,11},{10,... | collective-permute-start | bytes 491528 | tf_op jit(solution)/shard_map/ppermute | solution.py:371
  15.4 0.5 collective-permute-start.3
  15.9 2.3 %prepare.1.parts_ref = bf16[3072,512]{1,0:T(8,128)(2,1)S(1)} custom-call(f32[20,32768]{1,0:T(8,128)} %refs_0_), custom_call_target="tpu_custom_call" | custom-call | bytes 1024 | tf_op jit(solution)/shard_map/prepare/pallas_call | solution.py:360
  18.3 3.3 %all-to-all-done.msg_ref.info_ref = f32[8,20,128]{2,1,0:T(8,128)S(1)} async-done(((f32[8,20,128]{2,1,0:T(8,128)}), f32[8,20,128]{2,1,0:T(8,128)S(1)}, u32[]{:S(2)}, u32[]{:S(2)}) %all-to-all-start) | async-done | bytes 81952 | tf_op jit(solution)/shard_map/all_to_all | solution.py:346
  21.5 3.7 %pick.1 = f32[8,20,128]{2,1,0:T(8,128)S(1)} custom-call(f32[8,20,128]{2,1,0:T(8,128)S(1)} %all-to-all-done.msg_ref.info_ref, bf16[3072,512]{1,0:T(8,128)(2,1)S(1)} %prepare.1.parts_ref), custom_call_target="tpu_custom_call" | custom-call | bytes 1024 | tf_op jit(solution)/shard_map/pick/pallas_call | solution.py:375
  25.2 9.6 %all_to_all.15.got_ref = f32[8,20,128]{2,1,0:T(8,128)S(1)} all-to-all(f32[8,20,128]{2,1,0:T(8,128)S(1)} %pick.1), channel_id=1, replica_groups=mesh['cols'=8,'mem'=4] {'cols'}, dimensions={0} | all-to-all | bytes 163840 | tf_op jit(solution)/shard_map/all_to_all | solution.py:385
  34.9 0.0 collective-permute-done.refs_2_
  34.9 0.0 collective-permute-done.1.refs_3_
  34.9 1.1 %place.1 = f32[8,84,128]{2,1,0:T(8,128)} custom-call(f32[8,20,128]{2,1,0:T(8,128)S(1)} %all_to_all.15.got_ref, s32[4,128]{1,0:T(4,128)S(1)} %copy-done, f32[4,128]{1,0:T(4,128)S(1)} %copy-done.1), custom_call_target="tpu_custom_call" | custom-call | tf_op jit(solution)/shard_map/place/pallas_call | solution.py:387
  36.0 0.0 collective-permute-done.2.refs_4_
  36.0 0.0 collective-permute-done.3.refs_5_
  36.0 3.8 %all-to-all-start.2 = ((f32[8,84,128]{2,1,0:T(8,128)}), f32[8,84,128]{2,1,0:T(8,128)S(1)}, u32[]{:S(2)}, u32[]{:S(2)}) async-start(f32[8,84,128]{2,1,0:T(8,128)} %place.1), calls=%async_computation.2 | async-start | bytes 720896 | tf_op jit(solution)/shard_map/all_to_all | solution.py:397
  39.8 0.5 collective-permute-start.8
  40.3 1.5 %collective-permute-start.4 = (f32[20,2048]{1,0:T(8,128)}, f32[20,2048]{1,0:T(8,128)S(1)}, u32[]{:S(2)}, u32[]{:S(2)}) collective-permute-start(f32[20,2048]{1,0:T(8,128)} %get-tuple-element.41), channel_id=1, source_target_pairs={{0,2},{1,3},{2,0},{3,1},{4,6},{5,7},{6,4},{7,5},{8,10},{9,11},{10,... | collective-permute-start | bytes 491528 | tf_op jit(solution)/shard_map/ppermute | solution.py:371
  41.8 0.0 collective-permute-start.5
  41.8 6.5 %collective-permute-done.4.refs_6_ = f32[20,2048]{1,0:T(8,128)S(1)} collective-permute-done((f32[20,2048]{1,0:T(8,128)}, f32[20,2048]{1,0:T(8,128)S(1)}, u32[]{:S(2)}, u32[]{:S(2)}) %collective-permute-start.4) | collective-permute-done | bytes 163872 | tf_op jit(solution)/shard_map/ppermute | solution.py:371
  48.3 2.5 %collective-permute-done.5.refs_7_ = f32[20,2048]{1,0:T(8,128)S(1)} collective-permute-done((f32[20,2048]{1,0:T(8,128)}, f32[20,2048]{1,0:T(8,128)S(1)}, u32[]{:S(2)}, u32[]{:S(2)}) %collective-permute-start.5) | collective-permute-done | bytes 163872 | tf_op jit(solution)/shard_map/ppermute | solution.py:371
  50.7 1.0 %all-to-all-done.2.a_ref = f32[8,84,128]{2,1,0:T(8,128)S(1)} async-done(((f32[8,84,128]{2,1,0:T(8,128)}), f32[8,84,128]{2,1,0:T(8,128)S(1)}, u32[]{:S(2)}, u32[]{:S(2)}) %all-to-all-start.2) | async-done | bytes 344096 | tf_op jit(solution)/shard_map/all_to_all | solution.py:397
  51.7 1.5 %collective-permute-start.7 = (f32[8,84,128]{2,1,0:T(8,128)S(1)}, f32[8,84,128]{2,1,0:T(8,128)S(1)}, u32[]{:S(2)}, u32[]{:S(2)}) collective-permute-start(f32[8,84,128]{2,1,0:T(8,128)S(1)} %all-to-all-done.2.a_ref), channel_id=1, source_target_pairs={{0,2},{1,3},{2,0},{3,1},{4,6},{5,7},{6,4},{7,5},{8,10},{9,11},{10,... | collective-permute-start | bytes 1032200 | tf_op jit(solution)/shard_map/ppermute | solution.py:371
  53.2 0.0 collective-permute-start.6
  53.2 0.0 collective-permute-done.8.refs_1_
  53.2 2.6 %split.1.ens_ref = bf16[160,8192]{1,0:T(8,128)(2,1)S(1)} custom-call(f32[20,32768]{1,0:T(8,128)} %refs_0_, f32[20,8192]{1,0:T(8,128)S(1)} %collective-permute-done.8.refs_1_, f32[20,4096]{1,0:T(8,128)} %collective-permute-done.refs_2_, f32[20,4096]{1,0:T(8,128)} %collective-permute-done.1.refs_3_, f32[20,2048]{1,0:T(8,128)S(1)} %collective-permute-done.2.refs_4_, ...), custom_call_target="tpu_custom_call" | custom-call | tf_op jit(solution)/shard_map/split/pallas_call | solution.py:399
  55.8 6.2 %collective-permute-done.7.c_ref = f32[8,84,128]{2,1,0:T(8,128)S(1)} collective-permute-done((f32[8,84,128]{2,1,0:T(8,128)S(1)}, f32[8,84,128]{2,1,0:T(8,128)S(1)}, u32[]{:S(2)}, u32[]{:S(2)}) %collective-permute-start.7) | collective-permute-done | bytes 344096 | tf_op jit(solution)/shard_map/ppermute | solution.py:371
  62.0 0.0 collective-permute-start.9
  62.0 0.0 collective-permute-done.6.b_ref
  62.0 1.7 %collective-permute-done.9.d_ref = f32[8,84,128]{2,1,0:T(8,128)S(1)} collective-permute-done((f32[8,84,128]{2,1,0:T(8,128)S(1)}, f32[8,84,128]{2,1,0:T(8,128)S(1)}, u32[]{:S(2)}, u32[]{:S(2)}) %collective-permute-start.9) | collective-permute-done | bytes 344096 | tf_op jit(solution)/shard_map/ppermute | solution.py:371
  63.7 9.3 %window.1 = f32[80,8192]{1,0:T(8,128)} custom-call(f32[8,84,128]{2,1,0:T(8,128)S(1)} %all-to-all-done.2.a_ref, f32[8,84,128]{2,1,0:T(8,128)S(1)} %collective-permute-done.6.b_ref, f32[8,84,128]{2,1,0:T(8,128)S(1)} %collective-permute-done.7.c_ref, f32[8,84,128]{2,1,0:T(8,128)S(1)} %collective-permute-done.9.d_ref, ...), custom_call_target="tpu_custom_call" | custom-call | tf_op jit(solution)/shard_map/window/pallas_call | solution.py:295
  (4 shorter events, 0.0 us)
Async XLA Ops:
  5.4 29.5 %collective-permute-start = (f32[20,4096]{1,0:T(8,128)}, f32[20,4096]{1,0:T(8,128)}, u32[]{:S(2)}, u32[]{:S(2)}) collective-permute-start(f32[20,4096]{1,0:T(8,128)} %get-tuple-element.32), channel_id=1, source_target_pairs={{0,2},{1,3},{2,0},{3,1},{4,6},{5,7},{6,4},{7,5},{8,10},{9,11},{10,... | collective-permute-start | bytes 983048 | tf_op jit(solution)/shard_map/ppermute | solution.py:371
  8.4 26.5 %collective-permute-start.1 = (f32[20,4096]{1,0:T(8,128)}, f32[20,4096]{1,0:T(8,128)}, u32[]{:S(2)}, u32[]{:S(2)}) collective-permute-start(f32[20,4096]{1,0:T(8,128)} %get-tuple-element.33), channel_id=1, source_target_pairs={{0,3},{1,2},{2,1},{3,0},{4,7},{5,6},{6,5},{7,4},{8,11},{9,10},{10,... | collective-permute-start | bytes 983048 | tf_op jit(solution)/shard_map/ppermute | solution.py:371
  8.4 13.1 %all-to-all-start = ((f32[8,20,128]{2,1,0:T(8,128)}), f32[8,20,128]{2,1,0:T(8,128)S(1)}, u32[]{:S(2)}, u32[]{:S(2)}) async-start(f32[8,20,128]{2,1,0:T(8,128)} %get-tuple-element.30), calls=%async_computation | async-start | bytes 196608 | tf_op jit(solution)/shard_map/all_to_all | solution.py:346
  14.2 21.7 %collective-permute-start.2 = (f32[20,2048]{1,0:T(8,128)}, f32[20,2048]{1,0:T(8,128)S(1)}, u32[]{:S(2)}, u32[]{:S(2)}) collective-permute-start(f32[20,2048]{1,0:T(8,128)} %get-tuple-element.38), channel_id=1, source_target_pairs={{0,2},{1,3},{2,0},{3,1},{4,6},{5,7},{6,4},{7,5},{8,10},{9,11},{10,... | collective-permute-start | bytes 491528 | tf_op jit(solution)/shard_map/ppermute | solution.py:371
  15.4 20.6 %collective-permute-start.3 = (f32[20,2048]{1,0:T(8,128)}, f32[20,2048]{1,0:T(8,128)}, u32[]{:S(2)}, u32[]{:S(2)}) collective-permute-start(f32[20,2048]{1,0:T(8,128)} %get-tuple-element.39), channel_id=1, source_target_pairs={{0,3},{1,2},{2,1},{3,0},{4,7},{5,6},{6,5},{7,4},{8,11},{9,10},{10,... | collective-permute-start | bytes 491528 | tf_op jit(solution)/shard_map/ppermute | solution.py:371
  18.2 16.6 %copy-start = (s32[4,128]{1,0:T(4,128)S(1)}, s32[4,128]{1,0:T(4,128)}, u32[]{:S(2)}) copy-start(s32[4,128]{1,0:T(4,128)} %get-tuple-element.35.sid_ref) | copy-start | bytes 6148
  18.3 16.6 %copy-start.1 = (f32[4,128]{1,0:T(4,128)S(1)}, f32[4,128]{1,0:T(4,128)}, u32[]{:S(2)}) copy-start(f32[4,128]{1,0:T(4,128)} %get-tuple-element.36.table_ref) | copy-start | bytes 6148
  36.0 15.7 %all-to-all-start.2 = ((f32[8,84,128]{2,1,0:T(8,128)}), f32[8,84,128]{2,1,0:T(8,128)S(1)}, u32[]{:S(2)}, u32[]{:S(2)}) async-start(f32[8,84,128]{2,1,0:T(8,128)} %place.1), calls=%async_computation.2 | async-start | bytes 720896 | tf_op jit(solution)/shard_map/all_to_all | solution.py:397
  39.8 13.4 %collective-permute-start.8 = (f32[20,8192]{1,0:T(8,128)}, f32[20,8192]{1,0:T(8,128)S(1)}, u32[]{:S(2)}, u32[]{:S(2)}) collective-permute-start(f32[20,8192]{1,0:T(8,128)} %get-tuple-element.44), channel_id=1, source_target_pairs={{0,1},{1,0},{2,3},{3,2},{4,5},{5,4},{6,7},{7,6},{8,9},{9,8},{10,11... | collective-permute-start | bytes 1966088 | tf_op jit(solution)/shard_map/ppermute | solution.py:371
  40.3 8.0 %collective-permute-start.4 = (f32[20,2048]{1,0:T(8,128)}, f32[20,2048]{1,0:T(8,128)S(1)}, u32[]{:S(2)}, u32[]{:S(2)}) collective-permute-start(f32[20,2048]{1,0:T(8,128)} %get-tuple-element.41), channel_id=1, source_target_pairs={{0,2},{1,3},{2,0},{3,1},{4,6},{5,7},{6,4},{7,5},{8,10},{9,11},{10,... | collective-permute-start | bytes 491528 | tf_op jit(solution)/shard_map/ppermute | solution.py:371
  41.8 8.9 %collective-permute-start.5 = (f32[20,2048]{1,0:T(8,128)}, f32[20,2048]{1,0:T(8,128)S(1)}, u32[]{:S(2)}, u32[]{:S(2)}) collective-permute-start(f32[20,2048]{1,0:T(8,128)} %get-tuple-element.42), channel_id=1, source_target_pairs={{0,3},{1,2},{2,1},{3,0},{4,7},{5,6},{6,5},{7,4},{8,11},{9,10},{10,... | collective-permute-start | bytes 491528 | tf_op jit(solution)/shard_map/ppermute | solution.py:371
  51.7 10.3 %collective-permute-start.7 = (f32[8,84,128]{2,1,0:T(8,128)S(1)}, f32[8,84,128]{2,1,0:T(8,128)S(1)}, u32[]{:S(2)}, u32[]{:S(2)}) collective-permute-start(f32[8,84,128]{2,1,0:T(8,128)S(1)} %all-to-all-done.2.a_ref), channel_id=1, source_target_pairs={{0,2},{1,3},{2,0},{3,1},{4,6},{5,7},{6,4},{7,5},{8,10},{9,11},{10,... | collective-permute-start | bytes 1032200 | tf_op jit(solution)/shard_map/ppermute | solution.py:371
  53.2 8.8 %collective-permute-start.6 = (f32[8,84,128]{2,1,0:T(8,128)S(1)}, f32[8,84,128]{2,1,0:T(8,128)S(1)}, u32[]{:S(2)}, u32[]{:S(2)}) collective-permute-start(f32[8,84,128]{2,1,0:T(8,128)S(1)} %all-to-all-done.2.a_ref), channel_id=1, source_target_pairs={{0,1},{1,0},{2,3},{3,2},{4,5},{5,4},{6,7},{7,6},{8,9},{9,8},{10,11... | collective-permute-start | bytes 1032200 | tf_op jit(solution)/shard_map/ppermute | solution.py:371
  62.0 1.7 %collective-permute-start.9 = (f32[8,84,128]{2,1,0:T(8,128)S(1)}, f32[8,84,128]{2,1,0:T(8,128)S(1)}, u32[]{:S(2)}, u32[]{:S(2)}) collective-permute-start(f32[8,84,128]{2,1,0:T(8,128)S(1)} %collective-permute-done.7.c_ref), channel_id=1, source_target_pairs={{0,1},{1,0},{2,3},{3,2},{4,5},{5,4},{6,7},{7,6},{8,9},{9,8},{10,11... | collective-permute-start | bytes 1032200 | tf_op jit(solution)/shard_map/ppermute | solution.py:371

commit v3 on v2

--- a/solution.py
+++ b/solution.py
@@ -13,11 +13,13 @@
 LANES = 128
 CHUNK = 256
 TILE = 512
+SWAPS = ((2, 0, 8), (3, 0, 8), (2, 8, 13), (3, 8, 13), (2, 13, 16), (3, 13, 16))
 PAD = 24
 WHOLE = pl.BlockSpec()
 FAR = pl.BlockSpec(memory_space=pltpu.HBM)
 PARAMS = pltpu.CompilerParams(vmem_limit_bytes=48 * 1024 * 1024)
 ALONE = pltpu.CompilerParams(vmem_limit_bytes=64 * 1024 * 1024)
+NEARLY = pltpu.CompilerParams(vmem_limit_bytes=64 * 1024 * 1024 - 200 * 1024)
 
 
 def cost(amount):
@@ -41,13 +43,27 @@
     return jnp.where(iota((slots, sid.shape[1]), 0) == sid, 1.0, 0.0).astype(bf16)
 
 
-def route_kernel(owners, slots_per, *refs):
-    ins, (msg_ref, sid_ref, table_ref), here, sems = refs[0:7], refs[7:10], refs[10:17], refs[17]
+def route_kernel(owners, slots_per, cuts, *refs):
+    n = len(cuts)
+    ins, state_ref, (msg_ref, sid_ref) = refs[0:7], refs[7], refs[8:10]
+    sends, here, held, sems = refs[10 : 10 + n], refs[10 + n : 17 + n], refs[17 + n : 17 + 2 * n], refs[17 + 2 * n]
+    cells = state_ref.shape[1] // 4
+    mem = lax.axis_index("mem")
     copies = [pltpu.make_async_copy(a, b, sems.at[i]) for i, (a, b) in enumerate(zip(ins, here))]
     for copy in copies:
         copy.start()
+    cutting = []
+    for i, (k, begin, end) in enumerate(cuts):
+        start = pl.multiple_of((mem ^ k) * cells + begin, LANES)
+        cutting.append(pltpu.make_async_copy(state_ref.at[:, pl.ds(start, end - begin)], held[i], sems.at[7 + i]))
+        cutting[-1].start()
     for copy in copies:
         copy.wait()
+    for copy in cutting:
+        copy.wait()
+    sending = [pltpu.make_async_copy(held[i], sends[i], sems.at[7 + n + i]) for i in range(n)]
+    for copy in sending:
+        copy.start()
     owner_ref, tile_ref, off_ref, val_ref, var_ref, acc_ref, mask_ref = here
     batches, _, per = owner_ref.shape
     slots = owners * slots_per
@@ -70,24 +86,27 @@
             [(cells >> 7).astype(f32), (cells & 127).astype(f32), jnp.ones((8, per), f32)], axis=0
         ).astype(bf16)
         total = total + dot(fields, slot_rows(sid, slots), ((1,), (1,)))
-    cells = total[0:4] * 128.0 + total[4:8] + (total[8:12] - 1.0)
+    where = total[0:4] * 128.0 + total[4:8] + (total[8:12] - 1.0)
     tiles = mask_ref.shape[1]
     kinds = mask_ref.shape[0]
     spread_out = jnp.where(iota((kinds, LANES), 0) == (iota((kinds, LANES), 1) & (kinds - 1)), 1.0, 0.0)
     wide = dot(mask_ref[...].astype(bf16), spread_out.astype(bf16), ((0,), (0,)))
     group = LANES // kinds
     lane_tile = iota((tiles, LANES), 1) // kinds
-    for r in range(tiles // group):
-        here = iota((tiles, LANES), 0) == lane_tile + r * group
-        table_ref[r : r + 1, :] = jnp.sum(jnp.where(here, wide, 0.0), axis=0, keepdims=True)
+    table = [
+        jnp.sum(jnp.where(iota((tiles, LANES), 0) == lane_tile + r * group, wide, 0.0), axis=0, keepdims=True)
+        for r in range(tiles // group)
+    ]
     owner = jnp.concatenate([owner_ref[b] for b in range(batches)], axis=0)
     where_tile = (owner * 64 + tile_ref[...]).astype(f32)
     shared = jnp.concatenate(
-        [val_ref[...], var_ref[...], acc_ref[...].astype(f32), where_tile], axis=0
+        [val_ref[...], var_ref[...], acc_ref[...].astype(f32), where_tile] + table, axis=0
     )
     for c in range(owners):
-        msg_ref[c, 0:4, :] = cells[:, c * slots_per : (c + 1) * slots_per]
-        msg_ref[c, 4:20, :] = shared
+        msg_ref[c, 0:4, :] = where[:, c * slots_per : (c + 1) * slots_per]
+        msg_ref[c, 4:24, :] = shared
+    for copy in sending:
+        copy.wait()
 
 
 def cut_kernel(cuts, state_ref, *refs):
@@ -112,10 +131,11 @@
         out_ref[t * 2 * PAD : (t + 1) * 2 * PAD, :] = jnp.concatenate([high, tile - high], axis=0).astype(bf16)
 
 
-def pick_kernel(rows, msg_ref, parts_ref, out_ref, weight_ref):
+def pick_kernel(rows, msg_ref, parts_ref, out_ref, table_ref, weight_ref):
     homes, _, slots_per = msg_ref.shape
     tiles = parts_ref.shape[0] // (2 * PAD)
     each = CHUNK // slots_per
+    table_ref[...] = msg_ref[:, 20:24, :]
     for g in range(homes // each):
         cells = jnp.concatenate([msg_ref[g * each + i, 0:4, :] for i in range(each)], axis=1)
         cells = jnp.maximum(cells.astype(i32), 0)
@@ -133,7 +153,7 @@
             out_ref[g * each + i] = total[0:rows, i * slots_per : (i + 1) * slots_per]
 
 
-def place_kernel(got_ref, sid_ref, table_ref, out_ref):
+def place_kernel(got_ref, sid_ref, out_ref):
     owners, rows, slots_per = got_ref.shape
     batches, per = sid_ref.shape
     slots = owners * slots_per
@@ -149,8 +169,6 @@
         out = out[0:PAD] + out[PAD : 2 * PAD] + out[2 * PAD : 3 * PAD]
         for c in range(owners):
             out_ref[c, b * rows : (b + 1) * rows, :] = out[0:rows]
-    for c in range(owners):
-        out_ref[c, batches * rows :, :] = table_ref[...]
 
 
 def fill_masks(tiles, members, kinds, info_ref, table, mask_ref):
@@ -177,29 +195,33 @@
         mask_ref[idx] = out
 
 
-def split_kernel(*refs):
-    state, near, pieces, out_ref = refs[0], refs[1], refs[2:-1], refs[-1]
-    rows, total = near.shape
+def split_kernel(cuts, *refs):
+    state, received, out_ref = refs[0], refs[1:-1], refs[-1]
+    rows, total = received[0].shape
     here = pl.multiple_of(lax.axis_index("mem") * total, total)
-    begin = 0
-    for i in range(0, len(pieces), 2):
-        end = begin + pieces[i].shape[1]
-        cells = slice(begin, end)
-        own = state[:, pl.ds(here + begin, end - begin)]
-        whole = jnp.concatenate([own, near[:, cells], pieces[i][...], pieces[i + 1][...]], axis=0)
-        high, low = two(whole)
-        out_ref[0 : 4 * rows, cells] = high
-        out_ref[4 * rows : 8 * rows, cells] = low
-        begin = end
-
-
-def window_kernel(tiles, rows, a_ref, b_ref, c_ref, d_ref, info_ref, ens_ref, out_ref, y_ref, w_ref, mask_ref):
+    marks = sorted({cut[1] for cut in cuts} | {cut[2] for cut in cuts})
+    for begin, end in zip(marks[:-1], marks[1:]):
+        parts = [state[:, pl.ds(here + begin, end - begin)]]
+        for k in (1, 2, 3):
+            for ref, (to, first, last) in zip(received, cuts):
+                if to == k and first <= begin and end <= last:
+                    parts.append(ref[:, begin - first : end - first])
+        high, low = two(jnp.concatenate(parts, axis=0))
+        out_ref[0 : 4 * rows, begin:end] = high
+        out_ref[4 * rows : 8 * rows, begin:end] = low
+
+
+def mask_kernel(tiles, rows, info_ref, a_ref, b_ref, c_ref, d_ref, mask_ref):
+    homes = info_ref.shape[0]
+    table = [ref[h] for ref in (a_ref, b_ref, c_ref, d_ref) for h in range(homes)]
+    table = jnp.concatenate(table, axis=0).astype(bf16)
+    fill_masks(tiles, 4 * rows, mask_ref.shape[1], info_ref, table, mask_ref)
+
+
+def window_kernel(tiles, rows, a_ref, b_ref, c_ref, d_ref, info_ref, mask_ref, ens_ref, out_ref, y_ref, w_ref, held_ref, sem):
     homes, all_rows, per = a_ref.shape
     batches = 4
     members = 4 * rows
-    table = [ref[h, batches * rows :, :] for ref in (a_ref, b_ref, c_ref, d_ref) for h in range(homes)]
-    table = jnp.concatenate(table, axis=0).astype(bf16)
-    fill_masks(tiles, members, mask_ref.shape[1], info_ref, table, mask_ref)
     blocks = homes
     mem = lax.axis_index("mem")
     obs_chunks = batches * homes * per // CHUNK
@@ -279,32 +301,38 @@
         stack = jnp.concatenate([first, second, rest - second], axis=0).astype(bf16)
         flat.append(dot(order, stack, ((1,), (0,))))
     flat = jnp.concatenate(flat, axis=1)
+    copies = []
     for t in range(tiles):
         weight = flat[:, t * members : (t + 1) * members]
         high = weight.astype(bf16).astype(f32)
         weight = jnp.concatenate([high, high, weight - high], axis=1).astype(bf16)
         cells = slice(t * size, (t + 1) * size)
         ens_high, ens_low = ens_ref[0:members, cells], ens_ref[members : 2 * members, cells]
-        out_ref[:, cells] = dot(weight, jnp.concatenate([ens_high, ens_low, ens_high], axis=0), ((1,), (0,)))
-
-
-def window_call(tiles, rows, kinds, mine, by_core, by_x, by_both, about, pieces):
+        held_ref[t] = dot(weight, jnp.concatenate([ens_high, ens_low, ens_high], axis=0), ((1,), (0,)))
+        copies.append(pltpu.make_async_copy(held_ref.at[t], out_ref.at[:, cells], sem.at[t]))
+        copies[-1].start()
+    for copy in copies:
+        copy.wait()
+
+
+def window_call(tiles, rows, mine, by_core, by_x, by_both, about, masks, pieces):
     owners, _, per = mine.shape
     members, cells = pieces.shape[0] // 2, pieces.shape[1]
-    chunks = (4 * owners * per + tiles * members) // CHUNK
+    chunks = masks.shape[0]
     return pl.pallas_call(
         functools.partial(window_kernel, tiles, rows),
         out_shape=jax.ShapeDtypeStruct((members, cells), f32),
-        in_specs=[WHOLE] * 6,
-        out_specs=WHOLE,
+        in_specs=[WHOLE] * 7,
+        out_specs=FAR,
         scratch_shapes=[
             pltpu.VMEM((chunks, members, CHUNK), f32),
             pltpu.VMEM((owners * members, 3 * members), bf16),
-            pltpu.VMEM((chunks, kinds, CHUNK), f32),
+            pltpu.VMEM((tiles, members, cells // tiles), f32),
+            pltpu.SemaphoreType.DMA((tiles,)),
         ],
         compiler_params=PARAMS,
         name="window",
-    )(mine, by_core, by_x, by_both, about, pieces)
+    )(mine, by_core, by_x, by_both, about, masks, pieces)
 
 
 def fast(state, obs_value, obs_var, owner, tile_of, offsets, accept, loc_mask):
@@ -329,31 +357,33 @@
         accept,
         loc_mask.transpose(1, 2, 0).reshape(kinds, tiles),
     )
-    msg, sid, table = pl.pallas_call(
-        functools.partial(route_kernel, owners, slots_per),
+    cuts = [(1, 0, cells)] + [(k, cells * a // 16, cells * b // 16) for k, a, b in SWAPS]
+    sooner, later = cuts[1:3], cuts[0:1] + cuts[3:]
+    msg, sid, *first = pl.pallas_call(
+        functools.partial(route_kernel, owners, slots_per, sooner),
         out_shape=(
-            jax.ShapeDtypeStruct((owners, 20, slots_per), f32),
+            jax.ShapeDtypeStruct((owners, 24, slots_per), f32),
             jax.ShapeDtypeStruct((batches, per), i32),
-            jax.ShapeDtypeStruct((tiles * kinds // LANES, LANES), f32),
+            *(jax.ShapeDtypeStruct((rows, end - begin), f32) for _, begin, end in sooner),
         ),
-        in_specs=[FAR] * 7,
-        out_specs=(WHOLE,) * 3,
-        scratch_shapes=[pltpu.VMEM(a.shape, a.dtype) for a in about] + [pltpu.SemaphoreType.DMA((7,))],
+        in_specs=[FAR] * 8,
+        out_specs=(WHOLE,) * 2 + (FAR,) * len(sooner),
+        scratch_shapes=[pltpu.VMEM(a.shape, a.dtype) for a in about]
+        + [pltpu.VMEM((rows, end - begin), f32) for _, begin, end in sooner]
+        + [pltpu.SemaphoreType.DMA((7 + 2 * len(sooner),))],
         compiler_params=ALONE,
         name="route",
-    )(*about)
+    )(*about, state)
     state, msg = lax.optimization_barrier((state, msg))
     arrived = lax.all_to_all(msg, "cols", split_axis=0, concat_axis=0, tiled=True)
 
-    marks = [0, cells * 8 // 16, cells * 12 // 16, cells]
-    cuts = [(1, 0, cells)] + [(k, marks[i], marks[i + 1]) for i in range(3) for k in (2, 3)]
     sends = pl.pallas_call(
-        functools.partial(cut_kernel, cuts),
-        out_shape=tuple(jax.ShapeDtypeStruct((rows, end - begin), f32) for _, begin, end in cuts),
+        functools.partial(cut_kernel, later),
+        out_shape=tuple(jax.ShapeDtypeStruct((rows, end - begin), f32) for _, begin, end in later),
         in_specs=[WHOLE],
-        out_specs=(FAR,) * len(cuts),
-        scratch_shapes=[pltpu.SemaphoreType.DMA((len(cuts),))],
-        compiler_params=ALONE,
+        out_specs=(FAR,) * len(later),
+        scratch_shapes=[pltpu.SemaphoreType.DMA((len(later),))],
+        compiler_params=NEARLY,
         cost_estimate=cost(1024),
         name="cut",
     )(state)
@@ -370,13 +400,17 @@
     def swap(array, k):
         return lax.ppermute(array, "mem", [(i, i ^ k) for i in range(4)])
 
-    far = [swap(array, k) for array, (k, _, _) in zip(sends[1:], cuts[1:])]
-    first, second, third = far[0:2], far[2:4], far[4:6]
-    priors = pl.pallas_call(
+    first = [swap(array, k) for array, (k, _, _) in zip(first, sooner)]
+    far = [swap(array, k) for array, (k, _, _) in zip(sends[1:], later[1:])]
+    second, third = far[0:2], far[2:]
+    priors, table = pl.pallas_call(
         functools.partial(pick_kernel, rows),
-        out_shape=jax.ShapeDtypeStruct((owners, rows, slots_per), f32),
+        out_shape=(
+            jax.ShapeDtypeStruct((owners, rows, slots_per), f32),
+            jax.ShapeDtypeStruct((owners, 4, LANES), f32),
+        ),
         in_specs=[WHOLE] * 2,
-        out_specs=WHOLE,
+        out_specs=(WHOLE,) * 2,
         scratch_shapes=[pltpu.VMEM((TILE, CHUNK), bf16)],
         compiler_params=PARAMS,
         cost_estimate=cost(1024),
@@ -386,28 +420,39 @@
     at_home, *first = lax.optimization_barrier((at_home, *first))
     everyone = pl.pallas_call(
         place_kernel,
-        out_shape=jax.ShapeDtypeStruct((owners, batches * rows + table.shape[0], per), f32),
-        in_specs=[WHOLE] * 3,
+        out_shape=jax.ShapeDtypeStruct((owners, batches * rows, per), f32),
+        in_specs=[WHOLE] * 2,
         out_specs=WHOLE,
         compiler_params=PARAMS,
         name="place",
-    )(at_home, sid, table)
-    everyone, near, *second = lax.optimization_barrier((everyone, sends[0], *second))
+    )(at_home, sid)
+    everyone, near, table, *second = lax.optimization_barrier((everyone, sends[0], table, *second))
+    tables = [table] + [swap(table, k) for k in (1, 2, 3)]
     near = swap(near, 1)
     mine = lax.all_to_all(everyone, "cols", split_axis=0, concat_axis=0, tiled=True)
-    mine, *third = lax.optimization_barrier((mine, *third))
+    mine, *rest = lax.optimization_barrier((mine, *tables, *third))
+    tables, third = rest[:4], rest[4:]
+    masks = pl.pallas_call(
+        functools.partial(mask_kernel, tiles, rows),
+        out_shape=jax.ShapeDtypeStruct(((batches * owners * per + tiles * members) // CHUNK, kinds, CHUNK), f32),
+        in_specs=[WHOLE] * 5,
+        out_specs=WHOLE,
+        compiler_params=PARAMS,
+        cost_estimate=cost(1024),
+        name="masks",
+    )(arrived, *tables)
     pieces = pl.pallas_call(
-        split_kernel,
+        functools.partial(split_kernel, cuts),
         out_shape=jax.ShapeDtypeStruct((2 * members, cells), bf16),
-        in_specs=[WHOLE] * 8,
+        in_specs=[WHOLE] * (1 + len(cuts)),
         out_specs=WHOLE,
         compiler_params=PARAMS,
         name="split",
     )(state, near, *first, *second, *third)
     by_core, by_x = swap(mine, 1), swap(mine, 2)
-    by_x, pieces = lax.optimization_barrier((by_x, pieces))
+    by_x, pieces, masks = lax.optimization_barrier((by_x, pieces, masks))
     by_both = swap(by_x, 1)
-    return window_call(tiles, rows, kinds, mine, by_core, by_x, by_both, arrived, pieces)
+    return window_call(tiles, rows, mine, by_core, by_x, by_both, arrived, masks, pieces)
 
 
 def innovations(prior_obs, observed, obs_noise, accepted):

time: 73.4 us -> 70.7 us (0.963)
  waiting for transfers between devices: 21.1 us -> 13.1 us
  blocking collectives: 9.64 us -> 12.8 us
  starting transfers between devices: 17.9 us -> 19.6 us
    ppermute x10 -> x13, waiting for transfers between devices: 16.8 us -> 13 us  [swap(): return lax.ppermute(array, 'mem', [(i, i ^ k) for i in range(4)])]
    all_to_all x1, blocking collectives: 9.64 us -> 12.8 us  [fast(): lax.all_to_all(priors, 'cols', split_axis=0, concat_axis=0, tiled=True)]
    all_to_all x1, waiting for transfers between devices: 3.27 us -> 0.16 us  [fast(): lax.all_to_all(msg, 'cols', split_axis=0, concat_axis=0, tiled=True)]
    ppermute x10 -> x13, starting transfers between devices: 8.24 us -> 10.2 us  [swap(): return lax.ppermute(array, 'mem', [(i, i ^ k) for i in range(4)])]
    pallas_call x4 -> x5, Pallas kernels: 11.7 us -> 12.9 us  [the longest x1 3.67 us: fast(): pl.pallas_call(functools.partial(pick_kernel, rows), out_shape=(jax.Shape...]
    pallas_call x1, Pallas kernels: 9.26 us -> 8.27 us  [window_call(): pl.pallas_call(functools.partial(window_kernel, tiles, rows), out_shape=j...]
    all_to_all x1, waiting for transfers between devices: 1 us -> 0.01 us  [fast(): lax.all_to_all(everyone, 'cols', split_axis=0, concat_axis=0, tiled=True)]
  transfers between devices with their start and end apart: 12 -> 15, of which waited for: 6 -> 7; matrix products, arithmetic and copies ran while one was open for 0% -> 0% of each run, Pallas kernels for 13% -> 19%
where the time goes in v3:
time: 70.7 us; the launch traced here: 70.3 us
  Pallas kernels  24.5 us (35%)
  starting transfers between devices  19.6 us (28%)
  waiting for transfers between devices  13.1 us (19%)
  blocking collectives  12.8 us (18%)
    ppermute x13, waiting for transfers between devices, swap(): return lax.ppermute(array, 'mem', [(i, i ^ k) for i in range(4)])  13 us
    all_to_all x1, blocking collectives, fast(): lax.all_to_all(priors, 'cols', split_axis=0, concat_axis=0, tiled=True)  12.8 us
    ppermute x13, starting transfers between devices, swap(): return lax.ppermute(array, 'mem', [(i, i ^ k) for i in range(4)])  10.2 us
    pallas_call x1, Pallas kernels, window_call(): pl.pallas_call(functools.partial(window_kernel, tiles, rows), out_shape=j...  8.27 us
    all_to_all x1, starting transfers between devices, fast(): lax.all_to_all(msg, 'cols', split_axis=0, concat_axis=0, tiled=True)  5.83 us
    pallas_call x1, Pallas kernels, fast(): pl.pallas_call(functools.partial(pick_kernel, rows), out_shape=(jax.Shape...  3.67 us
    all_to_all x1, starting transfers between devices, fast(): lax.all_to_all(everyone, 'cols', split_axis=0, concat_axis=0, tiled=True)  3.61 us
    pallas_call x1, Pallas kernels, fast(): pl.pallas_call(functools.partial(cut_kernel, later), out_shape=tuple((jax...  3.05 us
  transfers between devices with their start and end apart: 15, of which 7 were waited for; matrix products, arithmetic and copies ran while one was open for 0% of the time, Pallas kernels for 19%

profile of v3, /device:TPU:0, one launch (start us, length us, event | category | flops | bytes accessed | tf_op | source)
XLA Modules:
  0.0 70.3 jit_solution(8070984868682933118)
XLA Ops:
  0.0 2.9 %route.1 = (f32[8,24,128]{2,1,0:T(8,128)}, s32[4,128]{1,0:T(4,128)}, f32[20,4096]{1,0:T(8,128)}, f32[20,4096]{1,0:T(8,128)}) custom-call(s32[4,1,128]{2,1,0:T(1,128)} %bitcast.7, s32[4,128]{1,0:T(4,128)} %refs_1_.1, s32[4,4,128]{2,1,0:T(4,128)} %bitcast.6, f32[4,128]{1,0:T(4,128)} %refs_3_.1, f32[4,128]{1,0:T(4,128)} %refs_4_.1, s32[4,128]{1,0:T(4,128)} %refs_5_.1, ...), custom_call_target="tpu_custom_call" | custom-call | tf_op jit(solution)/shard_map/route/pallas_call | solution.py:362
  2.9 3.0 %collective-permute-start = (f32[20,4096]{1,0:T(8,128)}, f32[20,4096]{1,0:T(8,128)}, u32[]{:S(2)}, u32[]{:S(2)}) collective-permute-start(f32[20,4096]{1,0:T(8,128)} %get-tuple-element.40), channel_id=1, source_target_pairs={{0,2},{1,3},{2,0},{3,1},{4,6},{5,7},{6,4},{7,5},{8,10},{9,11},{10,... | collective-permute-start | bytes 983048 | tf_op jit(solution)/shard_map/ppermute | solution.py:401
  5.9 5.8 %all-to-all-start = ((f32[8,24,128]{2,1,0:T(8,128)}), f32[8,24,128]{2,1,0:T(8,128)S(1)}, u32[]{:S(2)}, u32[]{:S(2)}) async-start(f32[8,24,128]{2,1,0:T(8,128)} %get-tuple-element.37), calls=%async_computation | async-start | bytes 196608 | tf_op jit(solution)/shard_map/all_to_all | solution.py:378
  11.7 3.1 %cut.1 = (f32[20,8192]{1,0:T(8,128)}, f32[20,2560]{1,0:T(8,128)}, f32[20,2560]{1,0:T(8,128)}, f32[20,1536]{1,0:T(8,128)}, f32[20,1536]{1,0:T(8,128)}) custom-call(f32[20,32768]{1,0:T(8,128)} %refs_0_), custom_call_target="tpu_custom_call" | custom-call | bytes 1024 | tf_op jit(solution)/shard_map/cut/pallas_call | solution.py:380
  14.8 1.2 %collective-permute-start.2 = (f32[20,2560]{1,0:T(8,128)}, f32[20,2560]{1,0:T(8,128)S(1)}, u32[]{:S(2)}, u32[]{:S(2)}) collective-permute-start(f32[20,2560]{1,0:T(8,128)} %get-tuple-element.46), channel_id=1, source_target_pairs={{0,2},{1,3},{2,0},{3,1},{4,6},{5,7},{6,4},{7,5},{8,10},{9,11},{10,... | collective-permute-start | bytes 614408 | tf_op jit(solution)/shard_map/ppermute | solution.py:401
  16.0 0.5 collective-permute-start.3
  16.6 2.3 %prepare.1.parts_ref = bf16[3072,512]{1,0:T(8,128)(2,1)S(1)} custom-call(f32[20,32768]{1,0:T(8,128)} %refs_0_), custom_call_target="tpu_custom_call" | custom-call | bytes 1024 | tf_op jit(solution)/shard_map/prepare/pallas_call | solution.py:390
  18.9 0.2 all-to-all-done.msg_ref.info_ref
  19.0 3.7 %pick.1 = (f32[8,20,128]{2,1,0:T(8,128)S(1)}, f32[8,4,128]{2,1,0:T(4,128)S(1)}) custom-call(f32[8,24,128]{2,1,0:T(8,128)S(1)} %all-to-all-done.msg_ref.info_ref, bf16[3072,512]{1,0:T(8,128)(2,1)S(1)} %prepare.1.parts_ref), custom_call_target="tpu_custom_call" | custom-call | bytes 1024 | tf_op jit(solution)/shard_map/pick/pallas_call | solution.py:406
  22.7 12.8 %all_to_all.15.got_ref = f32[8,20,128]{2,1,0:T(8,128)S(1)} all-to-all(f32[8,20,128]{2,1,0:T(8,128)S(1)} %get-tuple-element.39), channel_id=1, replica_groups=mesh['cols'=8,'mem'=4] {'cols'}, dimensions={0} | all-to-all | bytes 163840 | tf_op jit(solution)/shard_map/all_to_all | solution.py:419
  35.5 1.1 %place.1 = f32[8,80,128]{2,1,0:T(8,128)} custom-call(f32[8,20,128]{2,1,0:T(8,128)S(1)} %all_to_all.15.got_ref, s32[4,128]{1,0:T(4,128)S(1)} %copy-done), custom_call_target="tpu_custom_call" | custom-call | tf_op jit(solution)/shard_map/place/pallas_call | solution.py:421
  36.6 3.6 %all-to-all-start.2 = ((f32[8,80,128]{2,1,0:T(8,128)}), f32[8,80,128]{2,1,0:T(8,128)S(1)}, u32[]{:S(2)}, u32[]{:S(2)}) async-start(f32[8,80,128]{2,1,0:T(8,128)} %place.1), calls=%async_computation.2 | async-start | bytes 655360 | tf_op jit(solution)/shard_map/all_to_all | solution.py:432
  40.2 0.1 collective-permute-start.11
  40.3 1.3 %collective-permute-start.7 = (f32[20,1536]{1,0:T(8,128)}, f32[20,1536]{1,0:T(8,128)S(1)}, u32[]{:S(2)}, u32[]{:S(2)}) collective-permute-start(f32[20,1536]{1,0:T(8,128)} %get-tuple-element.50), channel_id=1, source_target_pairs={{0,2},{1,3},{2,0},{3,1},{4,6},{5,7},{6,4},{7,5},{8,10},{9,11},{10,... | collective-permute-start | bytes 368648 | tf_op jit(solution)/shard_map/ppermute | solution.py:401
  41.6 0.5 collective-permute-start.8
  42.1 1.2 %collective-permute-start.6 = (f32[8,4,128]{2,1,0:T(4,128)S(1)}, f32[8,4,128]{2,1,0:T(4,128)S(1)}, u32[]{:S(2)}, u32[]{:S(2)}) collective-permute-start(f32[8,4,128]{2,1,0:T(4,128)S(1)} %get-tuple-element.60.a_ref), channel_id=1, source_target_pairs={{0,3},{1,2},{2,1},{3,0},{4,7},{5,6},{6,5},{7,4},{8,11},{9,10},{10,... | collective-permute-start | bytes 49160 | tf_op jit(solution)/shard_map/ppermute | solution.py:401
  43.4 0.7 %collective-permute-start.5 = (f32[8,4,128]{2,1,0:T(4,128)S(1)}, f32[8,4,128]{2,1,0:T(4,128)S(1)}, u32[]{:S(2)}, u32[]{:S(2)}) collective-permute-start(f32[8,4,128]{2,1,0:T(4,128)S(1)} %get-tuple-element.60.a_ref), channel_id=1, source_target_pairs={{0,2},{1,3},{2,0},{3,1},{4,6},{5,7},{6,4},{7,5},{8,10},{9,11},{10,... | collective-permute-start | bytes 49160 | tf_op jit(solution)/shard_map/ppermute | solution.py:401
  44.1 3.1 %collective-permute-done.7.refs_6_ = f32[20,1536]{1,0:T(8,128)S(1)} collective-permute-done((f32[20,1536]{1,0:T(8,128)}, f32[20,1536]{1,0:T(8,128)S(1)}, u32[]{:S(2)}, u32[]{:S(2)}) %collective-permute-start.7) | collective-permute-done | bytes 122912 | tf_op jit(solution)/shard_map/ppermute | solution.py:401
  47.2 0.0 collective-permute-start.4
  47.2 2.3 %collective-permute-done.8.refs_7_ = f32[20,1536]{1,0:T(8,128)S(1)} collective-permute-done((f32[20,1536]{1,0:T(8,128)}, f32[20,1536]{1,0:T(8,128)S(1)}, u32[]{:S(2)}, u32[]{:S(2)}) %collective-permute-start.8) | collective-permute-done | bytes 122912 | tf_op jit(solution)/shard_map/ppermute | solution.py:401
  49.4 0.4 collective-permute-done.6.d_ref
  49.8 0.8 %collective-permute-done.5.c_ref = f32[8,4,128]{2,1,0:T(4,128)S(1)} collective-permute-done((f32[8,4,128]{2,1,0:T(4,128)S(1)}, f32[8,4,128]{2,1,0:T(4,128)S(1)}, u32[]{:S(2)}, u32[]{:S(2)}) %collective-permute-start.5) | collective-permute-done | bytes 16416 | tf_op jit(solution)/shard_map/ppermute | solution.py:401
  50.6 0.0 all-to-all-done.2.a_ref
  50.6 1.5 %collective-permute-start.10 = (f32[8,80,128]{2,1,0:T(8,128)S(1)}, f32[8,80,128]{2,1,0:T(8,128)S(1)}, u32[]{:S(2)}, u32[]{:S(2)}) collective-permute-start(f32[8,80,128]{2,1,0:T(8,128)S(1)} %all-to-all-done.2.a_ref), channel_id=1, source_target_pairs={{0,2},{1,3},{2,0},{3,1},{4,6},{5,7},{6,4},{7,5},{8,10},{9,11},{10,... | collective-permute-start | bytes 983048 | tf_op jit(solution)/shard_map/ppermute | solution.py:401
  52.1 0.0 collective-permute-start.9
  52.1 0.6 masks.1.mask_ref
  52.7 2.7 %split.1.ens_ref = bf16[160,8192]{1,0:T(8,128)(2,1)S(1)} custom-call(f32[20,32768]{1,0:T(8,128)} %refs_0_, f32[20,8192]{1,0:T(8,128)S(1)} %collective-permute-done.11.refs_1_, f32[20,4096]{1,0:T(8,128)} %collective-permute-done.refs_2_, f32[20,4096]{1,0:T(8,128)} %collective-permute-done.1.refs_3_, f32[20,2560]{1,0:T(8,128)S(1)} %collective-permute-done.2.refs_4_, ...), custom_call_target="tpu_custom_call" | custom-call | tf_op jit(solution)/shard_map/split/pallas_call | solution.py:444
  55.4 4.8 %collective-permute-done.10.c_ref = f32[8,80,128]{2,1,0:T(8,128)S(1)} collective-permute-done((f32[8,80,128]{2,1,0:T(8,128)S(1)}, f32[8,80,128]{2,1,0:T(8,128)S(1)}, u32[]{:S(2)}, u32[]{:S(2)}) %collective-permute-start.10) | collective-permute-done | bytes 327712 | tf_op jit(solution)/shard_map/ppermute | solution.py:401
  60.2 0.0 collective-permute-start.12
  60.2 0.0 collective-permute-done.9.b_ref
  60.2 1.6 %collective-permute-done.12.d_ref = f32[8,80,128]{2,1,0:T(8,128)S(1)} collective-permute-done((f32[8,80,128]{2,1,0:T(8,128)S(1)}, f32[8,80,128]{2,1,0:T(8,128)S(1)}, u32[]{:S(2)}, u32[]{:S(2)}) %collective-permute-start.12) | collective-permute-done | bytes 327712 | tf_op jit(solution)/shard_map/ppermute | solution.py:401
  61.9 8.3 %window.1 = f32[80,8192]{1,0:T(8,128)} custom-call(f32[8,80,128]{2,1,0:T(8,128)S(1)} %all-to-all-done.2.a_ref, f32[8,80,128]{2,1,0:T(8,128)S(1)} %collective-permute-done.9.b_ref, f32[8,80,128]{2,1,0:T(8,128)S(1)} %collective-permute-done.10.c_ref, f32[8,80,128]{2,1,0:T(8,128)S(1)} %collective-permute-done.12.d_ref, ...), custom_call_target="tpu_custom_call" | custom-call | tf_op jit(solution)/shard_map/window/pallas_call | solution.py:322
  (9 shorter events, 0.0 us)
Async XLA Ops:
  2.9 32.6 %collective-permute-start = (f32[20,4096]{1,0:T(8,128)}, f32[20,4096]{1,0:T(8,128)}, u32[]{:S(2)}, u32[]{:S(2)}) collective-permute-start(f32[20,4096]{1,0:T(8,128)} %get-tuple-element.40), channel_id=1, source_target_pairs={{0,2},{1,3},{2,0},{3,1},{4,6},{5,7},{6,4},{7,5},{8,10},{9,11},{10,... | collective-permute-start | bytes 983048 | tf_op jit(solution)/shard_map/ppermute | solution.py:401
  5.9 29.6 %collective-permute-start.1 = (f32[20,4096]{1,0:T(8,128)}, f32[20,4096]{1,0:T(8,128)}, u32[]{:S(2)}, u32[]{:S(2)}) collective-permute-start(f32[20,4096]{1,0:T(8,128)} %get-tuple-element.41), channel_id=1, source_target_pairs={{0,3},{1,2},{2,1},{3,0},{4,7},{5,6},{6,5},{7,4},{8,11},{9,10},{10,... | collective-permute-start | bytes 983048 | tf_op jit(solution)/shard_map/ppermute | solution.py:401
  5.9 13.1 %all-to-all-start = ((f32[8,24,128]{2,1,0:T(8,128)}), f32[8,24,128]{2,1,0:T(8,128)S(1)}, u32[]{:S(2)}, u32[]{:S(2)}) async-start(f32[8,24,128]{2,1,0:T(8,128)} %get-tuple-element.37), calls=%async_computation | async-start | bytes 196608 | tf_op jit(solution)/shard_map/all_to_all | solution.py:378
  14.8 21.8 %collective-permute-start.2 = (f32[20,2560]{1,0:T(8,128)}, f32[20,2560]{1,0:T(8,128)S(1)}, u32[]{:S(2)}, u32[]{:S(2)}) collective-permute-start(f32[20,2560]{1,0:T(8,128)} %get-tuple-element.46), channel_id=1, source_target_pairs={{0,2},{1,3},{2,0},{3,1},{4,6},{5,7},{6,4},{7,5},{8,10},{9,11},{10,... | collective-permute-start | bytes 614408 | tf_op jit(solution)/shard_map/ppermute | solution.py:401
  16.0 20.5 %collective-permute-start.3 = (f32[20,2560]{1,0:T(8,128)}, f32[20,2560]{1,0:T(8,128)}, u32[]{:S(2)}, u32[]{:S(2)}) collective-permute-start(f32[20,2560]{1,0:T(8,128)} %get-tuple-element.47), channel_id=1, source_target_pairs={{0,3},{1,2},{2,1},{3,0},{4,7},{5,6},{6,5},{7,4},{8,11},{9,10},{10,... | collective-permute-start | bytes 614408 | tf_op jit(solution)/shard_map/ppermute | solution.py:401
  18.9 16.6 %copy-start = (s32[4,128]{1,0:T(4,128)S(1)}, s32[4,128]{1,0:T(4,128)}, u32[]{:S(2)}) copy-start(s32[4,128]{1,0:T(4,128)} %get-tuple-element.43.sid_ref) | copy-start | bytes 6148
  36.6 14.1 %all-to-all-start.2 = ((f32[8,80,128]{2,1,0:T(8,128)}), f32[8,80,128]{2,1,0:T(8,128)S(1)}, u32[]{:S(2)}, u32[]{:S(2)}) async-start(f32[8,80,128]{2,1,0:T(8,128)} %place.1), calls=%async_computation.2 | async-start | bytes 655360 | tf_op jit(solution)/shard_map/all_to_all | solution.py:432
  40.2 12.5 %collective-permute-start.11 = (f32[20,8192]{1,0:T(8,128)}, f32[20,8192]{1,0:T(8,128)S(1)}, u32[]{:S(2)}, u32[]{:S(2)}) collective-permute-start(f32[20,8192]{1,0:T(8,128)} %get-tuple-element.53), channel_id=1, source_target_pairs={{0,1},{1,0},{2,3},{3,2},{4,5},{5,4},{6,7},{7,6},{8,9},{9,8},{10,11... | collective-permute-start | bytes 1966088 | tf_op jit(solution)/shard_map/ppermute | solution.py:401
  40.3 6.9 %collective-permute-start.7 = (f32[20,1536]{1,0:T(8,128)}, f32[20,1536]{1,0:T(8,128)S(1)}, u32[]{:S(2)}, u32[]{:S(2)}) collective-permute-start(f32[20,1536]{1,0:T(8,128)} %get-tuple-element.50), channel_id=1, source_target_pairs={{0,2},{1,3},{2,0},{3,1},{4,6},{5,7},{6,4},{7,5},{8,10},{9,11},{10,... | collective-permute-start | bytes 368648 | tf_op jit(solution)/shard_map/ppermute | solution.py:401
  41.6 7.8 %collective-permute-start.8 = (f32[20,1536]{1,0:T(8,128)}, f32[20,1536]{1,0:T(8,128)S(1)}, u32[]{:S(2)}, u32[]{:S(2)}) collective-permute-start(f32[20,1536]{1,0:T(8,128)} %get-tuple-element.51), channel_id=1, source_target_pairs={{0,3},{1,2},{2,1},{3,0},{4,7},{5,6},{6,5},{7,4},{8,11},{9,10},{10,... | collective-permute-start | bytes 368648 | tf_op jit(solution)/shard_map/ppermute | solution.py:401
  42.1 7.7 %collective-permute-start.6 = (f32[8,4,128]{2,1,0:T(4,128)S(1)}, f32[8,4,128]{2,1,0:T(4,128)S(1)}, u32[]{:S(2)}, u32[]{:S(2)}) collective-permute-start(f32[8,4,128]{2,1,0:T(4,128)S(1)} %get-tuple-element.60.a_ref), channel_id=1, source_target_pairs={{0,3},{1,2},{2,1},{3,0},{4,7},{5,6},{6,5},{7,4},{8,11},{9,10},{10,... | collective-permute-start | bytes 49160 | tf_op jit(solution)/shard_map/ppermute | solution.py:401
  43.4 7.2 %collective-permute-start.5 = (f32[8,4,128]{2,1,0:T(4,128)S(1)}, f32[8,4,128]{2,1,0:T(4,128)S(1)}, u32[]{:S(2)}, u32[]{:S(2)}) collective-permute-start(f32[8,4,128]{2,1,0:T(4,128)S(1)} %get-tuple-element.60.a_ref), channel_id=1, source_target_pairs={{0,2},{1,3},{2,0},{3,1},{4,6},{5,7},{6,4},{7,5},{8,10},{9,11},{10,... | collective-permute-start | bytes 49160 | tf_op jit(solution)/shard_map/ppermute | solution.py:401
  47.2 3.4 %collective-permute-start.4 = (f32[8,4,128]{2,1,0:T(4,128)S(1)}, f32[8,4,128]{2,1,0:T(4,128)S(1)}, u32[]{:S(2)}, u32[]{:S(2)}) collective-permute-start(f32[8,4,128]{2,1,0:T(4,128)S(1)} %get-tuple-element.60.a_ref), channel_id=1, source_target_pairs={{0,1},{1,0},{2,3},{3,2},{4,5},{5,4},{6,7},{7,6},{8,9},{9,8},{10,11... | collective-permute-start | bytes 49160 | tf_op jit(solution)/shard_map/ppermute | solution.py:401
  50.6 9.6 %collective-permute-start.10 = (f32[8,80,128]{2,1,0:T(8,128)S(1)}, f32[8,80,128]{2,1,0:T(8,128)S(1)}, u32[]{:S(2)}, u32[]{:S(2)}) collective-permute-start(f32[8,80,128]{2,1,0:T(8,128)S(1)} %all-to-all-done.2.a_ref), channel_id=1, source_target_pairs={{0,2},{1,3},{2,0},{3,1},{4,6},{5,7},{6,4},{7,5},{8,10},{9,11},{10,... | collective-permute-start | bytes 983048 | tf_op jit(solution)/shard_map/ppermute | solution.py:401
  52.1 8.1 %collective-permute-start.9 = (f32[8,80,128]{2,1,0:T(8,128)S(1)}, f32[8,80,128]{2,1,0:T(8,128)S(1)}, u32[]{:S(2)}, u32[]{:S(2)}) collective-permute-start(f32[8,80,128]{2,1,0:T(8,128)S(1)} %all-to-all-done.2.a_ref), channel_id=1, source_target_pairs={{0,1},{1,0},{2,3},{3,2},{4,5},{5,4},{6,7},{7,6},{8,9},{9,8},{10,11... | collective-permute-start | bytes 983048 | tf_op jit(solution)/shard_map/ppermute | solution.py:401
  60.2 1.6 %collective-permute-start.12 = (f32[8,80,128]{2,1,0:T(8,128)S(1)}, f32[8,80,128]{2,1,0:T(8,128)S(1)}, u32[]{:S(2)}, u32[]{:S(2)}) collective-permute-start(f32[8,80,128]{2,1,0:T(8,128)S(1)} %collective-permute-done.10.c_ref), channel_id=1, source_target_pairs={{0,1},{1,0},{2,3},{3,2},{4,5},{5,4},{6,7},{7,6},{8,9},{9,8},{10,11... | collective-permute-start | bytes 983048 | tf_op jit(solution)/shard_map/ppermute | solution.py:401

commit v4 on v3

--- a/solution.py
+++ b/solution.py
@@ -59,11 +59,6 @@
         cutting[-1].start()
     for copy in copies:
         copy.wait()
-    for copy in cutting:
-        copy.wait()
-    sending = [pltpu.make_async_copy(held[i], sends[i], sems.at[7 + n + i]) for i in range(n)]
-    for copy in sending:
-        copy.start()
     owner_ref, tile_ref, off_ref, val_ref, var_ref, acc_ref, mask_ref = here
     batches, _, per = owner_ref.shape
     slots = owners * slots_per
@@ -86,6 +81,10 @@
             [(cells >> 7).astype(f32), (cells & 127).astype(f32), jnp.ones((8, per), f32)], axis=0
         ).astype(bf16)
         total = total + dot(fields, slot_rows(sid, slots), ((1,), (1,)))
+    sending = [pltpu.make_async_copy(held[i], sends[i], sems.at[7 + n + i]) for i in range(n)]
+    for copy_in, copy_out in zip(cutting, sending):
+        copy_in.wait()
+        copy_out.start()
     where = total[0:4] * 128.0 + total[4:8] + (total[8:12] - 1.0)
     tiles = mask_ref.shape[1]
     kinds = mask_ref.shape[0]
@@ -124,16 +123,17 @@
 
 def prepare_kernel(state_ref, out_ref):
     rows = state_ref.shape[0]
-    fill = jnp.zeros((PAD - rows, TILE), f32)
-    for t in range(state_ref.shape[1] // TILE):
-        tile = jnp.concatenate([state_ref[:, t * TILE : (t + 1) * TILE], fill], axis=0)
-        high = tile.astype(bf16).astype(f32)
-        out_ref[t * 2 * PAD : (t + 1) * 2 * PAD, :] = jnp.concatenate([high, tile - high], axis=0).astype(bf16)
+    for i in range(state_ref.shape[1] // (2 * TILE)):
+        left, right = (state_ref[:, j * TILE : (j + 1) * TILE] for j in (2 * i, 2 * i + 1))
+        pair = jnp.concatenate([left, right], axis=0)
+        high = pair.astype(bf16).astype(f32)
+        out_ref[i * 4 * rows : (i + 1) * 4 * rows, :] = jnp.concatenate([high, pair - high], axis=0).astype(bf16)
 
 
 def pick_kernel(rows, msg_ref, parts_ref, out_ref, table_ref, weight_ref):
     homes, _, slots_per = msg_ref.shape
-    tiles = parts_ref.shape[0] // (2 * PAD)
+    pairs = parts_ref.shape[0] // (4 * rows)
+    below = jnp.where(iota((2 * rows, CHUNK), 0) >= rows, 1, 0)
     each = CHUNK // slots_per
     table_ref[...] = msg_ref[:, 20:24, :]
     for g in range(homes // each):
@@ -143,14 +143,16 @@
         for p in range(4):
             weight = weight + jnp.where(iota((TILE, CHUNK), 0) == (cells[p : p + 1] & (TILE - 1)), 0.25, 0.0)
         weight_ref[...] = weight.astype(bf16)
-        tile = cells[0:1] >> 9
+        tile = (cells[0:1] >> 9) - below
         sums = dot(parts_ref[...], weight_ref[...], ((1,), (0,)))
-        total = jnp.zeros((PAD, CHUNK), f32)
-        for t in range(tiles):
-            both = sums[t * 2 * PAD : t * 2 * PAD + PAD] + sums[t * 2 * PAD + PAD : (t + 1) * 2 * PAD]
-            total = total + jnp.where(tile == t, both, 0.0)
+        total = jnp.zeros((2 * rows, CHUNK), f32)
+        for j in range(pairs):
+            at = j * 4 * rows
+            both = sums[at : at + 2 * rows] + sums[at + 2 * rows : at + 4 * rows]
+            total = total + jnp.where(tile == 2 * j, both, 0.0)
+        total = total[0:rows] + total[rows : 2 * rows]
         for i in range(each):
-            out_ref[g * each + i] = total[0:rows, i * slots_per : (i + 1) * slots_per]
+            out_ref[g * each + i] = total[:, i * slots_per : (i + 1) * slots_per]
 
 
 def place_kernel(got_ref, sid_ref, out_ref):
@@ -164,11 +166,14 @@
     rest = got - first
     second = rest.astype(bf16).astype(f32)
     parts = jnp.concatenate([first, second, rest - second], axis=0).astype(bf16)
+    placed = []
     for b in range(batches):
         out = dot(parts, slot_rows(sid_ref[b : b + 1, :], slots), ((1,), (0,)))
         out = out[0:PAD] + out[PAD : 2 * PAD] + out[2 * PAD : 3 * PAD]
-        for c in range(owners):
-            out_ref[c, b * rows : (b + 1) * rows, :] = out[0:rows]
+        placed.append(out[0:rows])
+    placed = jnp.concatenate(placed, axis=0)
+    for c in range(owners):
+        out_ref[c] = placed
 
 
 def fill_masks(tiles, members, kinds, info_ref, table, mask_ref):
@@ -240,7 +245,6 @@
             tile = tile + jnp.where(column >= t * members, 1, 0)
         y_ref[obs_chunks + q] = jnp.where(member == column - tile * members, 1.0, 0.0)
 
-    lane3 = iota((members, 3 * members), 1)
     for b in range(batches):
         for g in range(homes // 2):
             def field(f):
@@ -264,10 +268,9 @@
                 lanes = slice(i * per, (i + 1) * per)
                 left = jnp.concatenate([ih[:, lanes], ih[:, lanes], il[:, lanes]], axis=1)
                 right = jnp.concatenate([sh[:, lanes], sl[:, lanes], sh[:, lanes]], axis=1)
-                right = jnp.concatenate([right, right, right], axis=0)
                 block = dot(left, right, ((1,), (1,)))
                 high = block.astype(bf16).astype(f32)
-                block = jnp.where(lane3 < 2 * members, high, block - high)
+                block = jnp.concatenate([high, high, block - high], axis=1)
                 h = 2 * g + i
                 w_ref[h * members : (h + 1) * members, :] = block.astype(bf16)
 
@@ -389,7 +392,7 @@
     )(state)
     parts = pl.pallas_call(
         prepare_kernel,
-        out_shape=jax.ShapeDtypeStruct((slab // TILE * 2 * PAD, TILE), bf16),
+        out_shape=jax.ShapeDtypeStruct((slab // TILE * 2 * rows, TILE), bf16),
         in_specs=[WHOLE],
         out_specs=WHOLE,
         compiler_params=PARAMS,

time: 70.7 us -> 69.5 us (0.983)
  Pallas kernels: 24.5 us -> 21.2 us
  local copies, waits for them, and re-layouts: 0.01 us -> 1.89 us
    unnamed x2 -> x4, local copies, waits for them, and re-layouts: 0.01 us -> 1.89 us
    pallas_call x1, Pallas kernels: 2.3 us -> 0.41 us  [fast(): pl.pallas_call(prepare_kernel, out_shape=jax.ShapeDtypeStruct((slab // TI...]
    pallas_call x1, Pallas kernels: 8.27 us -> 7.33 us  [window_call(): pl.pallas_call(functools.partial(window_kernel, tiles, rows), out_shape=j...]
  transfers between devices with their start and end apart: 15 -> 15, of which waited for: 7 -> 8; matrix products, arithmetic and copies ran while one was open for 0% -> 0% of each run, Pallas kernels for 19% -> 16%
where the time goes in v4:
time: 69.5 us; the launch traced here: 69 us
  Pallas kernels  21.2 us (31%)
  starting transfers between devices  19.6 us (28%)
  waiting for transfers between devices  13.3 us (19%)
  blocking collectives  12.7 us (18%)
  local copies, waits for them, and re-layouts  1.89 us (3%)
    all_to_all x1, blocking collectives, fast(): lax.all_to_all(priors, 'cols', split_axis=0, concat_axis=0, tiled=True)  12.7 us
    ppermute x13, waiting for transfers between devices, swap(): return lax.ppermute(array, 'mem', [(i, i ^ k) for i in range(4)])  12.7 us
    ppermute x13, starting transfers between devices, swap(): return lax.ppermute(array, 'mem', [(i, i ^ k) for i in range(4)])  10.2 us
    pallas_call x1, Pallas kernels, window_call(): pl.pallas_call(functools.partial(window_kernel, tiles, rows), out_shape=j...  7.33 us
    all_to_all x1, starting transfers between devices, fast(): lax.all_to_all(msg, 'cols', split_axis=0, concat_axis=0, tiled=True)  5.83 us
    all_to_all x1, starting transfers between devices, fast(): lax.all_to_all(everyone, 'cols', split_axis=0, concat_axis=0, tiled=True)  3.61 us
    pallas_call x1, Pallas kernels, fast(): pl.pallas_call(functools.partial(pick_kernel, rows), out_shape=(jax.Shape...  3.13 us
    pallas_call x1, Pallas kernels, fast(): pl.pallas_call(functools.partial(cut_kernel, later), out_shape=tuple((jax...  3.05 us
  transfers between devices with their start and end apart: 15, of which 8 were waited for; matrix products, arithmetic and copies ran while one was open for 0% of the time, Pallas kernels for 16%

profile of v4, /device:TPU:0, one launch (start us, length us, event | category | flops | bytes accessed | tf_op | source)
XLA Modules:
  0.0 69.0 jit_solution(3265979939371373474)
XLA Ops:
  0.0 3.0 %route.1 = (f32[8,24,128]{2,1,0:T(8,128)}, s32[4,128]{1,0:T(4,128)}, f32[20,4096]{1,0:T(8,128)}, f32[20,4096]{1,0:T(8,128)}) custom-call(s32[4,1,128]{2,1,0:T(1,128)} %bitcast.7, s32[4,128]{1,0:T(4,128)} %refs_1_.1, s32[4,4,128]{2,1,0:T(4,128)} %bitcast.6, f32[4,128]{1,0:T(4,128)} %refs_3_.1, f32[4,128]{1,0:T(4,128)} %refs_4_.1, s32[4,128]{1,0:T(4,128)} %refs_5_.1, ...), custom_call_target="tpu_custom_call" | custom-call | tf_op jit(solution)/shard_map/route/pallas_call | solution.py:365
  3.0 3.0 %collective-permute-start = (f32[20,4096]{1,0:T(8,128)}, f32[20,4096]{1,0:T(8,128)}, u32[]{:S(2)}, u32[]{:S(2)}) collective-permute-start(f32[20,4096]{1,0:T(8,128)} %get-tuple-element.40), channel_id=1, source_target_pairs={{0,2},{1,3},{2,0},{3,1},{4,6},{5,7},{6,4},{7,5},{8,10},{9,11},{10,... | collective-permute-start | bytes 983048 | tf_op jit(solution)/shard_map/ppermute | solution.py:404
  6.0 5.8 %all-to-all-start = ((f32[8,24,128]{2,1,0:T(8,128)}), f32[8,24,128]{2,1,0:T(8,128)S(1)}, u32[]{:S(2)}, u32[]{:S(2)}) async-start(f32[8,24,128]{2,1,0:T(8,128)} %get-tuple-element.37), calls=%async_computation | async-start | bytes 196608 | tf_op jit(solution)/shard_map/all_to_all | solution.py:381
  11.9 3.0 %cut.1 = (f32[20,8192]{1,0:T(8,128)}, f32[20,2560]{1,0:T(8,128)}, f32[20,2560]{1,0:T(8,128)}, f32[20,1536]{1,0:T(8,128)}, f32[20,1536]{1,0:T(8,128)}) custom-call(f32[20,32768]{1,0:T(8,128)} %refs_0_), custom_call_target="tpu_custom_call" | custom-call | bytes 1024 | tf_op jit(solution)/shard_map/cut/pallas_call | solution.py:383
  14.9 1.2 %collective-permute-start.2 = (f32[20,2560]{1,0:T(8,128)}, f32[20,2560]{1,0:T(8,128)S(1)}, u32[]{:S(2)}, u32[]{:S(2)}) collective-permute-start(f32[20,2560]{1,0:T(8,128)} %get-tuple-element.46), channel_id=1, source_target_pairs={{0,2},{1,3},{2,0},{3,1},{4,6},{5,7},{6,4},{7,5},{8,10},{9,11},{10,... | collective-permute-start | bytes 614408 | tf_op jit(solution)/shard_map/ppermute | solution.py:404
  16.2 0.5 collective-permute-start.3
  16.7 1.9 %copy-done = f32[20,32768]{1,0:T(8,128)S(1)} copy-done((f32[20,32768]{1,0:T(8,128)S(1)}, f32[20,32768]{1,0:T(8,128)}, u32[]{:S(2)}) %copy-start) | copy-done | bytes 2621464
  18.6 0.4 prepare.1.parts_ref
  19.0 0.2 all-to-all-done.msg_ref.info_ref
  19.2 3.1 %pick.1 = (f32[8,20,128]{2,1,0:T(8,128)S(1)}, f32[8,4,128]{2,1,0:T(4,128)S(1)}) custom-call(f32[8,24,128]{2,1,0:T(8,128)S(1)} %all-to-all-done.msg_ref.info_ref, bf16[2560,512]{1,0:T(8,128)(2,1)S(1)} %prepare.1.parts_ref), custom_call_target="tpu_custom_call" | custom-call | bytes 1024 | tf_op jit(solution)/shard_map/pick/pallas_call | solution.py:409
  22.3 12.7 %all_to_all.15.got_ref = f32[8,20,128]{2,1,0:T(8,128)S(1)} all-to-all(f32[8,20,128]{2,1,0:T(8,128)S(1)} %get-tuple-element.39), channel_id=1, replica_groups=mesh['cols'=8,'mem'=4] {'cols'}, dimensions={0} | all-to-all | bytes 163840 | tf_op jit(solution)/shard_map/all_to_all | solution.py:422
  35.1 0.0 collective-permute-done.refs_2_
  35.1 0.0 collective-permute-done.1.refs_3_
  35.1 1.1 %place.1 = f32[8,80,128]{2,1,0:T(8,128)} custom-call(f32[8,20,128]{2,1,0:T(8,128)S(1)} %all_to_all.15.got_ref, s32[4,128]{1,0:T(4,128)S(1)} %copy-done.1), custom_call_target="tpu_custom_call" | custom-call | tf_op jit(solution)/shard_map/place/pallas_call | solution.py:424
  36.2 0.0 collective-permute-done.2.refs_4_
  36.2 3.6 %all-to-all-start.2 = ((f32[8,80,128]{2,1,0:T(8,128)}), f32[8,80,128]{2,1,0:T(8,128)S(1)}, u32[]{:S(2)}, u32[]{:S(2)}) async-start(f32[8,80,128]{2,1,0:T(8,128)} %place.1), calls=%async_computation.2 | async-start | bytes 655360 | tf_op jit(solution)/shard_map/all_to_all | solution.py:435
  39.8 0.1 collective-permute-start.11
  39.9 1.5 %collective-permute-start.7 = (f32[20,1536]{1,0:T(8,128)}, f32[20,1536]{1,0:T(8,128)S(1)}, u32[]{:S(2)}, u32[]{:S(2)}) collective-permute-start(f32[20,1536]{1,0:T(8,128)} %get-tuple-element.50), channel_id=1, source_target_pairs={{0,2},{1,3},{2,0},{3,1},{4,6},{5,7},{6,4},{7,5},{8,10},{9,11},{10,... | collective-permute-start | bytes 368648 | tf_op jit(solution)/shard_map/ppermute | solution.py:404
  41.4 0.3 collective-permute-start.8
  41.7 1.4 %collective-permute-start.6 = (f32[8,4,128]{2,1,0:T(4,128)S(1)}, f32[8,4,128]{2,1,0:T(4,128)S(1)}, u32[]{:S(2)}, u32[]{:S(2)}) collective-permute-start(f32[8,4,128]{2,1,0:T(4,128)S(1)} %get-tuple-element.60.a_ref), channel_id=1, source_target_pairs={{0,3},{1,2},{2,1},{3,0},{4,7},{5,6},{6,5},{7,4},{8,11},{9,10},{10,... | collective-permute-start | bytes 49160 | tf_op jit(solution)/shard_map/ppermute | solution.py:404
  43.2 0.5 collective-permute-start.5
  43.7 3.1 %collective-permute-done.7.refs_6_ = f32[20,1536]{1,0:T(8,128)S(1)} collective-permute-done((f32[20,1536]{1,0:T(8,128)}, f32[20,1536]{1,0:T(8,128)S(1)}, u32[]{:S(2)}, u32[]{:S(2)}) %collective-permute-start.7) | collective-permute-done | bytes 122912 | tf_op jit(solution)/shard_map/ppermute | solution.py:404
  46.8 2.2 %collective-permute-done.8.refs_7_ = f32[20,1536]{1,0:T(8,128)S(1)} collective-permute-done((f32[20,1536]{1,0:T(8,128)}, f32[20,1536]{1,0:T(8,128)S(1)}, u32[]{:S(2)}, u32[]{:S(2)}) %collective-permute-start.8) | collective-permute-done | bytes 122912 | tf_op jit(solution)/shard_map/ppermute | solution.py:404
  49.0 0.4 collective-permute-done.6.d_ref
  49.4 0.8 %collective-permute-done.5.c_ref = f32[8,4,128]{2,1,0:T(4,128)S(1)} collective-permute-done((f32[8,4,128]{2,1,0:T(4,128)S(1)}, f32[8,4,128]{2,1,0:T(4,128)S(1)}, u32[]{:S(2)}, u32[]{:S(2)}) %collective-permute-start.5) | collective-permute-done | bytes 16416 | tf_op jit(solution)/shard_map/ppermute | solution.py:404
  50.2 0.5 all-to-all-done.2.a_ref
  50.7 1.5 %collective-permute-start.10 = (f32[8,80,128]{2,1,0:T(8,128)S(1)}, f32[8,80,128]{2,1,0:T(8,128)S(1)}, u32[]{:S(2)}, u32[]{:S(2)}) collective-permute-start(f32[8,80,128]{2,1,0:T(8,128)S(1)} %all-to-all-done.2.a_ref), channel_id=1, source_target_pairs={{0,2},{1,3},{2,0},{3,1},{4,6},{5,7},{6,4},{7,5},{8,10},{9,11},{10,... | collective-permute-start | bytes 983048 | tf_op jit(solution)/shard_map/ppermute | solution.py:404
  52.1 0.6 masks.1.mask_ref
  52.8 2.6 %split.1.ens_ref = bf16[160,8192]{1,0:T(8,128)(2,1)S(1)} custom-call(f32[20,32768]{1,0:T(8,128)} %refs_0_, f32[20,8192]{1,0:T(8,128)S(1)} %collective-permute-done.11.refs_1_, f32[20,4096]{1,0:T(8,128)} %collective-permute-done.refs_2_, f32[20,4096]{1,0:T(8,128)} %collective-permute-done.1.refs_3_, f32[20,2560]{1,0:T(8,128)S(1)} %collective-permute-done.2.refs_4_, ...), custom_call_target="tpu_custom_call" | custom-call | tf_op jit(solution)/shard_map/split/pallas_call | solution.py:447
  55.4 4.6 %collective-permute-done.10.c_ref = f32[8,80,128]{2,1,0:T(8,128)S(1)} collective-permute-done((f32[8,80,128]{2,1,0:T(8,128)S(1)}, f32[8,80,128]{2,1,0:T(8,128)S(1)}, u32[]{:S(2)}, u32[]{:S(2)}) %collective-permute-start.10) | collective-permute-done | bytes 327712 | tf_op jit(solution)/shard_map/ppermute | solution.py:404
  59.9 1.6 %collective-permute-done.12.d_ref = f32[8,80,128]{2,1,0:T(8,128)S(1)} collective-permute-done((f32[8,80,128]{2,1,0:T(8,128)S(1)}, f32[8,80,128]{2,1,0:T(8,128)S(1)}, u32[]{:S(2)}, u32[]{:S(2)}) %collective-permute-start.12) | collective-permute-done | bytes 327712 | tf_op jit(solution)/shard_map/ppermute | solution.py:404
  61.5 7.3 %window.1 = f32[80,8192]{1,0:T(8,128)} custom-call(f32[8,80,128]{2,1,0:T(8,128)S(1)} %all-to-all-done.2.a_ref, f32[8,80,128]{2,1,0:T(8,128)S(1)} %collective-permute-done.9.b_ref, f32[8,80,128]{2,1,0:T(8,128)S(1)} %collective-permute-done.10.c_ref, f32[8,80,128]{2,1,0:T(8,128)S(1)} %collective-permute-done.12.d_ref, ...), custom_call_target="tpu_custom_call" | custom-call | tf_op jit(solution)/shard_map/window/pallas_call | solution.py:325
  (11 shorter events, 0.0 us)
Async XLA Ops:
  3.0 32.0 %collective-permute-start = (f32[20,4096]{1,0:T(8,128)}, f32[20,4096]{1,0:T(8,128)}, u32[]{:S(2)}, u32[]{:S(2)}) collective-permute-start(f32[20,4096]{1,0:T(8,128)} %get-tuple-element.40), channel_id=1, source_target_pairs={{0,2},{1,3},{2,0},{3,1},{4,6},{5,7},{6,4},{7,5},{8,10},{9,11},{10,... | collective-permute-start | bytes 983048 | tf_op jit(solution)/shard_map/ppermute | solution.py:404
  6.0 29.0 %collective-permute-start.1 = (f32[20,4096]{1,0:T(8,128)}, f32[20,4096]{1,0:T(8,128)}, u32[]{:S(2)}, u32[]{:S(2)}) collective-permute-start(f32[20,4096]{1,0:T(8,128)} %get-tuple-element.41), channel_id=1, source_target_pairs={{0,3},{1,2},{2,1},{3,0},{4,7},{5,6},{6,5},{7,4},{8,11},{9,10},{10,... | collective-permute-start | bytes 983048 | tf_op jit(solution)/shard_map/ppermute | solution.py:404
  6.0 13.1 %all-to-all-start = ((f32[8,24,128]{2,1,0:T(8,128)}), f32[8,24,128]{2,1,0:T(8,128)S(1)}, u32[]{:S(2)}, u32[]{:S(2)}) async-start(f32[8,24,128]{2,1,0:T(8,128)} %get-tuple-element.37), calls=%async_computation | async-start | bytes 196608 | tf_op jit(solution)/shard_map/all_to_all | solution.py:381
  14.9 21.2 %collective-permute-start.2 = (f32[20,2560]{1,0:T(8,128)}, f32[20,2560]{1,0:T(8,128)S(1)}, u32[]{:S(2)}, u32[]{:S(2)}) collective-permute-start(f32[20,2560]{1,0:T(8,128)} %get-tuple-element.46), channel_id=1, source_target_pairs={{0,2},{1,3},{2,0},{3,1},{4,6},{5,7},{6,4},{7,5},{8,10},{9,11},{10,... | collective-permute-start | bytes 614408 | tf_op jit(solution)/shard_map/ppermute | solution.py:404
  16.2 20.0 %collective-permute-start.3 = (f32[20,2560]{1,0:T(8,128)}, f32[20,2560]{1,0:T(8,128)S(1)}, u32[]{:S(2)}, u32[]{:S(2)}) collective-permute-start(f32[20,2560]{1,0:T(8,128)} %get-tuple-element.47), channel_id=1, source_target_pairs={{0,3},{1,2},{2,1},{3,0},{4,7},{5,6},{6,5},{7,4},{8,11},{9,10},{10,... | collective-permute-start | bytes 614408 | tf_op jit(solution)/shard_map/ppermute | solution.py:404
  16.7 1.9 %copy-start = (f32[20,32768]{1,0:T(8,128)S(1)}, f32[20,32768]{1,0:T(8,128)}, u32[]{:S(2)}) copy-start(f32[20,32768]{1,0:T(8,128)} %refs_0_) | copy-start | bytes 7864324
  19.0 16.1 %copy-start.1 = (s32[4,128]{1,0:T(4,128)S(1)}, s32[4,128]{1,0:T(4,128)}, u32[]{:S(2)}) copy-start(s32[4,128]{1,0:T(4,128)} %get-tuple-element.43.sid_ref) | copy-start | bytes 6148
  36.2 14.5 %all-to-all-start.2 = ((f32[8,80,128]{2,1,0:T(8,128)}), f32[8,80,128]{2,1,0:T(8,128)S(1)}, u32[]{:S(2)}, u32[]{:S(2)}) async-start(f32[8,80,128]{2,1,0:T(8,128)} %place.1), calls=%async_computation.2 | async-start | bytes 655360 | tf_op jit(solution)/shard_map/all_to_all | solution.py:435
  39.8 13.0 %collective-permute-start.11 = (f32[20,8192]{1,0:T(8,128)}, f32[20,8192]{1,0:T(8,128)S(1)}, u32[]{:S(2)}, u32[]{:S(2)}) collective-permute-start(f32[20,8192]{1,0:T(8,128)} %get-tuple-element.53), channel_id=1, source_target_pairs={{0,1},{1,0},{2,3},{3,2},{4,5},{5,4},{6,7},{7,6},{8,9},{9,8},{10,11... | collective-permute-start | bytes 1966088 | tf_op jit(solution)/shard_map/ppermute | solution.py:404
  39.9 6.9 %collective-permute-start.7 = (f32[20,1536]{1,0:T(8,128)}, f32[20,1536]{1,0:T(8,128)S(1)}, u32[]{:S(2)}, u32[]{:S(2)}) collective-permute-start(f32[20,1536]{1,0:T(8,128)} %get-tuple-element.50), channel_id=1, source_target_pairs={{0,2},{1,3},{2,0},{3,1},{4,6},{5,7},{6,4},{7,5},{8,10},{9,11},{10,... | collective-permute-start | bytes 368648 | tf_op jit(solution)/shard_map/ppermute | solution.py:404
  41.4 7.6 %collective-permute-start.8 = (f32[20,1536]{1,0:T(8,128)}, f32[20,1536]{1,0:T(8,128)S(1)}, u32[]{:S(2)}, u32[]{:S(2)}) collective-permute-start(f32[20,1536]{1,0:T(8,128)} %get-tuple-element.51), channel_id=1, source_target_pairs={{0,3},{1,2},{2,1},{3,0},{4,7},{5,6},{6,5},{7,4},{8,11},{9,10},{10,... | collective-permute-start | bytes 368648 | tf_op jit(solution)/shard_map/ppermute | solution.py:404
  41.7 7.7 %collective-permute-start.6 = (f32[8,4,128]{2,1,0:T(4,128)S(1)}, f32[8,4,128]{2,1,0:T(4,128)S(1)}, u32[]{:S(2)}, u32[]{:S(2)}) collective-permute-start(f32[8,4,128]{2,1,0:T(4,128)S(1)} %get-tuple-element.60.a_ref), channel_id=1, source_target_pairs={{0,3},{1,2},{2,1},{3,0},{4,7},{5,6},{6,5},{7,4},{8,11},{9,10},{10,... | collective-permute-start | bytes 49160 | tf_op jit(solution)/shard_map/ppermute | solution.py:404
  43.2 7.0 %collective-permute-start.5 = (f32[8,4,128]{2,1,0:T(4,128)S(1)}, f32[8,4,128]{2,1,0:T(4,128)S(1)}, u32[]{:S(2)}, u32[]{:S(2)}) collective-permute-start(f32[8,4,128]{2,1,0:T(4,128)S(1)} %get-tuple-element.60.a_ref), channel_id=1, source_target_pairs={{0,2},{1,3},{2,0},{3,1},{4,6},{5,7},{6,4},{7,5},{8,10},{9,11},{10,... | collective-permute-start | bytes 49160 | tf_op jit(solution)/shard_map/ppermute | solution.py:404
  46.8 3.4 %collective-permute-start.4 = (f32[8,4,128]{2,1,0:T(4,128)S(1)}, f32[8,4,128]{2,1,0:T(4,128)S(1)}, u32[]{:S(2)}, u32[]{:S(2)}) collective-permute-start(f32[8,4,128]{2,1,0:T(4,128)S(1)} %get-tuple-element.60.a_ref), channel_id=1, source_target_pairs={{0,1},{1,0},{2,3},{3,2},{4,5},{5,4},{6,7},{7,6},{8,9},{9,8},{10,11... | collective-permute-start | bytes 49160 | tf_op jit(solution)/shard_map/ppermute | solution.py:404
  50.7 9.3 %collective-permute-start.10 = (f32[8,80,128]{2,1,0:T(8,128)S(1)}, f32[8,80,128]{2,1,0:T(8,128)S(1)}, u32[]{:S(2)}, u32[]{:S(2)}) collective-permute-start(f32[8,80,128]{2,1,0:T(8,128)S(1)} %all-to-all-done.2.a_ref), channel_id=1, source_target_pairs={{0,2},{1,3},{2,0},{3,1},{4,6},{5,7},{6,4},{7,5},{8,10},{9,11},{10,... | collective-permute-start | bytes 983048 | tf_op jit(solution)/shard_map/ppermute | solution.py:404
  52.1 7.8 %collective-permute-start.9 = (f32[8,80,128]{2,1,0:T(8,128)S(1)}, f32[8,80,128]{2,1,0:T(8,128)S(1)}, u32[]{:S(2)}, u32[]{:S(2)}) collective-permute-start(f32[8,80,128]{2,1,0:T(8,128)S(1)} %all-to-all-done.2.a_ref), channel_id=1, source_target_pairs={{0,1},{1,0},{2,3},{3,2},{4,5},{5,4},{6,7},{7,6},{8,9},{9,8},{10,11... | collective-permute-start | bytes 983048 | tf_op jit(solution)/shard_map/ppermute | solution.py:404
  59.9 1.6 %collective-permute-start.12 = (f32[8,80,128]{2,1,0:T(8,128)S(1)}, f32[8,80,128]{2,1,0:T(8,128)S(1)}, u32[]{:S(2)}, u32[]{:S(2)}) collective-permute-start(f32[8,80,128]{2,1,0:T(8,128)S(1)} %collective-permute-done.10.c_ref), channel_id=1, source_target_pairs={{0,1},{1,0},{2,3},{3,2},{4,5},{5,4},{6,7},{7,6},{8,9},{9,8},{10,11... | collective-permute-start | bytes 983048 | tf_op jit(solution)/shard_map/ppermute | solution.py:404

commit v5 on v4

--- a/solution.py
+++ b/solution.py
@@ -109,15 +109,20 @@
 
 
 def cut_kernel(cuts, state_ref, *refs):
-    sends, sem = refs[:-1], refs[-1]
+    n = len(cuts)
+    sends, held, sems = refs[0:n], refs[n : 2 * n], refs[2 * n]
     cells = state_ref.shape[1] // 4
     mem = lax.axis_index("mem")
-    copies = []
-    for ref, (k, begin, end) in zip(sends, cuts):
+    taken, sent = [], []
+    for i, (k, begin, end) in enumerate(cuts):
         start = pl.multiple_of((mem ^ k) * cells + begin, LANES)
-        copies.append(pltpu.make_async_copy(state_ref.at[:, pl.ds(start, end - begin)], ref, sem.at[len(copies)]))
-        copies[-1].start()
-    for copy in copies:
+        taken.append(pltpu.make_async_copy(state_ref.at[:, pl.ds(start, end - begin)], held[i], sems.at[i]))
+        sent.append(pltpu.make_async_copy(held[i], sends[i], sems.at[n + i]))
+        taken[i].start()
+    for copy_in, copy_out in zip(taken, sent):
+        copy_in.wait()
+        copy_out.start()
+    for copy in sent:
         copy.wait()
 
 
@@ -383,9 +388,10 @@
     sends = pl.pallas_call(
         functools.partial(cut_kernel, later),
         out_shape=tuple(jax.ShapeDtypeStruct((rows, end - begin), f32) for _, begin, end in later),
-        in_specs=[WHOLE],
+        in_specs=[FAR],
         out_specs=(FAR,) * len(later),
-        scratch_shapes=[pltpu.SemaphoreType.DMA((len(later),))],
+        scratch_shapes=[pltpu.VMEM((rows, end - begin), f32) for _, begin, end in later]
+        + [pltpu.SemaphoreType.DMA((2 * len(later),))],
         compiler_params=NEARLY,
         cost_estimate=cost(1024),
         name="cut",

time: 69.5 us -> 69.5 us (level)
  starting transfers between devices: 19.6 us -> 20.4 us
  Pallas kernels: 21.2 us -> 20.5 us
  blocking collectives: 12.7 us -> 12 us
  waiting for transfers between devices: 13.3 us -> 14 us
    all_to_all x1, blocking collectives: 12.7 us -> 12 us  [fast(): lax.all_to_all(priors, 'cols', split_axis=0, concat_axis=0, tiled=True)]
    pallas_call x1, Pallas kernels: 3.05 us -> 2.33 us  [fast(): pl.pallas_call(functools.partial(cut_kernel, later), out_shape=tuple((jax...]
    all_to_all x1, waiting for transfers between devices: 0.16 us -> 0.87 us  [fast(): lax.all_to_all(msg, 'cols', split_axis=0, concat_axis=0, tiled=True)]
  transfers between devices with their start and end apart: 15 -> 15, of which waited for: 8 -> 8; matrix products, arithmetic and copies ran while one was open for 0% -> 0% of each run, Pallas kernels for 16% -> 15%
where the time goes in v5:
time: 69.5 us; the launch traced here: 69.1 us
  Pallas kernels  20.5 us (29%)
  starting transfers between devices  20.4 us (29%)
  waiting for transfers between devices  14 us (20%)
  blocking collectives  12 us (17%)
  local copies, waits for them, and re-layouts  1.89 us (3%)
    ppermute x13, waiting for transfers between devices, swap(): return lax.ppermute(array, 'mem', [(i, i ^ k) for i in range(4)])  12.3 us
    all_to_all x1, blocking collectives, fast(): lax.all_to_all(priors, 'cols', split_axis=0, concat_axis=0, tiled=True)  12 us
    ppermute x13, starting transfers between devices, swap(): return lax.ppermute(array, 'mem', [(i, i ^ k) for i in range(4)])  10.5 us
    pallas_call x1, Pallas kernels, window_call(): pl.pallas_call(functools.partial(window_kernel, tiles, rows), out_shape=j...  7.34 us
    all_to_all x1, starting transfers between devices, fast(): lax.all_to_all(msg, 'cols', split_axis=0, concat_axis=0, tiled=True)  5.83 us
    all_to_all x1, starting transfers between devices, fast(): lax.all_to_all(everyone, 'cols', split_axis=0, concat_axis=0, tiled=True)  4.07 us
    pallas_call x1, Pallas kernels, fast(): pl.pallas_call(functools.partial(pick_kernel, rows), out_shape=(jax.Shape...  3.13 us
    pallas_call x1, Pallas kernels, fast(): pl.pallas_call(functools.partial(route_kernel, owners, slots_per, sooner)...  3.01 us
  transfers between devices with their start and end apart: 15, of which 8 were waited for; matrix products, arithmetic and copies ran while one was open for 0% of the time, Pallas kernels for 15%

profile of v5, /device:TPU:0, one launch (start us, length us, event | category | flops | bytes accessed | tf_op | source)
XLA Modules:
  0.0 69.1 jit_solution(13168622592303197398)
XLA Ops:
  0.0 3.0 %route.1 = (f32[8,24,128]{2,1,0:T(8,128)}, s32[4,128]{1,0:T(4,128)}, f32[20,4096]{1,0:T(8,128)}, f32[20,4096]{1,0:T(8,128)}) custom-call(s32[4,1,128]{2,1,0:T(1,128)} %bitcast.7, s32[4,128]{1,0:T(4,128)} %refs_1_.1, s32[4,4,128]{2,1,0:T(4,128)} %bitcast.6, f32[4,128]{1,0:T(4,128)} %refs_3_.1, f32[4,128]{1,0:T(4,128)} %refs_4_.1, s32[4,128]{1,0:T(4,128)} %refs_5_.1, ...), custom_call_target="tpu_custom_call" | custom-call | tf_op jit(solution)/shard_map/route/pallas_call | solution.py:370
  3.0 3.0 %collective-permute-start = (f32[20,4096]{1,0:T(8,128)}, f32[20,4096]{1,0:T(8,128)}, u32[]{:S(2)}, u32[]{:S(2)}) collective-permute-start(f32[20,4096]{1,0:T(8,128)} %get-tuple-element.40), channel_id=1, source_target_pairs={{0,2},{1,3},{2,0},{3,1},{4,6},{5,7},{6,4},{7,5},{8,10},{9,11},{10,... | collective-permute-start | bytes 983048 | tf_op jit(solution)/shard_map/ppermute | solution.py:410
  6.0 0.0 collective-permute-start.1
  6.0 5.8 %all-to-all-start = ((f32[8,24,128]{2,1,0:T(8,128)}), f32[8,24,128]{2,1,0:T(8,128)S(1)}, u32[]{:S(2)}, u32[]{:S(2)}) async-start(f32[8,24,128]{2,1,0:T(8,128)} %get-tuple-element.37), calls=%async_computation | async-start | bytes 196608 | tf_op jit(solution)/shard_map/all_to_all | solution.py:386
  11.9 2.3 %cut.1 = (f32[20,8192]{1,0:T(8,128)}, f32[20,2560]{1,0:T(8,128)}, f32[20,2560]{1,0:T(8,128)}, f32[20,1536]{1,0:T(8,128)}, f32[20,1536]{1,0:T(8,128)}) custom-call(f32[20,32768]{1,0:T(8,128)} %refs_0_), custom_call_target="tpu_custom_call" | custom-call | bytes 1024 | tf_op jit(solution)/shard_map/cut/pallas_call | solution.py:388
  14.2 1.2 %collective-permute-start.2 = (f32[20,2560]{1,0:T(8,128)}, f32[20,2560]{1,0:T(8,128)S(1)}, u32[]{:S(2)}, u32[]{:S(2)}) collective-permute-start(f32[20,2560]{1,0:T(8,128)} %get-tuple-element.46), channel_id=1, source_target_pairs={{0,2},{1,3},{2,0},{3,1},{4,6},{5,7},{6,4},{7,5},{8,10},{9,11},{10,... | collective-permute-start | bytes 614408 | tf_op jit(solution)/shard_map/ppermute | solution.py:410
  15.4 0.5 collective-permute-start.3
  16.0 1.9 %copy-done = f32[20,32768]{1,0:T(8,128)S(1)} copy-done((f32[20,32768]{1,0:T(8,128)S(1)}, f32[20,32768]{1,0:T(8,128)}, u32[]{:S(2)}) %copy-start) | copy-done | bytes 2621464
  17.9 0.4 prepare.1.parts_ref
  18.3 0.9 %all-to-all-done.msg_ref.info_ref = f32[8,24,128]{2,1,0:T(8,128)S(1)} async-done(((f32[8,24,128]{2,1,0:T(8,128)}), f32[8,24,128]{2,1,0:T(8,128)S(1)}, u32[]{:S(2)}, u32[]{:S(2)}) %all-to-all-start) | async-done | bytes 98336 | tf_op jit(solution)/shard_map/all_to_all | solution.py:386
  19.2 3.1 %pick.1 = (f32[8,20,128]{2,1,0:T(8,128)S(1)}, f32[8,4,128]{2,1,0:T(4,128)S(1)}) custom-call(f32[8,24,128]{2,1,0:T(8,128)S(1)} %all-to-all-done.msg_ref.info_ref, bf16[2560,512]{1,0:T(8,128)(2,1)S(1)} %prepare.1.parts_ref), custom_call_target="tpu_custom_call" | custom-call | bytes 1024 | tf_op jit(solution)/shard_map/pick/pallas_call | solution.py:415
  22.3 12.0 %all_to_all.15.got_ref = f32[8,20,128]{2,1,0:T(8,128)S(1)} all-to-all(f32[8,20,128]{2,1,0:T(8,128)S(1)} %get-tuple-element.39), channel_id=1, replica_groups=mesh['cols'=8,'mem'=4] {'cols'}, dimensions={0} | all-to-all | bytes 163840 | tf_op jit(solution)/shard_map/all_to_all | solution.py:428
  34.3 1.1 %place.1 = f32[8,80,128]{2,1,0:T(8,128)} custom-call(f32[8,20,128]{2,1,0:T(8,128)S(1)} %all_to_all.15.got_ref, s32[4,128]{1,0:T(4,128)S(1)} %copy-done.1), custom_call_target="tpu_custom_call" | custom-call | tf_op jit(solution)/shard_map/place/pallas_call | solution.py:430
  35.4 4.1 %all-to-all-start.2 = ((f32[8,80,128]{2,1,0:T(8,128)}), f32[8,80,128]{2,1,0:T(8,128)S(1)}, u32[]{:S(2)}, u32[]{:S(2)}) async-start(f32[8,80,128]{2,1,0:T(8,128)} %place.1), calls=%async_computation.2 | async-start | bytes 655360 | tf_op jit(solution)/shard_map/all_to_all | solution.py:441
  39.5 0.4 collective-permute-start.11
  39.9 1.5 %collective-permute-start.7 = (f32[20,1536]{1,0:T(8,128)}, f32[20,1536]{1,0:T(8,128)S(1)}, u32[]{:S(2)}, u32[]{:S(2)}) collective-permute-start(f32[20,1536]{1,0:T(8,128)} %get-tuple-element.50), channel_id=1, source_target_pairs={{0,2},{1,3},{2,0},{3,1},{4,6},{5,7},{6,4},{7,5},{8,10},{9,11},{10,... | collective-permute-start | bytes 368648 | tf_op jit(solution)/shard_map/ppermute | solution.py:410
  41.4 1.7 %collective-permute-start.6 = (f32[8,4,128]{2,1,0:T(4,128)S(1)}, f32[8,4,128]{2,1,0:T(4,128)S(1)}, u32[]{:S(2)}, u32[]{:S(2)}) collective-permute-start(f32[8,4,128]{2,1,0:T(4,128)S(1)} %get-tuple-element.60.a_ref), channel_id=1, source_target_pairs={{0,3},{1,2},{2,1},{3,0},{4,7},{5,6},{6,5},{7,4},{8,11},{9,10},{10,... | collective-permute-start | bytes 49160 | tf_op jit(solution)/shard_map/ppermute | solution.py:410
  43.2 0.5 collective-permute-start.5
  43.7 3.1 %collective-permute-done.7.refs_6_ = f32[20,1536]{1,0:T(8,128)S(1)} collective-permute-done((f32[20,1536]{1,0:T(8,128)}, f32[20,1536]{1,0:T(8,128)S(1)}, u32[]{:S(2)}, u32[]{:S(2)}) %collective-permute-start.7) | collective-permute-done | bytes 122912 | tf_op jit(solution)/shard_map/ppermute | solution.py:410
  46.8 0.0 collective-permute-start.4
  46.8 1.7 %collective-permute-done.8.refs_7_ = f32[20,1536]{1,0:T(8,128)S(1)} collective-permute-done((f32[20,1536]{1,0:T(8,128)}, f32[20,1536]{1,0:T(8,128)S(1)}, u32[]{:S(2)}, u32[]{:S(2)}) %collective-permute-start.8) | collective-permute-done | bytes 122912 | tf_op jit(solution)/shard_map/ppermute | solution.py:410
  48.6 0.1 collective-permute-done.6.d_ref
  48.7 1.2 %collective-permute-done.5.c_ref = f32[8,4,128]{2,1,0:T(4,128)S(1)} collective-permute-done((f32[8,4,128]{2,1,0:T(4,128)S(1)}, f32[8,4,128]{2,1,0:T(4,128)S(1)}, u32[]{:S(2)}, u32[]{:S(2)}) %collective-permute-start.5) | collective-permute-done | bytes 16416 | tf_op jit(solution)/shard_map/ppermute | solution.py:410
  49.8 0.0 collective-permute-done.4.b_ref
  49.8 0.8 %all-to-all-done.2.a_ref = f32[8,80,128]{2,1,0:T(8,128)S(1)} async-done(((f32[8,80,128]{2,1,0:T(8,128)}), f32[8,80,128]{2,1,0:T(8,128)S(1)}, u32[]{:S(2)}, u32[]{:S(2)}) %all-to-all-start.2) | async-done | bytes 327712 | tf_op jit(solution)/shard_map/all_to_all | solution.py:441
  50.7 1.5 %collective-permute-start.10 = (f32[8,80,128]{2,1,0:T(8,128)S(1)}, f32[8,80,128]{2,1,0:T(8,128)S(1)}, u32[]{:S(2)}, u32[]{:S(2)}) collective-permute-start(f32[8,80,128]{2,1,0:T(8,128)S(1)} %all-to-all-done.2.a_ref), channel_id=1, source_target_pairs={{0,2},{1,3},{2,0},{3,1},{4,6},{5,7},{6,4},{7,5},{8,10},{9,11},{10,... | collective-permute-start | bytes 983048 | tf_op jit(solution)/shard_map/ppermute | solution.py:410
  52.1 0.6 masks.1.mask_ref
  52.8 2.6 %split.1.ens_ref = bf16[160,8192]{1,0:T(8,128)(2,1)S(1)} custom-call(f32[20,32768]{1,0:T(8,128)} %refs_0_, f32[20,8192]{1,0:T(8,128)S(1)} %collective-permute-done.11.refs_1_, f32[20,4096]{1,0:T(8,128)} %collective-permute-done.refs_2_, f32[20,4096]{1,0:T(8,128)} %collective-permute-done.1.refs_3_, f32[20,2560]{1,0:T(8,128)S(1)} %collective-permute-done.2.refs_4_, ...), custom_call_target="tpu_custom_call" | custom-call | tf_op jit(solution)/shard_map/split/pallas_call | solution.py:453
  55.4 4.6 %collective-permute-done.10.c_ref = f32[8,80,128]{2,1,0:T(8,128)S(1)} collective-permute-done((f32[8,80,128]{2,1,0:T(8,128)S(1)}, f32[8,80,128]{2,1,0:T(8,128)S(1)}, u32[]{:S(2)}, u32[]{:S(2)}) %collective-permute-start.10) | collective-permute-done | bytes 327712 | tf_op jit(solution)/shard_map/ppermute | solution.py:410
  59.9 0.0 collective-permute-done.9.b_ref
  59.9 1.6 %collective-permute-done.12.d_ref = f32[8,80,128]{2,1,0:T(8,128)S(1)} collective-permute-done((f32[8,80,128]{2,1,0:T(8,128)S(1)}, f32[8,80,128]{2,1,0:T(8,128)S(1)}, u32[]{:S(2)}, u32[]{:S(2)}) %collective-permute-start.12) | collective-permute-done | bytes 327712 | tf_op jit(solution)/shard_map/ppermute | solution.py:410
  61.6 7.3 %window.1 = f32[80,8192]{1,0:T(8,128)} custom-call(f32[8,80,128]{2,1,0:T(8,128)S(1)} %all-to-all-done.2.a_ref, f32[8,80,128]{2,1,0:T(8,128)S(1)} %collective-permute-done.9.b_ref, f32[8,80,128]{2,1,0:T(8,128)S(1)} %collective-permute-done.10.c_ref, f32[8,80,128]{2,1,0:T(8,128)S(1)} %collective-permute-done.12.d_ref, ...), custom_call_target="tpu_custom_call" | custom-call | tf_op jit(solution)/shard_map/window/pallas_call | solution.py:330
  (11 shorter events, 0.0 us)
Async XLA Ops:
  3.0 31.3 %collective-permute-start = (f32[20,4096]{1,0:T(8,128)}, f32[20,4096]{1,0:T(8,128)}, u32[]{:S(2)}, u32[]{:S(2)}) collective-permute-start(f32[20,4096]{1,0:T(8,128)} %get-tuple-element.40), channel_id=1, source_target_pairs={{0,2},{1,3},{2,0},{3,1},{4,6},{5,7},{6,4},{7,5},{8,10},{9,11},{10,... | collective-permute-start | bytes 983048 | tf_op jit(solution)/shard_map/ppermute | solution.py:410
  6.0 28.3 %collective-permute-start.1 = (f32[20,4096]{1,0:T(8,128)}, f32[20,4096]{1,0:T(8,128)}, u32[]{:S(2)}, u32[]{:S(2)}) collective-permute-start(f32[20,4096]{1,0:T(8,128)} %get-tuple-element.41), channel_id=1, source_target_pairs={{0,3},{1,2},{2,1},{3,0},{4,7},{5,6},{6,5},{7,4},{8,11},{9,10},{10,... | collective-permute-start | bytes 983048 | tf_op jit(solution)/shard_map/ppermute | solution.py:410
  6.0 13.1 %all-to-all-start = ((f32[8,24,128]{2,1,0:T(8,128)}), f32[8,24,128]{2,1,0:T(8,128)S(1)}, u32[]{:S(2)}, u32[]{:S(2)}) async-start(f32[8,24,128]{2,1,0:T(8,128)} %get-tuple-element.37), calls=%async_computation | async-start | bytes 196608 | tf_op jit(solution)/shard_map/all_to_all | solution.py:386
  14.2 21.2 %collective-permute-start.2 = (f32[20,2560]{1,0:T(8,128)}, f32[20,2560]{1,0:T(8,128)S(1)}, u32[]{:S(2)}, u32[]{:S(2)}) collective-permute-start(f32[20,2560]{1,0:T(8,128)} %get-tuple-element.46), channel_id=1, source_target_pairs={{0,2},{1,3},{2,0},{3,1},{4,6},{5,7},{6,4},{7,5},{8,10},{9,11},{10,... | collective-permute-start | bytes 614408 | tf_op jit(solution)/shard_map/ppermute | solution.py:410
  15.4 20.0 %collective-permute-start.3 = (f32[20,2560]{1,0:T(8,128)}, f32[20,2560]{1,0:T(8,128)S(1)}, u32[]{:S(2)}, u32[]{:S(2)}) collective-permute-start(f32[20,2560]{1,0:T(8,128)} %get-tuple-element.47), channel_id=1, source_target_pairs={{0,3},{1,2},{2,1},{3,0},{4,7},{5,6},{6,5},{7,4},{8,11},{9,10},{10,... | collective-permute-start | bytes 614408 | tf_op jit(solution)/shard_map/ppermute | solution.py:410
  16.0 1.9 %copy-start = (f32[20,32768]{1,0:T(8,128)S(1)}, f32[20,32768]{1,0:T(8,128)}, u32[]{:S(2)}) copy-start(f32[20,32768]{1,0:T(8,128)} %refs_0_) | copy-start | bytes 7864324
  18.3 16.1 %copy-start.1 = (s32[4,128]{1,0:T(4,128)S(1)}, s32[4,128]{1,0:T(4,128)}, u32[]{:S(2)}) copy-start(s32[4,128]{1,0:T(4,128)} %get-tuple-element.43.sid_ref) | copy-start | bytes 6148
  35.4 15.2 %all-to-all-start.2 = ((f32[8,80,128]{2,1,0:T(8,128)}), f32[8,80,128]{2,1,0:T(8,128)S(1)}, u32[]{:S(2)}, u32[]{:S(2)}) async-start(f32[8,80,128]{2,1,0:T(8,128)} %place.1), calls=%async_computation.2 | async-start | bytes 655360 | tf_op jit(solution)/shard_map/all_to_all | solution.py:441
  39.5 13.3 %collective-permute-start.11 = (f32[20,8192]{1,0:T(8,128)}, f32[20,8192]{1,0:T(8,128)S(1)}, u32[]{:S(2)}, u32[]{:S(2)}) collective-permute-start(f32[20,8192]{1,0:T(8,128)} %get-tuple-element.53), channel_id=1, source_target_pairs={{0,1},{1,0},{2,3},{3,2},{4,5},{5,4},{6,7},{7,6},{8,9},{9,8},{10,11... | collective-permute-start | bytes 1966088 | tf_op jit(solution)/shard_map/ppermute | solution.py:410
  39.9 6.9 %collective-permute-start.7 = (f32[20,1536]{1,0:T(8,128)}, f32[20,1536]{1,0:T(8,128)S(1)}, u32[]{:S(2)}, u32[]{:S(2)}) collective-permute-start(f32[20,1536]{1,0:T(8,128)} %get-tuple-element.50), channel_id=1, source_target_pairs={{0,2},{1,3},{2,0},{3,1},{4,6},{5,7},{6,4},{7,5},{8,10},{9,11},{10,... | collective-permute-start | bytes 368648 | tf_op jit(solution)/shard_map/ppermute | solution.py:410
  41.4 7.2 %collective-permute-start.8 = (f32[20,1536]{1,0:T(8,128)}, f32[20,1536]{1,0:T(8,128)S(1)}, u32[]{:S(2)}, u32[]{:S(2)}) collective-permute-start(f32[20,1536]{1,0:T(8,128)} %get-tuple-element.51), channel_id=1, source_target_pairs={{0,3},{1,2},{2,1},{3,0},{4,7},{5,6},{6,5},{7,4},{8,11},{9,10},{10,... | collective-permute-start | bytes 368648 | tf_op jit(solution)/shard_map/ppermute | solution.py:410
  41.4 7.2 %collective-permute-start.6 = (f32[8,4,128]{2,1,0:T(4,128)S(1)}, f32[8,4,128]{2,1,0:T(4,128)S(1)}, u32[]{:S(2)}, u32[]{:S(2)}) collective-permute-start(f32[8,4,128]{2,1,0:T(4,128)S(1)} %get-tuple-element.60.a_ref), channel_id=1, source_target_pairs={{0,3},{1,2},{2,1},{3,0},{4,7},{5,6},{6,5},{7,4},{8,11},{9,10},{10,... | collective-permute-start | bytes 49160 | tf_op jit(solution)/shard_map/ppermute | solution.py:410
  43.2 6.7 %collective-permute-start.5 = (f32[8,4,128]{2,1,0:T(4,128)S(1)}, f32[8,4,128]{2,1,0:T(4,128)S(1)}, u32[]{:S(2)}, u32[]{:S(2)}) collective-permute-start(f32[8,4,128]{2,1,0:T(4,128)S(1)} %get-tuple-element.60.a_ref), channel_id=1, source_target_pairs={{0,2},{1,3},{2,0},{3,1},{4,6},{5,7},{6,4},{7,5},{8,10},{9,11},{10,... | collective-permute-start | bytes 49160 | tf_op jit(solution)/shard_map/ppermute | solution.py:410
  46.8 3.0 %collective-permute-start.4 = (f32[8,4,128]{2,1,0:T(4,128)S(1)}, f32[8,4,128]{2,1,0:T(4,128)S(1)}, u32[]{:S(2)}, u32[]{:S(2)}) collective-permute-start(f32[8,4,128]{2,1,0:T(4,128)S(1)} %get-tuple-element.60.a_ref), channel_id=1, source_target_pairs={{0,1},{1,0},{2,3},{3,2},{4,5},{5,4},{6,7},{7,6},{8,9},{9,8},{10,11... | collective-permute-start | bytes 49160 | tf_op jit(solution)/shard_map/ppermute | solution.py:410
  50.7 9.3 %collective-permute-start.10 = (f32[8,80,128]{2,1,0:T(8,128)S(1)}, f32[8,80,128]{2,1,0:T(8,128)S(1)}, u32[]{:S(2)}, u32[]{:S(2)}) collective-permute-start(f32[8,80,128]{2,1,0:T(8,128)S(1)} %all-to-all-done.2.a_ref), channel_id=1, source_target_pairs={{0,2},{1,3},{2,0},{3,1},{4,6},{5,7},{6,4},{7,5},{8,10},{9,11},{10,... | collective-permute-start | bytes 983048 | tf_op jit(solution)/shard_map/ppermute | solution.py:410
  52.1 7.8 %collective-permute-start.9 = (f32[8,80,128]{2,1,0:T(8,128)S(1)}, f32[8,80,128]{2,1,0:T(8,128)S(1)}, u32[]{:S(2)}, u32[]{:S(2)}) collective-permute-start(f32[8,80,128]{2,1,0:T(8,128)S(1)} %all-to-all-done.2.a_ref), channel_id=1, source_target_pairs={{0,1},{1,0},{2,3},{3,2},{4,5},{5,4},{6,7},{7,6},{8,9},{9,8},{10,11... | collective-permute-start | bytes 983048 | tf_op jit(solution)/shard_map/ppermute | solution.py:410
  59.9 1.6 %collective-permute-start.12 = (f32[8,80,128]{2,1,0:T(8,128)S(1)}, f32[8,80,128]{2,1,0:T(8,128)S(1)}, u32[]{:S(2)}, u32[]{:S(2)}) collective-permute-start(f32[8,80,128]{2,1,0:T(8,128)S(1)} %collective-permute-done.10.c_ref), channel_id=1, source_target_pairs={{0,1},{1,0},{2,3},{3,2},{4,5},{5,4},{6,7},{7,6},{8,9},{9,8},{10,11... | collective-permute-start | bytes 983048 | tf_op jit(solution)/shard_map/ppermute | solution.py:410
